TPU v7x, 128 devices: a whole 4x4x4 slice. The times are simulated.
128 devices in a mesh: attn: 16 (over z, x), expert: 8 (over y, core).
Axes of the slice: x: 4, y: 4, z: 4, core: 2. Of those that a mesh axis runs over, the one named last changes fastest.
Arguments:
- resid: bfloat16 [1024, 6144], P('attn', 'expert')
- query: bfloat16 [1024, 6144], P('attn', 'expert'), may hold values from -1 to 1
- key_cache: bfloat16 [1024, 8, 128, 128], P('attn', 'expert'), may hold values from -4 to 4
- value_cache: bfloat16 [1024, 8, 128, 128], P('attn', 'expert'), may hold values from -6 to 6
- new_key: bfloat16 [1024, 1024], P('attn', 'expert'), may hold values from -4 to 4
- new_value: bfloat16 [1024, 1024], P('attn', 'expert'), may hold values from -6 to 6
- lengths: int32 [1024], P('attn'), may hold values from 1 to 128, as said below
- norm_gain: float32 [6144], P('expert'), may hold values from 0.1 to 1.9
- router_weight: float32 [6144, 8], P('expert'), may hold values from -0.078125 to 0.078125
- expert_ids: int32 [1024, 2], P('attn'), may hold values from 0 to 7, as said below
- w_gate: bfloat16 [8, 6144, 8192], P('expert', None, 'attn'), may hold values from -0.078125 to 0.078125
- w_up: bfloat16 [8, 6144, 8192], P('expert', None, 'attn'), may hold values from -0.078125 to 0.078125
- w_down: bfloat16 [8, 8192, 6144], P('expert', 'attn'), may hold values from -0.0625 to 0.0625
Outputs:
- layer_out: bfloat16 [1024, 6144], P('attn', 'expert')
Inputs may be any that keep to these rules, and one draw needn't show every extreme that they name: `expert_ids`: each row names two different experts. Within each aligned block of 64 rows (the rows of one index of attn) no expert is named by more than 32 rows, and one expert, the same in every block, is named by exactly 32 rows in each block. `lengths`: some row has all 128 positions filled and some row has one.
All inputs are finite; a program needn't handle non-finite values.
Results may differ from a plain program's by a relative error of at most 0.0095.
Values may be sent and summed in bfloat16 or wider, within the bound.
No kernel may reach another device: no remote copies, remote signals or barrier semaphores. Data moves between devices by JAX's collectives and lax.ppermute only.
A program may use at most 128 MiB of HBM per device.

v0:
```python
import math

import jax
import jax.numpy as jnp
from jax import lax
from jax.sharding import PartitionSpec as P

D = 6144
E = 8
CAP = 32


EPSILON = 1e-05


def on_device(
    resid,
    query,
    key_cache,
    value_cache,
    new_key,
    new_value,
    lengths,
    norm_gain,
    router_weight,
    expert_ids,
    w_gate,
    w_up,
    w_down,
):
    row_count = resid.shape[0]
    width_local = resid.shape[1]
    kv_local = key_cache.shape[1]
    cache_slots = key_cache.shape[2]
    head_size = key_cache.shape[3]
    group_size = query.shape[1] // (kv_local * head_size)
    local_experts = w_gate.shape[0]
    expert_devices = lax.axis_size("expert")
    score_scale = 1.0 / math.sqrt(head_size)
    queries = query.reshape(row_count, kv_local, group_size, head_size)
    scores = (
        jnp.einsum("rkgd,rkld->rkgl", queries, key_cache, preferred_element_type=jnp.float32)
        * score_scale
    )
    fresh_score = (
        jnp.einsum(
            "rkgd,rkd->rkg",
            queries,
            new_key.reshape(row_count, kv_local, head_size),
            preferred_element_type=jnp.float32,
        )
        * score_scale
    )
    usable = lax.broadcasted_iota(jnp.int32, (row_count, cache_slots), 1) < lengths[:, None]
    powers = jnp.where(usable[:, None, None, :], jnp.exp(scores), jnp.float32(0.0))
    fresh_power = jnp.exp(fresh_score)
    denominator = jnp.sum(powers, axis=-1) + fresh_power
    weights_cache = (powers / denominator[..., None]).astype(jnp.bfloat16)
    weight_fresh = (fresh_power / denominator).astype(jnp.bfloat16)
    attended = jnp.einsum(
        "rkgl,rkld->rkgd", weights_cache, value_cache, preferred_element_type=jnp.float32
    )
    attended = attended + weight_fresh.astype(jnp.float32)[..., None] * new_value.astype(
        jnp.float32
    ).reshape(row_count, kv_local, 1, head_size)
    hidden_state = resid.astype(jnp.float32) + attended.reshape(row_count, width_local)
    total_square = lax.psum(jnp.sum(hidden_state * hidden_state, axis=1), "expert")
    normed = hidden_state * lax.rsqrt(total_square / D + EPSILON)[:, None] * norm_gain
    logits = lax.psum(jnp.dot(normed, router_weight, precision=lax.Precision.HIGHEST), "expert")
    narrow = normed.astype(jnp.bfloat16)
    choose = expert_ids[:, :, None] == lax.broadcasted_iota(jnp.int32, (1, 1, E), 2)
    picked = jnp.sum(jnp.where(choose, logits[:, None, :], jnp.float32(0.0)), axis=2)
    first_weight = 1.0 / (1.0 + jnp.exp(picked[:, 1] - picked[:, 0]))
    second_weight = 1.0 / (1.0 + jnp.exp(picked[:, 0] - picked[:, 1]))
    hits = jnp.sum(choose.astype(jnp.int32), axis=1)
    before = jnp.cumsum(hits, axis=0) - hits
    slot_index = jnp.sum(jnp.where(choose, before[:, None, :], 0), axis=2)
    slot_match = slot_index[:, :, None] == lax.broadcasted_iota(jnp.int32, (1, 1, CAP), 2)
    selector = jnp.einsum(
        "rke,rkc->ecr",
        choose.astype(jnp.bfloat16),
        slot_match.astype(jnp.bfloat16),
        preferred_element_type=jnp.float32,
    ).astype(jnp.bfloat16)
    whole_rows = lax.all_gather(narrow, "expert", axis=1, tiled=True)
    own_selector = lax.dynamic_slice_in_dim(
        selector, lax.axis_index("expert") * local_experts, local_experts, 0
    )
    outgoing = jnp.einsum(
        "ecr,rd->ecd", own_selector, whole_rows, preferred_element_type=jnp.float32
    ).astype(jnp.bfloat16)
    slab_rows = lax.all_gather(outgoing, "attn", axis=1, tiled=True)
    gate_part = jnp.einsum("end,edf->enf", slab_rows, w_gate, preferred_element_type=jnp.float32)
    up_part = jnp.einsum("end,edf->enf", slab_rows, w_up, preferred_element_type=jnp.float32)
    activation = (jax.nn.silu(gate_part) * up_part).astype(jnp.bfloat16)
    summed = lax.psum_scatter(
        jnp.einsum("enf,efd->ned", activation, w_down, preferred_element_type=jnp.float32).astype(
            jnp.bfloat16
        ),
        "attn",
        scatter_dimension=0,
        tiled=True,
    )
    expert_result = summed
    expert_result = expert_result.reshape(CAP, local_experts, expert_devices, width_local)
    returned = lax.all_to_all(expert_result, "expert", split_axis=2, concat_axis=1, tiled=True)
    flat_result = returned.reshape(CAP * E, width_local)
    target_index = slot_index * E + expert_ids
    picker = (
        target_index[:, :, None] == lax.broadcasted_iota(jnp.int32, (1, 1, CAP * E), 2)
    ).astype(jnp.bfloat16)
    taken = jnp.einsum("rkm,md->krd", picker, flat_result, preferred_element_type=jnp.float32)
    total = hidden_state + first_weight[:, None] * taken[0] + second_weight[:, None] * taken[1]
    return total.astype(jnp.bfloat16)


def solution(mesh):
    return jax.shard_map(
        on_device,
        mesh=mesh,
        in_specs=(
            P("attn", "expert"),
            P("attn", "expert"),
            P("attn", "expert", None, None),
            P("attn", "expert", None, None),
            P("attn", "expert"),
            P("attn", "expert"),
            P("attn"),
            P("expert"),
            P("expert", None),
            P("attn", None),
            P("expert", None, "attn"),
            P("expert", None, "attn"),
            P("expert", "attn", None),
        ),
        out_specs=P("attn", "expert"),
        check_vma=False,
    )
```

profile of v0, /device:TPU:1, one launch (start us, length us, event | category | flops | bytes accessed | tf_op | source)
XLA Modules:
  0.0 233.5 jit_solution(6571023977040186044)
XLA Ops:
  6.6 0.9 iota_compare_fusion.4
  7.4 0.8 copy.33
  8.5 1.2 select_reduce_fusion
  9.7 0.7 convert_element_type.60
  10.5 0.4 fusion.38
  11.0 1.0 reshape.126
  12.0 0.9 fusion.47
  13.0 1.3 fusion.53
  14.3 2.3 fusion.25
  16.7 13.5 %psum.14 = f32[64]{0:T(128)S(1)} all-reduce(f32[64]{0:T(128)S(1)} %get-tuple-element.5), channel_id=1, replica_groups=mesh['attn'=16,'expert'=8] {'expert'}, use_global_device_ids=true, to_apply=%region_2.3 | all-reduce | flops 64 | bytes 512 | tf_op jit(solution)/shard_map/psum | solution.py:67
  30.3 16.2 %all_gather.6 = bf16[64,6144]{1,0:T(8,128)(2,1)S(1)} all-gather(bf16[64,768]{1,0:T(8,128)(2,1)S(1)} %fusion.35), channel_id=1, replica_groups=mesh['attn'=16,'expert'=8] {'expert'}, dimensions={1}, use_global_device_ids=true | all-gather | bytes 884736 | tf_op jit(solution)/shard_map/all_gather | solution.py:85
  46.5 1.0 convolution_convert_fusion.1
  47.6 61.7 %all-gather.3.cloned.1.call-done = bf16[512,6144]{1,0:T(8,128)(2,1)} async-done(((bf16[32,6144]{1,0:T(8,128)(2,1)}), bf16[512,6144]{1,0:T(8,128)(2,1)}) %all-gather.3.cloned.1.call-update) | async-done | bytes 6291472 | tf_op jit(solution)/shard_map/all_gather | solution.py:92
  109.3 8.1 %fusion.4 = f32[512,512]{1,0:T(8,128)S(1)} fusion(bf16[512,6144]{1,0:T(8,128)(2,1)} %all-gather.3.cloned.1.call-done, bf16[1,6144,512]{2,1,0:T(8,128)(2,1)} %param.23), kind=kOutput, calls=%fused_computation.6 | convolution fusion | flops 3221225472 | bytes 13631488 | tf_op jit(solution)/shard_map/end,edf->enf/dot_general | solution.py:93
  117.5 6.5 %fusion.13 = bf16[512,512]{1,0:T(8,128)(2,1)S(1)} fusion(bf16[512,6144]{1,0:T(8,128)(2,1)S(1)} %copy-done.5, bf16[1,6144,512]{2,1,0:T(8,128)(2,1)} %param.24, f32[512,512]{1,0:T(8,128)S(1)} %fusion.4), kind=kOutput, calls=%fused_computation.13 | convolution fusion | flops 3222798336 | bytes 14155776 | tf_op jit(solution)/shard_map/end,edf->enf/dot_general | solution.py:94
  124.0 5.3 %fusion = bf16[512,1,6144]{2,0,1:T(8,128)(2,1)} fusion(bf16[512,512]{1,0:T(8,128)(2,1)S(1)} %fusion.13, bf16[1,512,6144]{2,1,0:T(8,128)(2,1)S(1)} %bitcast.89), kind=kOutput, calls=%fused_computation.1 | convolution fusion | flops 3224371200 | bytes 13107200 | tf_op jit(solution)/shard_map/enf,efd->ned/dot_general | solution.py:97
  129.4 0.6 copy-done.2
  130.4 12.5 %psum.15 = f32[64,8]{0,1:T(8,128)S(1)} all-reduce(f32[64,8]{0,1:T(8,128)S(1)} %fusion.36), channel_id=1, replica_groups=mesh['attn'=16,'expert'=8] {'expert'}, use_global_device_ids=true, to_apply=%region_3.4 | all-reduce | flops 512 | bytes 4096 | tf_op jit(solution)/shard_map/psum | solution.py:69
  143.4 66.2 %reduce-scatter.2.cloned.1.call-done = bf16[32,1,6144]{2,0,1:T(8,128)(2,1)} async-done(((bf16[512,1,6144]{2,0,1:T(8,128)(2,1)}), bf16[32,1,6144]{2,0,1:T(8,128)(2,1)}) %reduce-scatter.2.cloned.1.call-update) | async-done | bytes 393232 | tf_op jit(solution)/shard_map/reduce_scatter | solution.py:96
  209.6 1.8 copy.56
  211.4 6.1 %all-to-all-start = ((bf16[32,1,8,768]{3,0,1,2:T(8,128)(2,1)}), bf16[32,1,8,768]{3,0,1,2:T(8,128)(2,1)S(1)}, u32[]{:S(2)}, u32[]{:S(2)}) async-start(bf16[32,1,8,768]{3,0,1,2:T(8,128)(2,1)} %bitcast.84), calls=%async_computation.1 | async-start | bytes 786432 | tf_op jit(solution)/shard_map/all_to_all | solution.py:106
  217.5 8.0 %all-to-all-done = bf16[32,1,8,768]{3,0,1,2:T(8,128)(2,1)S(1)} async-done(((bf16[32,1,8,768]{3,0,1,2:T(8,128)(2,1)}), bf16[32,1,8,768]{3,0,1,2:T(8,128)(2,1)S(1)}, u32[]{:S(2)}, u32[]{:S(2)}) %all-to-all-start) | async-done | bytes 393248 | tf_op jit(solution)/shard_map/all_to_all | solution.py:106
  225.5 0.4 convolution_bitcast_fusion
  225.9 0.7 fusion.32
  (38 shorter events, 1.7 us)
Async XLA Ops:
  6.5 6.4 %copy-start = (bf16[64,1,128,128]{3,2,1,0:T(8,128)(2,1)S(1)}, bf16[64,1,128,128]{3,2,1,0:T(8,128)(2,1)}, u32[]{:S(2)}) copy-start(bf16[64,1,128,128]{3,2,1,0:T(8,128)(2,1)} %param.15) | copy-start | bytes 6291460
  6.5 10.1 %copy-start.1 = (bf16[64,768]{1,0:T(8,128)(2,1)S(1)}, bf16[64,768]{1,0:T(8,128)(2,1)}, u32[]{:S(2)}) copy-start(bf16[64,768]{1,0:T(8,128)(2,1)} %param.13) | copy-start | bytes 294916
  6.5 23.7 %copy-start.3 = (f32[768]{0:T(1024)S(1)}, f32[768]{0:T(1024)}, u32[]{:S(2)}) copy-start(f32[768]{0:T(1024)} %param.20) | copy-start | bytes 9220
  6.5 102.8 %all-gather.3.cloned.1.call-start = ((), (), s32[]{:S(2)}) async-start(), calls=%async_computation.3 | async-start | bytes 6684672 | tf_op jit(solution)/shard_map/all_gather | solution.py:92
  47.6 162.0 %reduce-scatter.2.cloned.1.call-start = ((), (), s32[]{:S(2)}) async-start(), calls=%async_computation.2 | async-start | bytes 6684672 | tf_op jit(solution)/shard_map/reduce_scatter | solution.py:96
  109.3 8.1 %copy-start.5 = (bf16[512,6144]{1,0:T(8,128)(2,1)S(1)}, bf16[512,6144]{1,0:T(8,128)(2,1)}, u32[]{:S(2)}) copy-start(bf16[512,6144]{1,0:T(8,128)(2,1)} %all-gather.3.cloned.1.call-done) | copy-start | bytes 18874372
  109.3 14.6 %slice-start = ((s8[6291456]{0:T(1024)(128)(4,1)}), s8[4194304]{0:T(1024)(128)(4,1)S(1)}, s32[]{:S(2)}) async-start(s8[6291456]{0:T(1024)(128)(4,1)} %bitcast.88), calls=%async_computation.4 | async-start | bytes 8388608
  117.5 6.5 %slice-start.1 = ((s8[6291456]{0:T(1024)(128)(4,1)}), s8[2097152]{0:T(1024)(128)(4,1)S(1)}, s32[]{:S(2)}) async-start(s8[6291456]{0:T(1024)(128)(4,1)} %bitcast.88), calls=%async_computation.5 | async-start | bytes 4194304
  129.3 0.7 copy-start.2
  129.3 88.1 %copy-start.4 = (s32[64,2]{0,1:T(2,128)S(1)}, s32[64,2]{0,1:T(2,128)}, u32[]{:S(2)}) copy-start(s32[64,2]{0,1:T(2,128)} %param.22) | copy-start | bytes 1540
  211.4 14.1 %all-to-all-start = ((bf16[32,1,8,768]{3,0,1,2:T(8,128)(2,1)}), bf16[32,1,8,768]{3,0,1,2:T(8,128)(2,1)S(1)}, u32[]{:S(2)}, u32[]{:S(2)}) async-start(bf16[32,1,8,768]{3,0,1,2:T(8,128)(2,1)} %bitcast.84), calls=%async_computation.1 | async-start | bytes 786432 | tf_op jit(solution)/shard_map/all_to_all | solution.py:106
Sparse Core Ops, SparseCore 0:
  47.7 61.5 all-gather.2
  129.5 80.0 reduce-scatter.1
where the time goes:
time: 234 us; the launch traced here: 233 us
  waiting for transfers between devices  136 us (58%)
  blocking collectives  42.2 us (18%)
  matrix products  26.5 us (11%)
  between operations  13.6 us (6%)
  starting transfers between devices  6.1 us (3%)
  local copies, waits for them, and re-layouts  4.74 us (2%)
  other arithmetic  4.38 us (2%)
    reduce_scatter x1, waiting for transfers between devices, on_device(): lax.psum_scatter(jnp.einsum('enf,efd->ned', activation, w_down, preferred...  66.2 us
    all_gather x1, waiting for transfers between devices, on_device(): slab_rows = lax.all_gather(outgoing, 'attn', axis=1, tiled=True)  61.7 us
    all_gather x1, blocking collectives, on_device(): whole_rows = lax.all_gather(narrow, 'expert', axis=1, tiled=True)  16.2 us
    psum x1, blocking collectives, on_device(): lax.psum(jnp.sum(hidden_state * hidden_state, axis=1), 'expert')  13.5 us
    psum x1, blocking collectives, on_device(): lax.psum(jnp.dot(normed, router_weight, precision=lax.Precision.HIGHEST),...  12.5 us
    dot_general x1, matrix products, on_device(): jnp.einsum('end,edf->enf', slab_rows, w_gate, preferred_element_type=jnp....  8.13 us
    all_to_all x1, waiting for transfers between devices, on_device(): lax.all_to_all(expert_result, 'expert', split_axis=2, concat_axis=1, tile...  8.04 us
    dot_general x1, matrix products, on_device(): jnp.einsum('end,edf->enf', slab_rows, w_up, preferred_element_type=jnp.fl...  6.47 us
  transfers between devices with their start and end apart: 3, of which 3 were waited for; matrix products, arithmetic and copies ran while one was open for 0% of the time, Pallas kernels for 0%

commit v1 on v0

--- a/solution.py
+++ b/solution.py
@@ -8,9 +8,54 @@
 D = 6144
 E = 8
 CAP = 32
+SIDE = 4
+HALF = CAP // 2
 
 
 EPSILON = 1e-05
+
+
+def shift_z(value, step):
+    pairs = [
+        (z * SIDE + x, ((z + step) % SIDE) * SIDE + x) for z in range(SIDE) for x in range(SIDE)
+    ]
+    return lax.ppermute(value, "attn", pairs)
+
+
+def shift_x(value, step):
+    pairs = [
+        (z * SIDE + x, z * SIDE + (x + step) % SIDE) for z in range(SIDE) for x in range(SIDE)
+    ]
+    return lax.ppermute(value, "attn", pairs)
+
+
+def spread_near(block, shift):
+    return shift(block, 1), shift(block, -1)
+
+
+def spread_far(behind, ahead, shift):
+    half = behind.shape[0] // 2
+    return jnp.concatenate([shift(behind[:half], 1), shift(ahead[half:], -1)], axis=0)
+
+
+def split_three(value):
+    high = value.astype(jnp.bfloat16)
+    rest = value - high.astype(jnp.float32)
+    middle = rest.astype(jnp.bfloat16)
+    low = (rest - middle.astype(jnp.float32)).astype(jnp.bfloat16)
+    return [high, middle, low]
+
+
+def ring_sum(behind, own, ahead, far, shift):
+    half = far.shape[0] // 2
+    sent = far.astype(jnp.bfloat16)
+    far_up = shift(sent[:half], 1).astype(jnp.float32)
+    far_down = shift(sent[half:], -1).astype(jnp.float32)
+    up = jnp.concatenate([ahead[:half] + far_up, ahead[half:]], axis=0)
+    down = jnp.concatenate([behind[:half], behind[half:] + far_down], axis=0)
+    got_up = shift(up.astype(jnp.bfloat16), 1).astype(jnp.float32)
+    got_down = shift(down.astype(jnp.bfloat16), -1).astype(jnp.float32)
+    return own + got_up + got_down
 
 
 def on_device(
@@ -34,7 +79,6 @@
     cache_slots = key_cache.shape[2]
     head_size = key_cache.shape[3]
     group_size = query.shape[1] // (kv_local * head_size)
-    local_experts = w_gate.shape[0]
     expert_devices = lax.axis_size("expert")
     score_scale = 1.0 / math.sqrt(head_size)
     queries = query.reshape(row_count, kv_local, group_size, head_size)
@@ -64,10 +108,33 @@
         jnp.float32
     ).reshape(row_count, kv_local, 1, head_size)
     hidden_state = resid.astype(jnp.float32) + attended.reshape(row_count, width_local)
-    total_square = lax.psum(jnp.sum(hidden_state * hidden_state, axis=1), "expert")
-    normed = hidden_state * lax.rsqrt(total_square / D + EPSILON)[:, None] * norm_gain
-    logits = lax.psum(jnp.dot(normed, router_weight, precision=lax.Precision.HIGHEST), "expert")
-    narrow = normed.astype(jnp.bfloat16)
+
+    gained = hidden_state * norm_gain
+    sums = jnp.concatenate(
+        [
+            jnp.sum(hidden_state * hidden_state, axis=1, keepdims=True),
+            jnp.dot(gained, router_weight, precision=lax.Precision.HIGHEST),
+        ],
+        axis=1,
+    )
+    pieces = split_three(sums)
+    columns = sums.shape[1]
+    payload = jnp.concatenate(
+        [gained.astype(jnp.bfloat16)]
+        + pieces
+        + [jnp.zeros((row_count, 128 - 3 * columns), jnp.bfloat16)],
+        axis=1,
+    )
+    gathered = lax.all_gather(payload, "expert", axis=0)
+    whole_rows = gathered[:, :, :width_local]
+    side = gathered[:, :, width_local:].astype(jnp.float32)
+    sums = jnp.sum(
+        side[:, :, :columns] + side[:, :, columns : 2 * columns] + side[:, :, 2 * columns : 3 * columns],
+        axis=0,
+    )
+    scale = lax.rsqrt(sums[:, :1] / D + EPSILON)
+    logits = sums[:, 1:] * scale
+
     choose = expert_ids[:, :, None] == lax.broadcasted_iota(jnp.int32, (1, 1, E), 2)
     picked = jnp.sum(jnp.where(choose, logits[:, None, :], jnp.float32(0.0)), axis=2)
     first_weight = 1.0 / (1.0 + jnp.exp(picked[:, 1] - picked[:, 0]))
@@ -75,34 +142,64 @@
     hits = jnp.sum(choose.astype(jnp.int32), axis=1)
     before = jnp.cumsum(hits, axis=0) - hits
     slot_index = jnp.sum(jnp.where(choose, before[:, None, :], 0), axis=2)
-    slot_match = slot_index[:, :, None] == lax.broadcasted_iota(jnp.int32, (1, 1, CAP), 2)
-    selector = jnp.einsum(
-        "rke,rkc->ecr",
-        choose.astype(jnp.bfloat16),
-        slot_match.astype(jnp.bfloat16),
+    own_expert = lax.axis_index("expert")
+    own_slot = jnp.sum(jnp.where(expert_ids == own_expert, slot_index + 1, 0), axis=1) - 1
+    own_selector = (
+        lax.broadcasted_iota(jnp.int32, (CAP, row_count), 0) == own_slot[None, :]
+    )
+    outgoing = jnp.einsum(
+        "cr,erd->ced",
+        own_selector.astype(jnp.bfloat16),
+        whole_rows,
         preferred_element_type=jnp.float32,
-    ).astype(jnp.bfloat16)
-    whole_rows = lax.all_gather(narrow, "expert", axis=1, tiled=True)
-    own_selector = lax.dynamic_slice_in_dim(
-        selector, lax.axis_index("expert") * local_experts, local_experts, 0
-    )
-    outgoing = jnp.einsum(
-        "ecr,rd->ecd", own_selector, whole_rows, preferred_element_type=jnp.float32
-    ).astype(jnp.bfloat16)
-    slab_rows = lax.all_gather(outgoing, "attn", axis=1, tiled=True)
-    gate_part = jnp.einsum("end,edf->enf", slab_rows, w_gate, preferred_element_type=jnp.float32)
-    up_part = jnp.einsum("end,edf->enf", slab_rows, w_up, preferred_element_type=jnp.float32)
-    activation = (jax.nn.silu(gate_part) * up_part).astype(jnp.bfloat16)
-    summed = lax.psum_scatter(
-        jnp.einsum("enf,efd->ned", activation, w_down, preferred_element_type=jnp.float32).astype(
-            jnp.bfloat16
-        ),
-        "attn",
-        scatter_dimension=0,
-        tiled=True,
-    )
-    expert_result = summed
-    expert_result = expert_result.reshape(CAP, local_experts, expert_devices, width_local)
+    ).reshape(CAP, D)
+    own_scale = jnp.sum(
+        jnp.where(own_selector, scale[:, 0][None, :], jnp.float32(0.0)), axis=1, keepdims=True
+    )
+    outgoing = (outgoing * own_scale).astype(jnp.bfloat16)
+
+    gate_weight = w_gate[0]
+    up_weight = w_up[0]
+    down_weight = w_down[0]
+
+    def feed(rows):
+        gate_part = jnp.dot(rows, gate_weight, preferred_element_type=jnp.float32)
+        up_part = jnp.dot(rows, up_weight, preferred_element_type=jnp.float32)
+        activation = (jax.nn.silu(gate_part) * up_part).astype(jnp.bfloat16)
+        return jnp.dot(activation, down_weight, preferred_element_type=jnp.float32)
+
+    a_own, b_own = outgoing[:HALF], outgoing[HALF:]
+    a_behind, a_ahead = spread_near(a_own, shift_z)
+    b_behind, b_ahead = spread_near(b_own, shift_x)
+    a_far = spread_far(a_behind, a_ahead, shift_z)
+    b_far = spread_far(b_behind, b_ahead, shift_x)
+    a_line = jnp.concatenate([a_own, a_behind, a_ahead, a_far], axis=0)
+    b_line = jnp.concatenate([b_own, b_behind, b_ahead, b_far], axis=0)
+    line = a_line.shape[0]
+    aa_behind, aa_ahead = spread_near(a_line, shift_x)
+    bb_behind, bb_ahead = spread_near(b_line, shift_z)
+    aa_far = spread_far(aa_behind, aa_ahead, shift_x)
+    bb_far = spread_far(bb_behind, bb_ahead, shift_z)
+
+    part_own = feed(jnp.concatenate([a_line, b_line], axis=0))
+    part_near = feed(jnp.concatenate([aa_behind, bb_behind, aa_ahead, bb_ahead], axis=0))
+    part_far = feed(jnp.concatenate([aa_far, bb_far], axis=0))
+
+    a_sum = ring_sum(
+        part_near[:line], part_own[:line], part_near[2 * line : 3 * line], part_far[:line], shift_x
+    )
+    b_sum = ring_sum(
+        part_near[line : 2 * line], part_own[line:], part_near[3 * line :], part_far[line:], shift_z
+    )
+    a_result = ring_sum(
+        a_sum[HALF : 2 * HALF], a_sum[:HALF], a_sum[2 * HALF : 3 * HALF], a_sum[3 * HALF :], shift_z
+    )
+    b_result = ring_sum(
+        b_sum[HALF : 2 * HALF], b_sum[:HALF], b_sum[2 * HALF : 3 * HALF], b_sum[3 * HALF :], shift_x
+    )
+    expert_result = jnp.concatenate([a_result, b_result], axis=0).astype(jnp.bfloat16)
+
+    expert_result = expert_result.reshape(CAP, 1, expert_devices, width_local)
     returned = lax.all_to_all(expert_result, "expert", split_axis=2, concat_axis=1, tiled=True)
     flat_result = returned.reshape(CAP * E, width_local)
     target_index = slot_index * E + expert_ids

time: 234 us -> 193 us (0.82)
  waiting for transfers between devices: 136 us -> 52.6 us
  starting transfers between devices: 6.1 us -> 58.5 us
  blocking collectives: 42.2 us -> 15.4 us
  matrix products: 26.5 us -> 41.9 us
  between operations: 13.6 us -> 0.72 us
  other arithmetic: 4.38 us -> 13.1 us
  local copies, waits for them, and re-layouts: 4.74 us -> 10 us
    reduce_scatter x1 -> x0, waiting for transfers between devices: 66.2 us -> none  [on_device(): lax.psum_scatter(jnp.einsum('enf,efd->ned', activation, w_down, preferred...]
    all_gather x1 -> x0, waiting for transfers between devices: 61.7 us -> none  [on_device(): slab_rows = lax.all_gather(outgoing, 'attn', axis=1, tiled=True)]
    ppermute x0 -> x32, starting transfers between devices: none -> 46.1 us  [the longest x16 23.3 us: shift_z(): return lax.ppermute(value, 'attn', pairs)]
    ppermute x0 -> x32, waiting for transfers between devices: none -> 44.6 us  [the longest x16 25.6 us: shift_x(): return lax.ppermute(value, 'attn', pairs)]
    psum x2 -> x0, blocking collectives: 26 us -> none  [the longest x1 13.5 us: on_device(): lax.psum(jnp.sum(hidden_state * hidden_state, axis=1), 'expert')]
    dot_general x6 -> x8, matrix products: 21.7 us -> 38.6 us  [the longest x3 28.7 us: feed(): return jnp.dot(activation, down_weight, preferred_element_type=jnp.float32)]
    all_to_all x1, starting transfers between devices: 6.05 us -> 12.4 us  [on_device(): lax.all_to_all(expert_result, 'expert', split_axis=2, concat_axis=1, tile...]
    another operation x0 -> x6, other arithmetic: none -> 5.85 us
  transfers between devices with their start and end apart: 3 -> 33, of which waited for: 3 -> 11; matrix products, arithmetic and copies ran while one was open for 0% -> 17% of each run, Pallas kernels for 0% -> 0%
where the time goes in v1:
time: 193 us; the launch traced here: 192 us
  starting transfers between devices  58.5 us (30%)
  waiting for transfers between devices  52.6 us (27%)
  matrix products  41.9 us (22%)
  blocking collectives  15.4 us (8%)
  other arithmetic  13.1 us (7%)
  local copies, waits for them, and re-layouts  10 us (5%)
    dot_general x3, matrix products, feed(): return jnp.dot(activation, down_weight, preferred_element_type=jnp.float32)  28.7 us
    ppermute x16, waiting for transfers between devices, shift_x(): return lax.ppermute(value, 'attn', pairs)  25.6 us
    ppermute x16, starting transfers between devices, shift_z(): return lax.ppermute(value, 'attn', pairs)  23.3 us
    ppermute x16, starting transfers between devices, shift_x(): return lax.ppermute(value, 'attn', pairs)  22.8 us
    ppermute x16, waiting for transfers between devices, shift_z(): return lax.ppermute(value, 'attn', pairs)  19 us
    all_gather x1, blocking collectives, on_device(): gathered = lax.all_gather(payload, 'expert', axis=0)  15.4 us
    all_to_all x1, starting transfers between devices, on_device(): lax.all_to_all(expert_result, 'expert', split_axis=2, concat_axis=1, tile...  12.4 us
    dot_general x3, matrix products, feed(): up_part = jnp.dot(rows, up_weight, preferred_element_type=jnp.float32)  9.46 us
  transfers between devices with their start and end apart: 33, of which 11 were waited for; matrix products, arithmetic and copies ran while one was open for 17% of the time, Pallas kernels for 0%

profile of v1, /device:TPU:1, one launch (start us, length us, event | category | flops | bytes accessed | tf_op | source)
XLA Modules:
  0.0 192.2 jit_solution(11548785981863615106)
XLA Ops:
  6.9 15.4 %all-gather = bf16[512,896]{1,0:T(8,128)(2,1)S(1)} all-gather(bf16[64,896]{1,0:T(8,128)(2,1)S(1)} %concatenate.70), channel_id=2, replica_groups=mesh['attn'=16,'expert'=8] {'expert'}, dimensions={0}, use_global_device_ids=true | all-gather | bytes 1032192 | tf_op jit(solution)/shard_map/all_gather | solution.py:128
  27.6 4.9 %collective-permute-done = bf16[16,6144]{1,0:T(8,128)(2,1)S(1)} collective-permute-done((bf16[16,6144]{1,0:T(8,128)(2,1)S(1)}, bf16[16,6144]{1,0:T(8,128)(2,1)S(1)}, u32[]{:S(2)}, u32[]{:S(2)}) %collective-permute-start) | collective-permute-done | bytes 196640 | tf_op jit(solution)/shard_map/ppermute | solution.py:22
  32.6 2.7 %collective-permute-start.3 = (bf16[8,6144]{1,0:T(8,128)(2,1)S(1)}, bf16[8,6144]{1,0:T(8,128)(2,1)S(1)}, u32[]{:S(2)}, u32[]{:S(2)}) collective-permute-start(bf16[8,6144]{1,0:T(8,128)(2,1)S(1)} %slice.255), channel_id=1, source_target_pairs={{0,96},{8,104},{16,112},{24,120},{32,0},{40,8},{48,16},{56,24},{64... | collective-permute-start | bytes 294920 | tf_op jit(solution)/shard_map/ppermute | solution.py:22
  43.2 2.7 %collective-permute-start.7 = (bf16[8,6144]{1,0:T(8,128)(2,1)S(1)}, bf16[8,6144]{1,0:T(8,128)(2,1)S(1)}, u32[]{:S(2)}, u32[]{:S(2)}) collective-permute-start(bf16[8,6144]{1,0:T(8,128)(2,1)S(1)} %slice.258), channel_id=1, source_target_pairs={{0,24},{8,0},{16,8},{24,16},{32,56},{40,32},{48,40},{56,48},{64,88... | collective-permute-start | bytes 294920 | tf_op jit(solution)/shard_map/ppermute | solution.py:29
  46.0 17.0 %collective-permute-done.6 = bf16[8,6144]{1,0:T(8,128)(2,1)S(1)} collective-permute-done((bf16[8,6144]{1,0:T(8,128)(2,1)S(1)}, bf16[8,6144]{1,0:T(8,128)(2,1)S(1)}, u32[]{:S(2)}, u32[]{:S(2)}) %collective-permute-start.6) | collective-permute-done | bytes 98336 | tf_op jit(solution)/shard_map/ppermute | solution.py:29
  63.1 2.9 %collective-permute-start.11 = (bf16[64,6144]{1,0:T(8,128)(2,1)S(1)}, bf16[64,6144]{1,0:T(8,128)(2,1)S(1)}, u32[]{:S(2)}, u32[]{:S(2)}) collective-permute-start(bf16[64,6144]{1,0:T(8,128)(2,1)S(1)} %get-tuple-element.48), channel_id=1, source_target_pairs={{0,96},{8,104},{16,112},{24,120},{32,0},{40,8},{48,16},{56,24},{64... | collective-permute-start | bytes 2359304 | tf_op jit(solution)/shard_map/ppermute | solution.py:22
  66.0 3.9 %fusion.9 = f32[128,512]{1,0:T(8,128)S(1)} fusion(bf16[128,6144]{1,0:T(8,128)(2,1)S(1)} %get-tuple-element.47, bf16[1,6144,512]{2,1,0:T(8,128)(2,1)} %param.24), kind=kOutput, calls=%fused_computation.10 | convolution fusion | flops 805306368 | bytes 8126464 | tf_op jit(solution)/shard_map/dot_general | solution.py:167
  70.2 2.7 %collective-permute-start.13 = (bf16[32,6144]{1,0:T(8,128)(2,1)S(1)}, bf16[32,6144]{1,0:T(8,128)(2,1)S(1)}, u32[]{:S(2)}, u32[]{:S(2)}) collective-permute-start(bf16[32,6144]{1,0:T(8,128)(2,1)S(1)} %slice.262), channel_id=1, source_target_pairs={{0,24},{8,0},{16,8},{24,16},{32,56},{40,32},{48,40},{56,48},{64,88... | collective-permute-start | bytes 1179656 | tf_op jit(solution)/shard_map/ppermute | solution.py:29
  72.9 8.6 %collective-permute-done.9 = bf16[64,6144]{1,0:T(8,128)(2,1)S(1)} collective-permute-done((bf16[64,6144]{1,0:T(8,128)(2,1)S(1)}, bf16[64,6144]{1,0:T(8,128)(2,1)S(1)}, u32[]{:S(2)}, u32[]{:S(2)}) %collective-permute-start.9) | collective-permute-done | bytes 786464 | tf_op jit(solution)/shard_map/ppermute | solution.py:22
  83.1 2.7 %collective-permute-start.15 = (bf16[32,6144]{1,0:T(8,128)(2,1)}, bf16[32,6144]{1,0:T(8,128)(2,1)}, u32[]{:S(2)}, u32[]{:S(2)}) collective-permute-start(bf16[32,6144]{1,0:T(8,128)(2,1)} %slice.264), channel_id=1, source_target_pairs={{0,96},{8,104},{16,112},{24,120},{32,0},{40,8},{48,16},{56,24},{64... | collective-permute-start | bytes 1179656 | tf_op jit(solution)/shard_map/ppermute | solution.py:22
  89.4 12.7 %fusion.102 = (bf16[256,6144]{1,0:T(8,128)(2,1)}, f32[256,6144]{1,0:T(8,128)}) fusion(bf16[1,512,6144]{2,1,0:T(8,128)(2,1)} %param.25, f32[256,512]{1,0:T(8,128)S(1)} %fusion.7, bf16[256,6144]{1,0:T(8,128)(2,1)} %copy-done.5, bf16[1,6144,512]{2,1,0:T(8,128)(2,1)} %param.23), kind=kOutput, calls=%fused_computation.163 | convolution fusion | flops 3223584768 | bytes 25690112 | tf_op jit(solution)/shard_map/dot_general | solution.py:169
  104.3 3.8 %fusion.5 = f32[128,512]{1,0:T(8,128)S(1)} fusion(bf16[128,6144]{1,0:T(8,128)(2,1)S(1)} %constant_dynamic-update-slice_fusion.24, bf16[1,6144,512]{2,1,0:T(8,128)(2,1)} %param.24), kind=kOutput, calls=%fused_computation.6 | convolution fusion | flops 805306368 | bytes 8126464 | tf_op jit(solution)/shard_map/dot_general | solution.py:167
  108.1 7.7 %convolution_convert_fusion = bf16[128,6144]{1,0:T(8,128)(2,1)} fusion(bf16[1,512,6144]{2,1,0:T(8,128)(2,1)} %param.25, f32[128,512]{1,0:T(8,128)S(1)} %fusion.5, bf16[128,6144]{1,0:T(8,128)(2,1)S(1)} %constant_dynamic-update-slice_fusion.24, bf16[1,6144,512]{2,1,0:T(8,128)(2,1)} %param.23), kind=kOutput, calls=%fused_computation | convolution fusion | flops 1611792384 | bytes 15990784 | tf_op jit(solution)/shard_map/dot_general | solution.py:169
  120.2 2.7 %collective-permute-start.26 = (bf16[32,6144]{1,0:T(8,128)(2,1)S(1)}, bf16[32,6144]{1,0:T(8,128)(2,1)S(1)}, u32[]{:S(2)}, u32[]{:S(2)}) collective-permute-start(bf16[32,6144]{1,0:T(8,128)(2,1)S(1)} %get-tuple-element.24), channel_id=1, source_target_pairs={{0,96},{8,104},{16,112},{24,120},{32,0},{40,8},{48,16},{56,24},{64... | collective-permute-start | bytes 1179656 | tf_op jit(solution)/shard_map/ppermute | solution.py:22
  123.0 2.8 %collective-permute-done.16 = bf16[32,6144]{1,0:T(8,128)(2,1)S(1)} collective-permute-done((bf16[32,6144]{1,0:T(8,128)(2,1)S(1)}, bf16[32,6144]{1,0:T(8,128)(2,1)S(1)}, u32[]{:S(2)}, u32[]{:S(2)}) %collective-permute-start.16) | collective-permute-done | bytes 393248 | tf_op jit(solution)/shard_map/ppermute | solution.py:29
  136.3 2.7 %collective-permute-start.19 = (bf16[64,6144]{1,0:T(8,128)(2,1)}, bf16[64,6144]{1,0:T(8,128)(2,1)}, u32[]{:S(2)}, u32[]{:S(2)}) collective-permute-start(bf16[64,6144]{1,0:T(8,128)(2,1)} %pad_maximum_fusion.1), channel_id=1, source_target_pairs={{0,24},{8,0},{16,8},{24,16},{32,56},{40,32},{48,40},{56,48},{64,88... | collective-permute-start | bytes 2359304 | tf_op jit(solution)/shard_map/ppermute | solution.py:29
  138.9 8.2 %fusion.3 = f32[128,6144]{1,0:T(8,128)} fusion(bf16[1,512,6144]{2,1,0:T(8,128)(2,1)} %param.25, f32[128,512]{1,0:T(8,128)S(1)} %fusion.9, bf16[128,6144]{1,0:T(8,128)(2,1)S(1)} %copy-done.3, bf16[1,6144,512]{2,1,0:T(8,128)(2,1)} %param.23), kind=kOutput, calls=%fused_computation.4 | convolution fusion | flops 1611005952 | bytes 17563648 | tf_op jit(solution)/shard_map/dot_general | solution.py:169
  147.2 3.1 %collective-permute-done.17 = bf16[64,6144]{1,0:T(8,128)(2,1)} collective-permute-done((bf16[64,6144]{1,0:T(8,128)(2,1)}, bf16[64,6144]{1,0:T(8,128)(2,1)}, u32[]{:S(2)}, u32[]{:S(2)}) %collective-permute-start.17) | collective-permute-done | bytes 786464 | tf_op jit(solution)/shard_map/ppermute | solution.py:29
  150.3 3.4 %fusion.93 = (bf16[64,6144]{1,0:T(8,128)(2,1)S(1)}, f32[64,6144]{1,0:T(8,128)S(1)}, bf16[64,6144]{1,0:T(8,128)(2,1)S(1)}, f32[64,6144]{1,0:T(8,128)S(1)}) fusion(bf16[64,6144]{1,0:T(8,128)(2,1)} %collective-permute-done.19, bf16[64,6144]{1,0:T(8,128)(2,1)} %collective-permute-done.17, f32[128,6144]{1,0:T(8,128)} %fusion.3, ...), kind=kLoop, calls=%fused_computation.156 | loop fusion | flops 3932160 | bytes 11010048 | tf_op jit(solution)/shard_map/convert.24
  156.6 3.5 %collective-permute-start.30 = (bf16[8,6144]{1,0:T(8,128)(2,1)S(1)}, bf16[8,6144]{1,0:T(8,128)(2,1)S(1)}, u32[]{:S(2)}, u32[]{:S(2)}) collective-permute-start(bf16[8,6144]{1,0:T(8,128)(2,1)S(1)} %get-tuple-element.34), channel_id=1, source_target_pairs={{0,24},{8,0},{16,8},{24,16},{32,56},{40,32},{48,40},{56,48},{64,88... | collective-permute-start | bytes 294920 | tf_op jit(solution)/shard_map/ppermute | solution.py:29
  160.3 2.7 %collective-permute-start.23 = (bf16[16,6144]{1,0:T(8,128)(2,1)S(1)}, bf16[16,6144]{1,0:T(8,128)(2,1)S(1)}, u32[]{:S(2)}, u32[]{:S(2)}) collective-permute-start(bf16[16,6144]{1,0:T(8,128)(2,1)S(1)} %pad_maximum_fusion.6), channel_id=1, source_target_pairs={{0,96},{8,104},{16,112},{24,120},{32,0},{40,8},{48,16},{56,24},{64... | collective-permute-start | bytes 589832 | tf_op jit(solution)/shard_map/ppermute | solution.py:22
  163.2 2.7 %collective-permute-start.31 = (bf16[16,6144]{1,0:T(8,128)(2,1)S(1)}, bf16[16,6144]{1,0:T(8,128)(2,1)S(1)}, u32[]{:S(2)}, u32[]{:S(2)}) collective-permute-start(bf16[16,6144]{1,0:T(8,128)(2,1)S(1)} %pad_maximum_fusion.8), channel_id=1, source_target_pairs={{0,24},{8,0},{16,8},{24,16},{32,56},{40,32},{48,40},{56,48},{64,88... | collective-permute-start | bytes 589832 | tf_op jit(solution)/shard_map/ppermute | solution.py:29
  170.6 12.4 %all-to-all-start = ((bf16[32,1,8,768]{3,0,1,2:T(8,128)(2,1)}), bf16[32,1,8,768]{3,0,1,2:T(8,128)(2,1)S(1)}, u32[]{:S(2)}, u32[]{:S(2)}) async-start(bf16[32,1,8,768]{3,0,1,2:T(8,128)(2,1)} %pad_maximum_fusion.4), calls=%async_computation | async-start | bytes 786432 | tf_op jit(solution)/shard_map/all_to_all | solution.py:203
  183.0 8.0 %all-to-all-done = bf16[32,1,8,768]{3,0,1,2:T(8,128)(2,1)S(1)} async-done(((bf16[32,1,8,768]{3,0,1,2:T(8,128)(2,1)}), bf16[32,1,8,768]{3,0,1,2:T(8,128)(2,1)S(1)}, u32[]{:S(2)}, u32[]{:S(2)}) %all-to-all-start) | async-done | bytes 393248 | tf_op jit(solution)/shard_map/all_to_all | solution.py:203
  (168 shorter events, 51.5 us)
Async XLA Ops:
  23.5 8.9 %collective-permute-start = (bf16[16,6144]{1,0:T(8,128)(2,1)S(1)}, bf16[16,6144]{1,0:T(8,128)(2,1)S(1)}, u32[]{:S(2)}, u32[]{:S(2)}) collective-permute-start(bf16[16,6144]{1,0:T(8,128)(2,1)S(1)} %get-tuple-element.42), channel_id=1, source_target_pairs={{0,32},{8,40},{16,48},{24,56},{32,64},{40,72},{48,80},{56,88},{64,... | collective-permute-start | bytes 589832 | tf_op jit(solution)/shard_map/ppermute | solution.py:22
  25.2 7.3 %collective-permute-start.1 = (bf16[16,6144]{1,0:T(8,128)(2,1)S(1)}, bf16[16,6144]{1,0:T(8,128)(2,1)S(1)}, u32[]{:S(2)}, u32[]{:S(2)}) collective-permute-start(bf16[16,6144]{1,0:T(8,128)(2,1)S(1)} %get-tuple-element.42), channel_id=1, source_target_pairs={{0,96},{8,104},{16,112},{24,120},{32,0},{40,8},{48,16},{56,24},{64... | collective-permute-start | bytes 589832 | tf_op jit(solution)/shard_map/ppermute | solution.py:22
  40.1 29.8 %collective-permute-start.8 = (bf16[64,6144]{1,0:T(8,128)(2,1)S(1)}, bf16[64,6144]{1,0:T(8,128)(2,1)S(1)}, u32[]{:S(2)}, u32[]{:S(2)}) collective-permute-start(bf16[64,6144]{1,0:T(8,128)(2,1)S(1)} %constant_dynamic-update-slice_fusion.10), channel_id=1, source_target_pairs={{0,8},{8,16},{16,24},{24,0},{32,40},{40,48},{48,56},{56,32},{64,72... | collective-permute-start | bytes 2359304 | tf_op jit(solution)/shard_map/ppermute | solution.py:29
  40.2 29.9 %collective-permute-start.10 = (bf16[64,6144]{1,0:T(8,128)(2,1)S(1)}, bf16[64,6144]{1,0:T(8,128)(2,1)S(1)}, u32[]{:S(2)}, u32[]{:S(2)}) collective-permute-start(bf16[64,6144]{1,0:T(8,128)(2,1)S(1)} %constant_dynamic-update-slice_fusion.10), channel_id=1, source_target_pairs={{0,24},{8,0},{16,8},{24,16},{32,56},{40,32},{48,40},{56,48},{64,88... | collective-permute-start | bytes 2359304 | tf_op jit(solution)/shard_map/ppermute | solution.py:29
  43.1 19.9 %collective-permute-start.6 = (bf16[8,6144]{1,0:T(8,128)(2,1)S(1)}, bf16[8,6144]{1,0:T(8,128)(2,1)S(1)}, u32[]{:S(2)}, u32[]{:S(2)}) collective-permute-start(bf16[8,6144]{1,0:T(8,128)(2,1)S(1)} %slice.257), channel_id=1, source_target_pairs={{0,8},{8,16},{16,24},{24,0},{32,40},{40,48},{48,56},{56,32},{64,72... | collective-permute-start | bytes 294920 | tf_op jit(solution)/shard_map/ppermute | solution.py:29
  43.2 19.8 %collective-permute-start.7 = (bf16[8,6144]{1,0:T(8,128)(2,1)S(1)}, bf16[8,6144]{1,0:T(8,128)(2,1)S(1)}, u32[]{:S(2)}, u32[]{:S(2)}) collective-permute-start(bf16[8,6144]{1,0:T(8,128)(2,1)S(1)} %slice.258), channel_id=1, source_target_pairs={{0,24},{8,0},{16,8},{24,16},{32,56},{40,32},{48,40},{56,48},{64,88... | collective-permute-start | bytes 294920 | tf_op jit(solution)/shard_map/ppermute | solution.py:29
  63.1 18.4 %collective-permute-start.9 = (bf16[64,6144]{1,0:T(8,128)(2,1)S(1)}, bf16[64,6144]{1,0:T(8,128)(2,1)S(1)}, u32[]{:S(2)}, u32[]{:S(2)}) collective-permute-start(bf16[64,6144]{1,0:T(8,128)(2,1)S(1)} %get-tuple-element.48), channel_id=1, source_target_pairs={{0,32},{8,40},{16,48},{24,56},{32,64},{40,72},{48,80},{56,88},{64,... | collective-permute-start | bytes 2359304 | tf_op jit(solution)/shard_map/ppermute | solution.py:22
  63.1 19.1 %collective-permute-start.11 = (bf16[64,6144]{1,0:T(8,128)(2,1)S(1)}, bf16[64,6144]{1,0:T(8,128)(2,1)S(1)}, u32[]{:S(2)}, u32[]{:S(2)}) collective-permute-start(bf16[64,6144]{1,0:T(8,128)(2,1)S(1)} %get-tuple-element.48), channel_id=1, source_target_pairs={{0,96},{8,104},{16,112},{24,120},{32,0},{40,8},{48,16},{56,24},{64... | collective-permute-start | bytes 2359304 | tf_op jit(solution)/shard_map/ppermute | solution.py:22
  70.0 32.1 %collective-permute-start.12 = (bf16[32,6144]{1,0:T(8,128)(2,1)S(1)}, bf16[32,6144]{1,0:T(8,128)(2,1)S(1)}, u32[]{:S(2)}, u32[]{:S(2)}) collective-permute-start(bf16[32,6144]{1,0:T(8,128)(2,1)S(1)} %slice.261), channel_id=1, source_target_pairs={{0,8},{8,16},{16,24},{24,0},{32,40},{40,48},{48,56},{56,32},{64,72... | collective-permute-start | bytes 1179656 | tf_op jit(solution)/shard_map/ppermute | solution.py:29
  70.2 32.0 %collective-permute-start.13 = (bf16[32,6144]{1,0:T(8,128)(2,1)S(1)}, bf16[32,6144]{1,0:T(8,128)(2,1)S(1)}, u32[]{:S(2)}, u32[]{:S(2)}) collective-permute-start(bf16[32,6144]{1,0:T(8,128)(2,1)S(1)} %slice.262), channel_id=1, source_target_pairs={{0,24},{8,0},{16,8},{24,16},{32,56},{40,32},{48,40},{56,48},{64,88... | collective-permute-start | bytes 1179656 | tf_op jit(solution)/shard_map/ppermute | solution.py:29
  82.3 20.0 %collective-permute-start.14 = (bf16[32,6144]{1,0:T(8,128)(2,1)}, bf16[32,6144]{1,0:T(8,128)(2,1)}, u32[]{:S(2)}, u32[]{:S(2)}) collective-permute-start(bf16[32,6144]{1,0:T(8,128)(2,1)} %slice.263), channel_id=1, source_target_pairs={{0,32},{8,40},{16,48},{24,56},{32,64},{40,72},{48,80},{56,88},{64,... | collective-permute-start | bytes 1179656 | tf_op jit(solution)/shard_map/ppermute | solution.py:22
  83.1 20.2 %collective-permute-start.15 = (bf16[32,6144]{1,0:T(8,128)(2,1)}, bf16[32,6144]{1,0:T(8,128)(2,1)}, u32[]{:S(2)}, u32[]{:S(2)}) collective-permute-start(bf16[32,6144]{1,0:T(8,128)(2,1)} %slice.264), channel_id=1, source_target_pairs={{0,96},{8,104},{16,112},{24,120},{32,0},{40,8},{48,16},{56,24},{64... | collective-permute-start | bytes 1179656 | tf_op jit(solution)/shard_map/ppermute | solution.py:22
  117.5 8.4 %collective-permute-start.16 = (bf16[32,6144]{1,0:T(8,128)(2,1)S(1)}, bf16[32,6144]{1,0:T(8,128)(2,1)S(1)}, u32[]{:S(2)}, u32[]{:S(2)}) collective-permute-start(bf16[32,6144]{1,0:T(8,128)(2,1)S(1)} %get-tuple-element.23), channel_id=1, source_target_pairs={{0,8},{8,16},{16,24},{24,0},{32,40},{40,48},{48,56},{56,32},{64,72... | collective-permute-start | bytes 1179656 | tf_op jit(solution)/shard_map/ppermute | solution.py:29
  117.5 8.3 %collective-permute-start.18 = (bf16[32,6144]{1,0:T(8,128)(2,1)S(1)}, bf16[32,6144]{1,0:T(8,128)(2,1)S(1)}, u32[]{:S(2)}, u32[]{:S(2)}) collective-permute-start(bf16[32,6144]{1,0:T(8,128)(2,1)S(1)} %get-tuple-element.26), channel_id=1, source_target_pairs={{0,24},{8,0},{16,8},{24,16},{32,56},{40,32},{48,40},{56,48},{64,88... | collective-permute-start | bytes 1179656 | tf_op jit(solution)/shard_map/ppermute | solution.py:29
  120.2 8.1 %collective-permute-start.24 = (bf16[32,6144]{1,0:T(8,128)(2,1)S(1)}, bf16[32,6144]{1,0:T(8,128)(2,1)S(1)}, u32[]{:S(2)}, u32[]{:S(2)}) collective-permute-start(bf16[32,6144]{1,0:T(8,128)(2,1)S(1)} %get-tuple-element.25), channel_id=1, source_target_pairs={{0,32},{8,40},{16,48},{24,56},{32,64},{40,72},{48,80},{56,88},{64,... | collective-permute-start | bytes 1179656 | tf_op jit(solution)/shard_map/ppermute | solution.py:22
  120.2 8.1 %collective-permute-start.26 = (bf16[32,6144]{1,0:T(8,128)(2,1)S(1)}, bf16[32,6144]{1,0:T(8,128)(2,1)S(1)}, u32[]{:S(2)}, u32[]{:S(2)}) collective-permute-start(bf16[32,6144]{1,0:T(8,128)(2,1)S(1)} %get-tuple-element.24), channel_id=1, source_target_pairs={{0,96},{8,104},{16,112},{24,120},{32,0},{40,8},{48,16},{56,24},{64... | collective-permute-start | bytes 1179656 | tf_op jit(solution)/shard_map/ppermute | solution.py:22
  130.6 16.6 %collective-permute-start.25 = (bf16[64,6144]{1,0:T(8,128)(2,1)S(1)}, bf16[64,6144]{1,0:T(8,128)(2,1)}, u32[]{:S(2)}, u32[]{:S(2)}) collective-permute-start(bf16[64,6144]{1,0:T(8,128)(2,1)S(1)} %pad_maximum_fusion.2), channel_id=1, source_target_pairs={{0,32},{8,40},{16,48},{24,56},{32,64},{40,72},{48,80},{56,88},{64,... | collective-permute-start | bytes 2359304 | tf_op jit(solution)/shard_map/ppermute | solution.py:22
  131.6 15.6 %collective-permute-start.27 = (bf16[64,6144]{1,0:T(8,128)(2,1)}, bf16[64,6144]{1,0:T(8,128)(2,1)}, u32[]{:S(2)}, u32[]{:S(2)}) collective-permute-start(bf16[64,6144]{1,0:T(8,128)(2,1)} %pad_maximum_fusion.3), channel_id=1, source_target_pairs={{0,96},{8,104},{16,112},{24,120},{32,0},{40,8},{48,16},{56,24},{64... | collective-permute-start | bytes 2359304 | tf_op jit(solution)/shard_map/ppermute | solution.py:22
  135.3 15.1 %collective-permute-start.17 = (bf16[64,6144]{1,0:T(8,128)(2,1)}, bf16[64,6144]{1,0:T(8,128)(2,1)}, u32[]{:S(2)}, u32[]{:S(2)}) collective-permute-start(bf16[64,6144]{1,0:T(8,128)(2,1)} %pad_maximum_fusion), channel_id=1, source_target_pairs={{0,8},{8,16},{16,24},{24,0},{32,40},{40,48},{48,56},{56,32},{64,72... | collective-permute-start | bytes 2359304 | tf_op jit(solution)/shard_map/ppermute | solution.py:29
  136.3 14.0 %collective-permute-start.19 = (bf16[64,6144]{1,0:T(8,128)(2,1)}, bf16[64,6144]{1,0:T(8,128)(2,1)}, u32[]{:S(2)}, u32[]{:S(2)}) collective-permute-start(bf16[64,6144]{1,0:T(8,128)(2,1)} %pad_maximum_fusion.1), channel_id=1, source_target_pairs={{0,24},{8,0},{16,8},{24,16},{32,56},{40,32},{48,40},{56,48},{64,88... | collective-permute-start | bytes 2359304 | tf_op jit(solution)/shard_map/ppermute | solution.py:29
  160.2 6.9 %collective-permute-start.21 = (bf16[16,6144]{1,0:T(8,128)(2,1)S(1)}, bf16[16,6144]{1,0:T(8,128)(2,1)S(1)}, u32[]{:S(2)}, u32[]{:S(2)}) collective-permute-start(bf16[16,6144]{1,0:T(8,128)(2,1)S(1)} %pad_maximum_fusion.5), channel_id=1, source_target_pairs={{0,32},{8,40},{16,48},{24,56},{32,64},{40,72},{48,80},{56,88},{64,... | collective-permute-start | bytes 589832 | tf_op jit(solution)/shard_map/ppermute | solution.py:22
  160.3 6.8 %collective-permute-start.23 = (bf16[16,6144]{1,0:T(8,128)(2,1)S(1)}, bf16[16,6144]{1,0:T(8,128)(2,1)S(1)}, u32[]{:S(2)}, u32[]{:S(2)}) collective-permute-start(bf16[16,6144]{1,0:T(8,128)(2,1)S(1)} %pad_maximum_fusion.6), channel_id=1, source_target_pairs={{0,96},{8,104},{16,112},{24,120},{32,0},{40,8},{48,16},{56,24},{64... | collective-permute-start | bytes 589832 | tf_op jit(solution)/shard_map/ppermute | solution.py:22
  163.1 6.5 %collective-permute-start.29 = (bf16[16,6144]{1,0:T(8,128)(2,1)S(1)}, bf16[16,6144]{1,0:T(8,128)(2,1)S(1)}, u32[]{:S(2)}, u32[]{:S(2)}) collective-permute-start(bf16[16,6144]{1,0:T(8,128)(2,1)S(1)} %pad_maximum_fusion.7), channel_id=1, source_target_pairs={{0,8},{8,16},{16,24},{24,0},{32,40},{40,48},{48,56},{56,32},{64,72... | collective-permute-start | bytes 589832 | tf_op jit(solution)/shard_map/ppermute | solution.py:29
  170.6 20.5 %all-to-all-start = ((bf16[32,1,8,768]{3,0,1,2:T(8,128)(2,1)}), bf16[32,1,8,768]{3,0,1,2:T(8,128)(2,1)S(1)}, u32[]{:S(2)}, u32[]{:S(2)}) async-start(bf16[32,1,8,768]{3,0,1,2:T(8,128)(2,1)} %pad_maximum_fusion.4), calls=%async_computation | async-start | bytes 786432 | tf_op jit(solution)/shard_map/all_to_all | solution.py:203
  (22 other events, 160.7 us)

commit v2 on v1

--- a/solution.py
+++ b/solution.py
@@ -1,8 +1,11 @@
+import functools
 import math
 
 import jax
 import jax.numpy as jnp
 from jax import lax
+from jax.experimental import pallas as pl
+from jax.experimental.pallas import tpu as pltpu
 from jax.sharding import PartitionSpec as P
 
 D = 6144
@@ -15,27 +18,27 @@
 EPSILON = 1e-05
 
 
-def shift_z(value, step):
-    pairs = [
-        (z * SIDE + x, ((z + step) % SIDE) * SIDE + x) for z in range(SIDE) for x in range(SIDE)
-    ]
-    return lax.ppermute(value, "attn", pairs)
-
-
-def shift_x(value, step):
-    pairs = [
-        (z * SIDE + x, z * SIDE + (x + step) % SIDE) for z in range(SIDE) for x in range(SIDE)
-    ]
-    return lax.ppermute(value, "attn", pairs)
-
-
-def spread_near(block, shift):
-    return shift(block, 1), shift(block, -1)
-
-
-def spread_far(behind, ahead, shift):
-    half = behind.shape[0] // 2
-    return jnp.concatenate([shift(behind[:half], 1), shift(ahead[half:], -1)], axis=0)
+def ring_pairs(step, second):
+    pairs = []
+    for z in range(SIDE):
+        for x in range(SIDE):
+            for y in range(SIDE):
+                for core in range(2):
+                    along_z = (core == 0) != second
+                    to_z = (z + step) % SIDE if along_z else z
+                    to_x = x if along_z else (x + step) % SIDE
+                    source = (z * SIDE + x) * E + y * 2 + core
+                    target = (to_z * SIDE + to_x) * E + y * 2 + core
+                    pairs.append((source, target))
+    return pairs
+
+
+def shift_first(value, step):
+    return lax.ppermute(value, ("attn", "expert"), ring_pairs(step, False))
+
+
+def shift_second(value, step):
+    return lax.ppermute(value, ("attn", "expert"), ring_pairs(step, True))
 
 
 def split_three(value):
@@ -46,16 +49,98 @@
     return [high, middle, low]
 
 
-def ring_sum(behind, own, ahead, far, shift):
-    half = far.shape[0] // 2
-    sent = far.astype(jnp.bfloat16)
-    far_up = shift(sent[:half], 1).astype(jnp.float32)
-    far_down = shift(sent[half:], -1).astype(jnp.float32)
-    up = jnp.concatenate([ahead[:half] + far_up, ahead[half:]], axis=0)
-    down = jnp.concatenate([behind[:half], behind[half:] + far_down], axis=0)
-    got_up = shift(up.astype(jnp.bfloat16), 1).astype(jnp.float32)
-    got_down = shift(down.astype(jnp.bfloat16), -1).astype(jnp.float32)
-    return own + got_up + got_down
+def add_rounded(one, other):
+    return (one.astype(jnp.float32) + other.astype(jnp.float32)).astype(jnp.bfloat16)
+
+
+def ring_sum(behind, own, ahead, far_low, far_high, shift):
+    half = far_low.shape[0]
+    got_low = shift(far_low, 1)
+    got_high = shift(far_high, -1)
+    up = jnp.concatenate([add_rounded(ahead[:half], got_low), ahead[half:]], axis=0)
+    down = jnp.concatenate([behind[:half], add_rounded(behind[half:], got_high)], axis=0)
+    from_behind = shift(up, 1)
+    from_ahead = shift(down, -1)
+    return (
+        own.astype(jnp.float32) + from_behind.astype(jnp.float32) + from_ahead.astype(jnp.float32)
+    )
+
+
+K_BLOCK = 1536
+N_BLOCK = 1536
+
+
+def feed_kernel(count, steps_in, *refs):
+    row_refs = refs[:count]
+    gate_ref, up_ref, down_ref, out_ref, rows, gate_sum, up_sum, active = refs[count:]
+    step = pl.program_id(0)
+
+    @pl.when(step == 0)
+    def _():
+        at = 0
+        for ref in row_refs:
+            rows[at : at + ref.shape[0], :] = ref[...]
+            at += ref.shape[0]
+
+    @pl.when(step < steps_in)
+    def _():
+        part = rows[:, pl.ds(pl.multiple_of(step * K_BLOCK, 128), K_BLOCK)]
+        gate_part = jnp.dot(part, gate_ref[0], preferred_element_type=jnp.float32)
+        up_part = jnp.dot(part, up_ref[0], preferred_element_type=jnp.float32)
+
+        @pl.when(step == 0)
+        def _():
+            gate_sum[...] = gate_part
+            up_sum[...] = up_part
+
+        @pl.when(step > 0)
+        def _():
+            gate_sum[...] += gate_part
+            up_sum[...] += up_part
+
+    @pl.when(step == steps_in - 1)
+    def _():
+        active[...] = (jax.nn.silu(gate_sum[...]) * up_sum[...]).astype(jnp.bfloat16)
+
+    @pl.when(step >= steps_in)
+    def _():
+        out_ref[...] = jnp.dot(
+            active[...], down_ref[0], preferred_element_type=jnp.float32
+        ).astype(jnp.bfloat16)
+
+
+def feed(row_arrays, w_gate, w_up, w_down):
+    count = sum(array.shape[0] for array in row_arrays)
+    width, hidden = w_gate.shape[1:]
+    steps_in = width // K_BLOCK
+    steps_out = width // N_BLOCK
+    return pl.pallas_call(
+        functools.partial(feed_kernel, len(row_arrays), steps_in),
+        grid=(steps_in + steps_out,),
+        in_specs=[
+            pl.BlockSpec(array.shape, lambda i: (0, 0), pipeline_mode=pl.Buffered(1))
+            for array in row_arrays
+        ]
+        + [
+            pl.BlockSpec((1, K_BLOCK, hidden), lambda i: (0, jnp.minimum(i, steps_in - 1), 0)),
+            pl.BlockSpec((1, K_BLOCK, hidden), lambda i: (0, jnp.minimum(i, steps_in - 1), 0)),
+            pl.BlockSpec((1, hidden, N_BLOCK), lambda i: (0, 0, jnp.maximum(i - steps_in, 0))),
+        ],
+        out_specs=pl.BlockSpec((count, N_BLOCK), lambda i: (0, jnp.maximum(i - steps_in, 0))),
+        out_shape=jax.ShapeDtypeStruct((count, width), jnp.bfloat16),
+        scratch_shapes=[
+            pltpu.VMEM((count, width), jnp.bfloat16),
+            pltpu.VMEM((count, hidden), jnp.float32),
+            pltpu.VMEM((count, hidden), jnp.float32),
+            pltpu.VMEM((count, hidden), jnp.bfloat16),
+        ],
+        compiler_params=pltpu.CompilerParams(vmem_limit_bytes=30 * 1024 * 1024),
+        cost_estimate=pl.CostEstimate(
+            flops=6 * count * width * hidden,
+            bytes_accessed=6 * width * hidden + 4 * count * width,
+            transcendentals=count * hidden,
+        ),
+    )(*row_arrays, w_gate, w_up, w_down)
 
 
 def on_device(
@@ -158,46 +243,37 @@
     )
     outgoing = (outgoing * own_scale).astype(jnp.bfloat16)
 
-    gate_weight = w_gate[0]
-    up_weight = w_up[0]
-    down_weight = w_down[0]
-
-    def feed(rows):
-        gate_part = jnp.dot(rows, gate_weight, preferred_element_type=jnp.float32)
-        up_part = jnp.dot(rows, up_weight, preferred_element_type=jnp.float32)
-        activation = (jax.nn.silu(gate_part) * up_part).astype(jnp.bfloat16)
-        return jnp.dot(activation, down_weight, preferred_element_type=jnp.float32)
-
-    a_own, b_own = outgoing[:HALF], outgoing[HALF:]
-    a_behind, a_ahead = spread_near(a_own, shift_z)
-    b_behind, b_ahead = spread_near(b_own, shift_x)
-    a_far = spread_far(a_behind, a_ahead, shift_z)
-    b_far = spread_far(b_behind, b_ahead, shift_x)
-    a_line = jnp.concatenate([a_own, a_behind, a_ahead, a_far], axis=0)
-    b_line = jnp.concatenate([b_own, b_behind, b_ahead, b_far], axis=0)
-    line = a_line.shape[0]
-    aa_behind, aa_ahead = spread_near(a_line, shift_x)
-    bb_behind, bb_ahead = spread_near(b_line, shift_z)
-    aa_far = spread_far(aa_behind, aa_ahead, shift_x)
-    bb_far = spread_far(bb_behind, bb_ahead, shift_z)
-
-    part_own = feed(jnp.concatenate([a_line, b_line], axis=0))
-    part_near = feed(jnp.concatenate([aa_behind, bb_behind, aa_ahead, bb_ahead], axis=0))
-    part_far = feed(jnp.concatenate([aa_far, bb_far], axis=0))
-
-    a_sum = ring_sum(
-        part_near[:line], part_own[:line], part_near[2 * line : 3 * line], part_far[:line], shift_x
-    )
-    b_sum = ring_sum(
-        part_near[line : 2 * line], part_own[line:], part_near[3 * line :], part_far[line:], shift_z
-    )
-    a_result = ring_sum(
-        a_sum[HALF : 2 * HALF], a_sum[:HALF], a_sum[2 * HALF : 3 * HALF], a_sum[3 * HALF :], shift_z
-    )
-    b_result = ring_sum(
-        b_sum[HALF : 2 * HALF], b_sum[:HALF], b_sum[2 * HALF : 3 * HALF], b_sum[3 * HALF :], shift_x
-    )
-    expert_result = jnp.concatenate([a_result, b_result], axis=0).astype(jnp.bfloat16)
+    near_up = shift_first(outgoing, 1)
+    near_down = shift_first(outgoing, -1)
+    far_low = shift_first(near_up[:HALF], 1)
+    far_high = shift_first(near_down[HALF:], -1)
+    line = jnp.concatenate([outgoing, near_up, near_down, far_low, far_high], axis=0)
+    middle = line.shape[0] // 2
+    line_up = shift_second(line, 1)
+    line_down = shift_second(line, -1)
+    line_far_low = shift_second(line_up[:middle], 1)
+    line_far_high = shift_second(line_down[middle:], -1)
+
+    part_own = feed([line], w_gate, w_up, w_down)
+    part_near = feed([line_up, line_down], w_gate, w_up, w_down)
+    part_far = feed([line_far_low, line_far_high], w_gate, w_up, w_down)
+
+    line_sum = ring_sum(
+        part_near[: 2 * middle],
+        part_own,
+        part_near[2 * middle :],
+        part_far[:middle],
+        part_far[middle:],
+        shift_second,
+    ).astype(jnp.bfloat16)
+    expert_result = ring_sum(
+        line_sum[CAP : 2 * CAP],
+        line_sum[:CAP],
+        line_sum[2 * CAP : 3 * CAP],
+        line_sum[3 * CAP : 3 * CAP + HALF],
+        line_sum[3 * CAP + HALF :],
+        shift_first,
+    ).astype(jnp.bfloat16)
 
     expert_result = expert_result.reshape(CAP, 1, expert_devices, width_local)
     returned = lax.all_to_all(expert_result, "expert", split_axis=2, concat_axis=1, tiled=True)

time: 193 us -> 159 us (0.82)
  matrix products: 41.9 us -> 3.71 us
  starting transfers between devices: 58.5 us -> 34.2 us
  Pallas kernels: 0 us -> 20.3 us
  waiting for transfers between devices: 52.6 us -> 66.2 us
  other arithmetic: 13.1 us -> 6.33 us
    dot_general x6 -> x0, matrix products: 38.2 us -> none  [the longest x3 28.7 us: feed(): return jnp.dot(activation, down_weight, preferred_element_type=jnp.float32)]
    ppermute x32 -> x16, starting transfers between devices: 46.1 us -> 22.9 us  [the longest x8 11.5 us: shift_second(): return lax.ppermute(value, ('attn', 'expert'), ring_pairs(step, True))]
    pallas_call x0 -> x3, Pallas kernels: none -> 20.3 us  [feed(): pl.pallas_call(functools.partial(feed_kernel, len(row_arrays), steps_in),...]
    ppermute x32 -> x16, waiting for transfers between devices: 44.6 us -> 58.2 us  [the longest x8 41.8 us: shift_second(): return lax.ppermute(value, ('attn', 'expert'), ring_pairs(step, True))]
    another operation x6 -> x0, other arithmetic: 5.85 us -> none
    unnamed x47 -> x31, local copies, waits for them, and re-layouts: 3.48 us -> 8.73 us
    concatenate x9 -> x4, other arithmetic: 3.83 us -> 0.28 us  [the longest x2 0.15 us: ring_sum(): jnp.concatenate([behind[:half], add_rounded(behind[half:], got_high)], ax...]
    slice x12 -> x7, local copies, waits for them, and re-layouts: 3.46 us -> 0.43 us  [the longest x1 0.14 us: on_device(): part_far[:middle]]
  transfers between devices with their start and end apart: 33 -> 17, of which waited for: 11 -> 9; matrix products, arithmetic and copies ran while one was open for 17% -> 0% of each run, Pallas kernels for 0% -> 10%
where the time goes in v2:
time: 159 us; the launch traced here: 158 us
  waiting for transfers between devices  66.2 us (42%)
  starting transfers between devices  34.2 us (22%)
  Pallas kernels  20.3 us (13%)
  blocking collectives  15.4 us (10%)
  local copies, waits for them, and re-layouts  11.9 us (7%)
  other arithmetic  6.33 us (4%)
  matrix products  3.71 us (2%)
    ppermute x8, waiting for transfers between devices, shift_second(): return lax.ppermute(value, ('attn', 'expert'), ring_pairs(step, True))  41.8 us
    pallas_call x3, Pallas kernels, feed(): pl.pallas_call(functools.partial(feed_kernel, len(row_arrays), steps_in),...  20.3 us
    ppermute x8, waiting for transfers between devices, shift_first(): return lax.ppermute(value, ('attn', 'expert'), ring_pairs(step, False))  16.4 us
    all_gather x1, blocking collectives, on_device(): gathered = lax.all_gather(payload, 'expert', axis=0)  15.4 us
    ppermute x8, starting transfers between devices, shift_second(): return lax.ppermute(value, ('attn', 'expert'), ring_pairs(step, True))  11.5 us
    ppermute x8, starting transfers between devices, shift_first(): return lax.ppermute(value, ('attn', 'expert'), ring_pairs(step, False))  11.4 us
    all_to_all x1, starting transfers between devices, on_device(): lax.all_to_all(expert_result, 'expert', split_axis=2, concat_axis=1, tile...  11.3 us
    unnamed x31, local copies, waits for them, and re-layouts  8.73 us
  transfers between devices with their start and end apart: 17, of which 9 were waited for; matrix products, arithmetic and copies ran while one was open for 0% of the time, Pallas kernels for 10%

profile of v2, /device:TPU:1, one launch (start us, length us, event | category | flops | bytes accessed | tf_op | source)
XLA Modules:
  0.0 158.4 jit_solution(4071521210642444133)
XLA Ops:
  6.9 15.4 %all-gather = bf16[512,896]{1,0:T(8,128)(2,1)S(1)} all-gather(bf16[64,896]{1,0:T(8,128)(2,1)S(1)} %concatenate.22), channel_id=2, replica_groups=mesh['attn'=16,'expert'=8] {'expert'}, dimensions={0}, use_global_device_ids=true | all-gather | bytes 1032192 | tf_op jit(solution)/shard_map/all_gather | solution.py:213
  24.8 1.5 collective-permute-start.1
  26.2 5.5 %collective-permute-done = bf16[32,6144]{1,0:T(8,128)(2,1)S(1)} collective-permute-done((bf16[32,6144]{1,0:T(8,128)(2,1)S(1)}, bf16[32,6144]{1,0:T(8,128)(2,1)S(1)}, u32[]{:S(2)}, u32[]{:S(2)}) %collective-permute-start) | collective-permute-done | bytes 393248 | tf_op jit(solution)/shard_map/ppermute | solution.py:37
  31.8 2.7 %collective-permute-start.3 = (bf16[16,6144]{1,0:T(8,128)(2,1)S(1)}, bf16[16,6144]{1,0:T(8,128)(2,1)S(1)}, u32[]{:S(2)}, u32[]{:S(2)}) collective-permute-start(bf16[16,6144]{1,0:T(8,128)(2,1)S(1)} %slice.134), channel_id=1, source_target_pairs={{0,96},{1,25},{2,98},{3,27},{4,100},{5,29},{6,102},{7,31},{8,104},... | collective-permute-start | bytes 589832 | tf_op jit(solution)/shard_map/ppermute | solution.py:37
  34.6 2.9 %collective-permute-done.2 = bf16[16,6144]{1,0:T(8,128)(2,1)S(1)} collective-permute-done((bf16[16,6144]{1,0:T(8,128)(2,1)S(1)}, bf16[16,6144]{1,0:T(8,128)(2,1)S(1)}, u32[]{:S(2)}, u32[]{:S(2)}) %collective-permute-start.2) | collective-permute-done | bytes 196640 | tf_op jit(solution)/shard_map/ppermute | solution.py:37
  39.0 2.8 %collective-permute-start.5 = (bf16[128,6144]{1,0:T(8,128)(2,1)S(1)}, bf16[128,6144]{1,0:T(8,128)(2,1)S(1)}, u32[]{:S(2)}, u32[]{:S(2)}) collective-permute-start(bf16[128,6144]{1,0:T(8,128)(2,1)S(1)} %constant_dynamic-update-slice_fusion.refs_0_), channel_id=1, source_target_pairs={{0,24},{1,97},{2,26},{3,99},{4,28},{5,101},{6,30},{7,103},{8,0},{9... | collective-permute-start | bytes 4718600 | tf_op jit(solution)/shard_map/ppermute | solution.py:41
  41.8 18.0 %collective-permute-done.4.refs_0_ = bf16[128,6144]{1,0:T(8,128)(2,1)S(1)} collective-permute-done((bf16[128,6144]{1,0:T(8,128)(2,1)S(1)}, bf16[128,6144]{1,0:T(8,128)(2,1)S(1)}, u32[]{:S(2)}, u32[]{:S(2)}) %collective-permute-start.4) | collective-permute-done | bytes 1572896 | tf_op jit(solution)/shard_map/ppermute | solution.py:41
  60.0 2.7 %collective-permute-start.7 = (bf16[64,6144]{1,0:T(8,128)(2,1)S(1)}, bf16[64,6144]{1,0:T(8,128)(2,1)S(1)}, u32[]{:S(2)}, u32[]{:S(2)}) collective-permute-start(bf16[64,6144]{1,0:T(8,128)(2,1)S(1)} %slice.137), channel_id=1, source_target_pairs={{0,24},{1,97},{2,26},{3,99},{4,28},{5,101},{6,30},{7,103},{8,0},{9... | collective-permute-start | bytes 2359304 | tf_op jit(solution)/shard_map/ppermute | solution.py:41
  62.7 2.8 %copy-done.1 = bf16[1,6144,512]{2,1,0:T(8,128)(2,1)S(1)} copy-done((bf16[1,6144,512]{2,1,0:T(8,128)(2,1)S(1)}, bf16[1,6144,512]{2,1,0:T(8,128)(2,1)}, u32[]{:S(2)}) %copy-start.1) | copy-done | bytes 6291480
  65.5 2.8 %copy-done.3 = bf16[1,6144,512]{2,1,0:T(8,128)(2,1)S(1)} copy-done((bf16[1,6144,512]{2,1,0:T(8,128)(2,1)S(1)}, bf16[1,6144,512]{2,1,0:T(8,128)(2,1)}, u32[]{:S(2)}) %copy-start.3) | copy-done | bytes 6291480
  68.3 10.4 %shard_map.128 = bf16[256,6144]{1,0:T(8,128)(2,1)S(1)} custom-call(bf16[128,6144]{1,0:T(8,128)(2,1)S(1)} %collective-permute-done.4.refs_0_, bf16[128,6144]{1,0:T(8,128)(2,1)S(1)} %collective-permute-done.5.refs_1_, bf16[1,6144,512]{2,1,0:T(8,128)(2,1)S(1)} %copy-done.1, bf16[1,6144,512]{2,1,0:T(8,128)(2,1)S(1)} %copy-done.3, bf16[1,512,6144]{2,1,0:T(8,128)(2,1)} %refs_4_.3), custom_call_target="tpu_custom_call" | custom-call | flops 4831838208 | bytes 25165824 | tf_op jit(solution)/shard_map/pallas_call | solution.py:117
  78.7 2.8 %copy-done.4 = bf16[1,512,6144]{2,1,0:T(8,128)(2,1)S(1)} copy-done((bf16[1,512,6144]{2,1,0:T(8,128)(2,1)S(1)}, bf16[1,512,6144]{2,1,0:T(8,128)(2,1)}, u32[]{:S(2)}) %copy-start.4) | copy-done | bytes 6291480
  81.5 4.9 %shard_map.129 = bf16[128,6144]{1,0:T(8,128)(2,1)S(1)} custom-call(bf16[64,6144]{1,0:T(8,128)(2,1)S(1)} %collective-permute-done.6.refs_0_, bf16[64,6144]{1,0:T(8,128)(2,1)S(1)} %collective-permute-done.7.refs_1_, bf16[1,6144,512]{2,1,0:T(8,128)(2,1)S(1)} %copy-done.2, bf16[1,6144,512]{2,1,0:T(8,128)(2,1)S(1)} %copy-done.3, bf16[1,512,6144]{2,1,0:T(8,128)(2,1)S(1)} %copy-done.4), custom_call_target="tpu_custom_call" | custom-call | flops 2415919104 | bytes 22020096 | tf_op jit(solution)/shard_map/pallas_call | solution.py:117
  88.3 9.6 %collective-permute-done.10 = bf16[64,6144]{1,0:T(8,128)(2,1)S(1)} collective-permute-done((bf16[64,6144]{1,0:T(8,128)(2,1)S(1)}, bf16[64,6144]{1,0:T(8,128)(2,1)S(1)}, u32[]{:S(2)}, u32[]{:S(2)}) %collective-permute-start.10) | collective-permute-done | bytes 786464 | tf_op jit(solution)/shard_map/ppermute | solution.py:41
  97.8 1.5 collective-permute-done.8
  100.0 2.9 %collective-permute-start.11 = (bf16[128,6144]{1,0:T(8,128)(2,1)S(1)}, bf16[128,6144]{1,0:T(8,128)(2,1)S(1)}, u32[]{:S(2)}, u32[]{:S(2)}) collective-permute-start(bf16[128,6144]{1,0:T(8,128)(2,1)S(1)} %pad_maximum_fusion.1), channel_id=1, source_target_pairs={{0,24},{1,97},{2,26},{3,99},{4,28},{5,101},{6,30},{7,103},{8,0},{9... | collective-permute-start | bytes 4718600 | tf_op jit(solution)/shard_map/ppermute | solution.py:41
  102.9 5.0 %shard_map.127 = bf16[128,6144]{1,0:T(8,128)(2,1)S(1)} custom-call(bf16[128,6144]{1,0:T(8,128)(2,1)S(1)} %copy-done.6, bf16[1,6144,512]{2,1,0:T(8,128)(2,1)S(1)} %copy-done.2, bf16[1,6144,512]{2,1,0:T(8,128)(2,1)S(1)} %copy-done.3, bf16[1,512,6144]{2,1,0:T(8,128)(2,1)S(1)} %copy-done.4), custom_call_target="tpu_custom_call" | custom-call | flops 2415919104 | bytes 22020096 | tf_op jit(solution)/shard_map/pallas_call | solution.py:117
  107.9 12.8 %collective-permute-done.9 = bf16[128,6144]{1,0:T(8,128)(2,1)S(1)} collective-permute-done((bf16[128,6144]{1,0:T(8,128)(2,1)S(1)}, bf16[128,6144]{1,0:T(8,128)(2,1)S(1)}, u32[]{:S(2)}, u32[]{:S(2)}) %collective-permute-start.9) | collective-permute-done | bytes 1572896 | tf_op jit(solution)/shard_map/ppermute | solution.py:41
  121.6 2.8 %collective-permute-start.14 = (bf16[16,6144]{1,0:T(8,128)(2,1)S(1)}, bf16[16,6144]{1,0:T(8,128)(2,1)S(1)}, u32[]{:S(2)}, u32[]{:S(2)}) collective-permute-start(bf16[16,6144]{1,0:T(8,128)(2,1)S(1)} %get-tuple-element.16), channel_id=1, source_target_pairs={{0,96},{1,25},{2,98},{3,27},{4,100},{5,29},{6,102},{7,31},{8,104},... | collective-permute-start | bytes 589832 | tf_op jit(solution)/shard_map/ppermute | solution.py:37
  124.4 3.0 %collective-permute-done.12 = bf16[16,6144]{1,0:T(8,128)(2,1)S(1)} collective-permute-done((bf16[16,6144]{1,0:T(8,128)(2,1)S(1)}, bf16[16,6144]{1,0:T(8,128)(2,1)S(1)}, u32[]{:S(2)}, u32[]{:S(2)}) %collective-permute-start.12) | collective-permute-done | bytes 196640 | tf_op jit(solution)/shard_map/ppermute | solution.py:37
  128.5 2.0 %collective-permute-start.15 = (bf16[32,6144]{1,0:T(8,128)(2,1)S(1)}, bf16[32,6144]{1,0:T(8,128)(2,1)}, u32[]{:S(2)}, u32[]{:S(2)}) collective-permute-start(bf16[32,6144]{1,0:T(8,128)(2,1)S(1)} %pad_maximum_fusion.3), channel_id=1, source_target_pairs={{0,96},{1,25},{2,98},{3,27},{4,100},{5,29},{6,102},{7,31},{8,104},... | collective-permute-start | bytes 1179656 | tf_op jit(solution)/shard_map/ppermute | solution.py:37
  130.6 5.0 %collective-permute-done.13 = bf16[32,6144]{1,0:T(8,128)(2,1)} collective-permute-done((bf16[32,6144]{1,0:T(8,128)(2,1)S(1)}, bf16[32,6144]{1,0:T(8,128)(2,1)}, u32[]{:S(2)}, u32[]{:S(2)}) %collective-permute-start.13) | collective-permute-done | bytes 393248 | tf_op jit(solution)/shard_map/ppermute | solution.py:37
  137.9 11.3 %all-to-all-start = ((bf16[32,1,8,768]{3,0,1,2:T(8,128)(2,1)}), bf16[32,1,8,768]{3,0,1,2:T(8,128)(2,1)S(1)}, u32[]{:S(2)}, u32[]{:S(2)}) async-start(bf16[32,1,8,768]{3,0,1,2:T(8,128)(2,1)} %copy.58), calls=%async_computation | async-start | bytes 786432 | tf_op jit(solution)/shard_map/all_to_all | solution.py:279
  149.3 8.0 %all-to-all-done = bf16[32,1,8,768]{3,0,1,2:T(8,128)(2,1)S(1)} async-done(((bf16[32,1,8,768]{3,0,1,2:T(8,128)(2,1)}), bf16[32,1,8,768]{3,0,1,2:T(8,128)(2,1)S(1)}, u32[]{:S(2)}, u32[]{:S(2)}) %all-to-all-start) | async-done | bytes 393248 | tf_op jit(solution)/shard_map/all_to_all | solution.py:279
  (100 shorter events, 19.0 us)
Async XLA Ops:
  0.0 3.7 %copy-start = (bf16[64,1,128,128]{3,2,1,0:T(8,128)(2,1)S(1)}, bf16[64,1,128,128]{3,2,1,0:T(8,128)(2,1)}, u32[]{:S(2)}) copy-start(bf16[64,1,128,128]{3,2,1,0:T(8,128)(2,1)} %param.15) | copy-start | bytes 6291460
  1.2 3.9 %copy-start.8 = (bf16[64,1,128,128]{3,2,1,0:T(8,128)(2,1)S(1)}, bf16[64,1,128,128]{3,2,1,0:T(8,128)(2,1)}, u32[]{:S(2)}) copy-start(bf16[64,1,128,128]{3,2,1,0:T(8,128)(2,1)} %param.16) | copy-start | bytes 6291460
  6.1 16.5 %copy-start.12 = (s32[64,2]{0,1:T(2,128)S(1)}, s32[64,2]{0,1:T(2,128)}, u32[]{:S(2)}) copy-start(s32[64,2]{0,1:T(2,128)} %param.22) | copy-start | bytes 1540
  23.5 8.2 %collective-permute-start = (bf16[32,6144]{1,0:T(8,128)(2,1)S(1)}, bf16[32,6144]{1,0:T(8,128)(2,1)S(1)}, u32[]{:S(2)}, u32[]{:S(2)}) collective-permute-start(bf16[32,6144]{1,0:T(8,128)(2,1)S(1)} %get-tuple-element.6), channel_id=1, source_target_pairs={{0,32},{1,9},{2,34},{3,11},{4,36},{5,13},{6,38},{7,15},{8,40},{9,1... | collective-permute-start | bytes 1179656 | tf_op jit(solution)/shard_map/ppermute | solution.py:37
  24.8 7.0 %collective-permute-start.1 = (bf16[32,6144]{1,0:T(8,128)(2,1)S(1)}, bf16[32,6144]{1,0:T(8,128)(2,1)S(1)}, u32[]{:S(2)}, u32[]{:S(2)}) collective-permute-start(bf16[32,6144]{1,0:T(8,128)(2,1)S(1)} %get-tuple-element.6), channel_id=1, source_target_pairs={{0,96},{1,25},{2,98},{3,27},{4,100},{5,29},{6,102},{7,31},{8,104},... | collective-permute-start | bytes 1179656 | tf_op jit(solution)/shard_map/ppermute | solution.py:37
  31.7 5.8 %collective-permute-start.2 = (bf16[16,6144]{1,0:T(8,128)(2,1)S(1)}, bf16[16,6144]{1,0:T(8,128)(2,1)S(1)}, u32[]{:S(2)}, u32[]{:S(2)}) collective-permute-start(bf16[16,6144]{1,0:T(8,128)(2,1)S(1)} %slice.133), channel_id=1, source_target_pairs={{0,32},{1,9},{2,34},{3,11},{4,36},{5,13},{6,38},{7,15},{8,40},{9,1... | collective-permute-start | bytes 589832 | tf_op jit(solution)/shard_map/ppermute | solution.py:37
  31.8 5.7 %collective-permute-start.3 = (bf16[16,6144]{1,0:T(8,128)(2,1)S(1)}, bf16[16,6144]{1,0:T(8,128)(2,1)S(1)}, u32[]{:S(2)}, u32[]{:S(2)}) collective-permute-start(bf16[16,6144]{1,0:T(8,128)(2,1)S(1)} %slice.134), channel_id=1, source_target_pairs={{0,96},{1,25},{2,98},{3,27},{4,100},{5,29},{6,102},{7,31},{8,104},... | collective-permute-start | bytes 589832 | tf_op jit(solution)/shard_map/ppermute | solution.py:37
  37.6 22.4 %copy-start.5 = (bf16[128,6144]{1,0:T(8,128)(2,1)}, bf16[128,6144]{1,0:T(8,128)(2,1)S(1)}, u32[]{:S(2)}) copy-start(bf16[128,6144]{1,0:T(8,128)(2,1)S(1)} %constant_dynamic-update-slice_fusion.refs_0_) | copy-start | bytes 4718596
  37.6 22.2 %collective-permute-start.4 = (bf16[128,6144]{1,0:T(8,128)(2,1)S(1)}, bf16[128,6144]{1,0:T(8,128)(2,1)S(1)}, u32[]{:S(2)}, u32[]{:S(2)}) collective-permute-start(bf16[128,6144]{1,0:T(8,128)(2,1)S(1)} %constant_dynamic-update-slice_fusion.refs_0_), channel_id=1, source_target_pairs={{0,8},{1,33},{2,10},{3,35},{4,12},{5,37},{6,14},{7,39},{8,16},{9,4... | collective-permute-start | bytes 4718600 | tf_op jit(solution)/shard_map/ppermute | solution.py:41
  39.0 21.0 %collective-permute-start.5 = (bf16[128,6144]{1,0:T(8,128)(2,1)S(1)}, bf16[128,6144]{1,0:T(8,128)(2,1)S(1)}, u32[]{:S(2)}, u32[]{:S(2)}) collective-permute-start(bf16[128,6144]{1,0:T(8,128)(2,1)S(1)} %constant_dynamic-update-slice_fusion.refs_0_), channel_id=1, source_target_pairs={{0,24},{1,97},{2,26},{3,99},{4,28},{5,101},{6,30},{7,103},{8,0},{9... | collective-permute-start | bytes 4718600 | tf_op jit(solution)/shard_map/ppermute | solution.py:41
  59.9 18.8 %collective-permute-start.6 = (bf16[64,6144]{1,0:T(8,128)(2,1)S(1)}, bf16[64,6144]{1,0:T(8,128)(2,1)S(1)}, u32[]{:S(2)}, u32[]{:S(2)}) collective-permute-start(bf16[64,6144]{1,0:T(8,128)(2,1)S(1)} %slice.136), channel_id=1, source_target_pairs={{0,8},{1,33},{2,10},{3,35},{4,12},{5,37},{6,14},{7,39},{8,16},{9,4... | collective-permute-start | bytes 2359304 | tf_op jit(solution)/shard_map/ppermute | solution.py:41
  60.0 18.7 %collective-permute-start.7 = (bf16[64,6144]{1,0:T(8,128)(2,1)S(1)}, bf16[64,6144]{1,0:T(8,128)(2,1)S(1)}, u32[]{:S(2)}, u32[]{:S(2)}) collective-permute-start(bf16[64,6144]{1,0:T(8,128)(2,1)S(1)} %slice.137), channel_id=1, source_target_pairs={{0,24},{1,97},{2,26},{3,99},{4,28},{5,101},{6,30},{7,103},{8,0},{9... | collective-permute-start | bytes 2359304 | tf_op jit(solution)/shard_map/ppermute | solution.py:41
  68.3 10.4 %copy-start.2 = (bf16[1,6144,512]{2,1,0:T(8,128)(2,1)S(1)}, bf16[1,6144,512]{2,1,0:T(8,128)(2,1)}, u32[]{:S(2)}) copy-start(bf16[1,6144,512]{2,1,0:T(8,128)(2,1)} %refs_2_.5) | copy-start | bytes 18874372
  86.6 11.2 %collective-permute-start.10 = (bf16[64,6144]{1,0:T(8,128)(2,1)S(1)}, bf16[64,6144]{1,0:T(8,128)(2,1)S(1)}, u32[]{:S(2)}, u32[]{:S(2)}) collective-permute-start(bf16[64,6144]{1,0:T(8,128)(2,1)S(1)} %get-tuple-element.20), channel_id=1, source_target_pairs={{0,24},{1,97},{2,26},{3,99},{4,28},{5,101},{6,30},{7,103},{8,0},{9... | collective-permute-start | bytes 2359304 | tf_op jit(solution)/shard_map/ppermute | solution.py:41
  86.9 12.3 %collective-permute-start.8 = (bf16[64,6144]{1,0:T(8,128)(2,1)S(1)}, bf16[64,6144]{1,0:T(8,128)(2,1)S(1)}, u32[]{:S(2)}, u32[]{:S(2)}) collective-permute-start(bf16[64,6144]{1,0:T(8,128)(2,1)S(1)} %get-tuple-element.19), channel_id=1, source_target_pairs={{0,8},{1,33},{2,10},{3,35},{4,12},{5,37},{6,14},{7,39},{8,16},{9,4... | collective-permute-start | bytes 2359304 | tf_op jit(solution)/shard_map/ppermute | solution.py:41
  99.8 20.8 %collective-permute-start.9 = (bf16[128,6144]{1,0:T(8,128)(2,1)S(1)}, bf16[128,6144]{1,0:T(8,128)(2,1)S(1)}, u32[]{:S(2)}, u32[]{:S(2)}) collective-permute-start(bf16[128,6144]{1,0:T(8,128)(2,1)S(1)} %pad_maximum_fusion), channel_id=1, source_target_pairs={{0,8},{1,33},{2,10},{3,35},{4,12},{5,37},{6,14},{7,39},{8,16},{9,4... | collective-permute-start | bytes 4718600 | tf_op jit(solution)/shard_map/ppermute | solution.py:41
  99.9 3.0 %copy-start.6 = (bf16[128,6144]{1,0:T(8,128)(2,1)S(1)}, bf16[128,6144]{1,0:T(8,128)(2,1)}, u32[]{:S(2)}) copy-start(bf16[128,6144]{1,0:T(8,128)(2,1)} %copy-done.5) | copy-start | bytes 4718596
  100.0 20.6 %collective-permute-start.11 = (bf16[128,6144]{1,0:T(8,128)(2,1)S(1)}, bf16[128,6144]{1,0:T(8,128)(2,1)S(1)}, u32[]{:S(2)}, u32[]{:S(2)}) collective-permute-start(bf16[128,6144]{1,0:T(8,128)(2,1)S(1)} %pad_maximum_fusion.1), channel_id=1, source_target_pairs={{0,24},{1,97},{2,26},{3,99},{4,28},{5,101},{6,30},{7,103},{8,0},{9... | collective-permute-start | bytes 4718600 | tf_op jit(solution)/shard_map/ppermute | solution.py:41
  121.5 6.1 %copy-start.7 = (bf16[128,6144]{1,0:T(8,128)(2,1)}, bf16[128,6144]{1,0:T(8,128)(2,1)S(1)}, u32[]{:S(2)}) copy-start(bf16[128,6144]{1,0:T(8,128)(2,1)S(1)} %add_convert_fusion) | copy-start | bytes 4718596
  121.5 5.9 %collective-permute-start.12 = (bf16[16,6144]{1,0:T(8,128)(2,1)S(1)}, bf16[16,6144]{1,0:T(8,128)(2,1)S(1)}, u32[]{:S(2)}, u32[]{:S(2)}) collective-permute-start(bf16[16,6144]{1,0:T(8,128)(2,1)S(1)} %get-tuple-element.15), channel_id=1, source_target_pairs={{0,32},{1,9},{2,34},{3,11},{4,36},{5,13},{6,38},{7,15},{8,40},{9,1... | collective-permute-start | bytes 589832 | tf_op jit(solution)/shard_map/ppermute | solution.py:37
  121.6 5.8 %collective-permute-start.14 = (bf16[16,6144]{1,0:T(8,128)(2,1)S(1)}, bf16[16,6144]{1,0:T(8,128)(2,1)S(1)}, u32[]{:S(2)}, u32[]{:S(2)}) collective-permute-start(bf16[16,6144]{1,0:T(8,128)(2,1)S(1)} %get-tuple-element.16), channel_id=1, source_target_pairs={{0,96},{1,25},{2,98},{3,27},{4,100},{5,29},{6,102},{7,31},{8,104},... | collective-permute-start | bytes 589832 | tf_op jit(solution)/shard_map/ppermute | solution.py:37
  127.5 8.1 %collective-permute-start.13 = (bf16[32,6144]{1,0:T(8,128)(2,1)S(1)}, bf16[32,6144]{1,0:T(8,128)(2,1)}, u32[]{:S(2)}, u32[]{:S(2)}) collective-permute-start(bf16[32,6144]{1,0:T(8,128)(2,1)S(1)} %pad_maximum_fusion.2), channel_id=1, source_target_pairs={{0,32},{1,9},{2,34},{3,11},{4,36},{5,13},{6,38},{7,15},{8,40},{9,1... | collective-permute-start | bytes 1179656 | tf_op jit(solution)/shard_map/ppermute | solution.py:37
  128.5 7.2 %collective-permute-start.15 = (bf16[32,6144]{1,0:T(8,128)(2,1)S(1)}, bf16[32,6144]{1,0:T(8,128)(2,1)}, u32[]{:S(2)}, u32[]{:S(2)}) collective-permute-start(bf16[32,6144]{1,0:T(8,128)(2,1)S(1)} %pad_maximum_fusion.3), channel_id=1, source_target_pairs={{0,96},{1,25},{2,98},{3,27},{4,100},{5,29},{6,102},{7,31},{8,104},... | collective-permute-start | bytes 1179656 | tf_op jit(solution)/shard_map/ppermute | solution.py:37
  137.9 19.4 %all-to-all-start = ((bf16[32,1,8,768]{3,0,1,2:T(8,128)(2,1)}), bf16[32,1,8,768]{3,0,1,2:T(8,128)(2,1)S(1)}, u32[]{:S(2)}, u32[]{:S(2)}) async-start(bf16[32,1,8,768]{3,0,1,2:T(8,128)(2,1)} %copy.58), calls=%async_computation | async-start | bytes 786432 | tf_op jit(solution)/shard_map/all_to_all | solution.py:279
  (6 other events, 11.3 us)

commit v3 on v2

--- a/solution.py
+++ b/solution.py
@@ -12,7 +12,8 @@
 E = 8
 CAP = 32
 SIDE = 4
-HALF = CAP // 2
+CHAINS = 2
+CHAIN_ROWS = CAP // CHAINS
 
 
 EPSILON = 1e-05
@@ -66,81 +67,84 @@
     )
 
 
-K_BLOCK = 1536
-N_BLOCK = 1536
-
-
-def feed_kernel(count, steps_in, *refs):
+CHUNKS = 4
+
+
+def feed_kernel(count, *refs):
     row_refs = refs[:count]
-    gate_ref, up_ref, down_ref, out_ref, rows, gate_sum, up_sum, active = refs[count:]
-    step = pl.program_id(0)
-
-    @pl.when(step == 0)
-    def _():
-        at = 0
-        for ref in row_refs:
-            rows[at : at + ref.shape[0], :] = ref[...]
-            at += ref.shape[0]
-
-    @pl.when(step < steps_in)
-    def _():
-        part = rows[:, pl.ds(pl.multiple_of(step * K_BLOCK, 128), K_BLOCK)]
-        gate_part = jnp.dot(part, gate_ref[0], preferred_element_type=jnp.float32)
-        up_part = jnp.dot(part, up_ref[0], preferred_element_type=jnp.float32)
-
-        @pl.when(step == 0)
-        def _():
-            gate_sum[...] = gate_part
-            up_sum[...] = up_part
-
-        @pl.when(step > 0)
-        def _():
-            gate_sum[...] += gate_part
-            up_sum[...] += up_part
-
-    @pl.when(step == steps_in - 1)
-    def _():
-        active[...] = (jax.nn.silu(gate_sum[...]) * up_sum[...]).astype(jnp.bfloat16)
-
-    @pl.when(step >= steps_in)
-    def _():
-        out_ref[...] = jnp.dot(
-            active[...], down_ref[0], preferred_element_type=jnp.float32
+    gate_hbm, up_hbm, down_hbm, out_ref, rows, gate, up, down, ready = refs[count:]
+    width, hidden = gate.shape
+    depth = width // CHUNKS
+    copies = []
+    for k in range(CHUNKS):
+        part = pl.ds(k * depth, depth)
+        copies.append(
+            pltpu.make_async_copy(gate_hbm.at[0, part, :], gate.at[part, :], ready.at[0, k])
+        )
+        copies.append(pltpu.make_async_copy(up_hbm.at[0, part, :], up.at[part, :], ready.at[1, k]))
+    for k in range(CHUNKS):
+        part = pl.ds(k * depth, depth)
+        copies.append(
+            pltpu.make_async_copy(down_hbm.at[0, :, part], down.at[:, part], ready.at[2, k])
+        )
+    for copy in copies:
+        copy.start()
+    at = 0
+    for ref in row_refs:
+        rows[at : at + ref.shape[0], :] = ref[...]
+        at += ref.shape[0]
+    gate_sum = jnp.zeros((rows.shape[0], hidden), jnp.float32)
+    up_sum = jnp.zeros((rows.shape[0], hidden), jnp.float32)
+    for k in range(CHUNKS):
+        part = rows[:, k * depth : (k + 1) * depth]
+        copies[2 * k].wait()
+        gate_sum += jnp.dot(
+            part, gate[k * depth : (k + 1) * depth, :], preferred_element_type=jnp.float32
+        )
+        copies[2 * k + 1].wait()
+        up_sum += jnp.dot(
+            part, up[k * depth : (k + 1) * depth, :], preferred_element_type=jnp.float32
+        )
+    active = (jax.nn.silu(gate_sum) * up_sum).astype(jnp.bfloat16)
+    for k in range(CHUNKS):
+        copies[2 * CHUNKS + k].wait()
+        out_ref[:, k * depth : (k + 1) * depth] = jnp.dot(
+            active, down[:, k * depth : (k + 1) * depth], preferred_element_type=jnp.float32
         ).astype(jnp.bfloat16)
 
 
 def feed(row_arrays, w_gate, w_up, w_down):
     count = sum(array.shape[0] for array in row_arrays)
     width, hidden = w_gate.shape[1:]
-    steps_in = width // K_BLOCK
-    steps_out = width // N_BLOCK
     return pl.pallas_call(
-        functools.partial(feed_kernel, len(row_arrays), steps_in),
-        grid=(steps_in + steps_out,),
-        in_specs=[
-            pl.BlockSpec(array.shape, lambda i: (0, 0), pipeline_mode=pl.Buffered(1))
-            for array in row_arrays
-        ]
-        + [
-            pl.BlockSpec((1, K_BLOCK, hidden), lambda i: (0, jnp.minimum(i, steps_in - 1), 0)),
-            pl.BlockSpec((1, K_BLOCK, hidden), lambda i: (0, jnp.minimum(i, steps_in - 1), 0)),
-            pl.BlockSpec((1, hidden, N_BLOCK), lambda i: (0, 0, jnp.maximum(i - steps_in, 0))),
-        ],
-        out_specs=pl.BlockSpec((count, N_BLOCK), lambda i: (0, jnp.maximum(i - steps_in, 0))),
+        functools.partial(feed_kernel, len(row_arrays)),
+        in_specs=[pl.BlockSpec(memory_space=pltpu.VMEM)] * len(row_arrays)
+        + [pl.BlockSpec(memory_space=pltpu.HBM)] * 3,
+        out_specs=pl.BlockSpec(memory_space=pltpu.VMEM),
         out_shape=jax.ShapeDtypeStruct((count, width), jnp.bfloat16),
         scratch_shapes=[
             pltpu.VMEM((count, width), jnp.bfloat16),
-            pltpu.VMEM((count, hidden), jnp.float32),
-            pltpu.VMEM((count, hidden), jnp.float32),
-            pltpu.VMEM((count, hidden), jnp.bfloat16),
+            pltpu.VMEM((width, hidden), jnp.bfloat16),
+            pltpu.VMEM((width, hidden), jnp.bfloat16),
+            pltpu.VMEM((hidden, width), jnp.bfloat16),
+            pltpu.SemaphoreType.DMA((3, CHUNKS)),
         ],
-        compiler_params=pltpu.CompilerParams(vmem_limit_bytes=30 * 1024 * 1024),
+        compiler_params=pltpu.CompilerParams(vmem_limit_bytes=46 * 1024 * 1024),
         cost_estimate=pl.CostEstimate(
             flops=6 * count * width * hidden,
             bytes_accessed=6 * width * hidden + 4 * count * width,
             transcendentals=count * hidden,
         ),
     )(*row_arrays, w_gate, w_up, w_down)
+
+
+def gather_ring(block, shift):
+    half = block.shape[0] // 2
+    near_up = shift(block, 1)
+    near_down = shift(block, -1)
+    far_low = shift(near_up[:half], 1)
+    far_high = shift(near_down[half:], -1)
+    return block, near_up, near_down, far_low, far_high
 
 
 def on_device(
@@ -243,37 +247,38 @@
     )
     outgoing = (outgoing * own_scale).astype(jnp.bfloat16)
 
-    near_up = shift_first(outgoing, 1)
-    near_down = shift_first(outgoing, -1)
-    far_low = shift_first(near_up[:HALF], 1)
-    far_high = shift_first(near_down[HALF:], -1)
-    line = jnp.concatenate([outgoing, near_up, near_down, far_low, far_high], axis=0)
-    middle = line.shape[0] // 2
-    line_up = shift_second(line, 1)
-    line_down = shift_second(line, -1)
-    line_far_low = shift_second(line_up[:middle], 1)
-    line_far_high = shift_second(line_down[middle:], -1)
-
-    part_own = feed([line], w_gate, w_up, w_down)
-    part_near = feed([line_up, line_down], w_gate, w_up, w_down)
-    part_far = feed([line_far_low, line_far_high], w_gate, w_up, w_down)
-
-    line_sum = ring_sum(
-        part_near[: 2 * middle],
-        part_own,
-        part_near[2 * middle :],
-        part_far[:middle],
-        part_far[middle:],
-        shift_second,
-    ).astype(jnp.bfloat16)
-    expert_result = ring_sum(
-        line_sum[CAP : 2 * CAP],
-        line_sum[:CAP],
-        line_sum[2 * CAP : 3 * CAP],
-        line_sum[3 * CAP : 3 * CAP + HALF],
-        line_sum[3 * CAP + HALF :],
-        shift_first,
-    ).astype(jnp.bfloat16)
+    weights = (w_gate, w_up, w_down)
+    lines = []
+    for chain in range(CHAINS):
+        slab = outgoing[chain * CHAIN_ROWS : (chain + 1) * CHAIN_ROWS]
+        line = jnp.concatenate(gather_ring(slab, shift_first), axis=0)
+        lines.append(gather_ring(line, shift_second))
+    part_own = feed([line[0] for line in lines], *weights)
+    part_near = [feed([line[1], line[2]], *weights) for line in lines]
+    part_far = feed([piece for line in lines for piece in line[3:]], *weights)
+    results = []
+    for chain in range(CHAINS):
+        count = SIDE * CHAIN_ROWS
+        line_sum = ring_sum(
+            part_near[chain][:count],
+            part_own[chain * count : (chain + 1) * count],
+            part_near[chain][count:],
+            part_far[chain * count : chain * count + count // 2],
+            part_far[chain * count + count // 2 : (chain + 1) * count],
+            shift_second,
+        ).astype(jnp.bfloat16)
+        row = CHAIN_ROWS
+        results.append(
+            ring_sum(
+                line_sum[row : 2 * row],
+                line_sum[:row],
+                line_sum[2 * row : 3 * row],
+                line_sum[3 * row : 3 * row + row // 2],
+                line_sum[3 * row + row // 2 :],
+                shift_first,
+            ).astype(jnp.bfloat16)
+        )
+    expert_result = jnp.concatenate(results, axis=0)
 
     expert_result = expert_result.reshape(CAP, 1, expert_devices, width_local)
     returned = lax.all_to_all(expert_result, "expert", split_axis=2, concat_axis=1, tiled=True)

time: 159 us -> 152 us (0.956)
  waiting for transfers between devices: 66.2 us -> 31.3 us
  starting transfers between devices: 34.2 us -> 57.4 us
  Pallas kernels: 20.3 us -> 27.7 us
  local copies, waits for them, and re-layouts: 11.9 us -> 4.73 us
  other arithmetic: 6.33 us -> 10.4 us
    ppermute x8 -> x16, waiting for transfers between devices: 41.8 us -> 19.6 us  [shift_second(): return lax.ppermute(value, ('attn', 'expert'), ring_pairs(step, True))]
    ppermute x8 -> x16, waiting for transfers between devices: 16.4 us -> 3.59 us  [shift_first(): return lax.ppermute(value, ('attn', 'expert'), ring_pairs(step, False))]
    ppermute x8 -> x16, starting transfers between devices: 11.5 us -> 23.4 us  [shift_second(): return lax.ppermute(value, ('attn', 'expert'), ring_pairs(step, True))]
    ppermute x8 -> x16, starting transfers between devices: 11.4 us -> 22.1 us  [shift_first(): return lax.ppermute(value, ('attn', 'expert'), ring_pairs(step, False))]
    pallas_call x3 -> x4, Pallas kernels: 20.3 us -> 27.7 us  [feed(): pl.pallas_call(functools.partial(feed_kernel, len(row_arrays)), in_specs=...]
    unnamed x31 -> x24, local copies, waits for them, and re-layouts: 8.73 us -> 1.51 us
    concatenate x2 -> x4, other arithmetic: 0.15 us -> 1.94 us  [ring_sum(): jnp.concatenate([behind[:half], add_rounded(behind[half:], got_high)], ax...]
    concatenate x2 -> x4, other arithmetic: 0.14 us -> 1.92 us  [ring_sum(): jnp.concatenate([add_rounded(ahead[:half], got_low), ahead[half:]], axis=0)]
  transfers between devices with their start and end apart: 17 -> 33, of which waited for: 9 -> 9; matrix products, arithmetic and copies ran while one was open for 0% -> 3% of each run, Pallas kernels for 10% -> 14%
where the time goes in v3:
time: 152 us; the launch traced here: 151 us
  starting transfers between devices  57.4 us (38%)
  waiting for transfers between devices  31.3 us (21%)
  Pallas kernels  27.7 us (18%)
  blocking collectives  15.4 us (10%)
  other arithmetic  10.4 us (7%)
  local copies, waits for them, and re-layouts  4.73 us (3%)
  matrix products  3.72 us (2%)
    pallas_call x4, Pallas kernels, feed(): pl.pallas_call(functools.partial(feed_kernel, len(row_arrays)), in_specs=...  27.7 us
    ppermute x16, starting transfers between devices, shift_second(): return lax.ppermute(value, ('attn', 'expert'), ring_pairs(step, True))  23.4 us
    ppermute x16, starting transfers between devices, shift_first(): return lax.ppermute(value, ('attn', 'expert'), ring_pairs(step, False))  22.1 us
    ppermute x16, waiting for transfers between devices, shift_second(): return lax.ppermute(value, ('attn', 'expert'), ring_pairs(step, True))  19.6 us
    all_gather x1, blocking collectives, on_device(): gathered = lax.all_gather(payload, 'expert', axis=0)  15.4 us
    all_to_all x1, starting transfers between devices, on_device(): lax.all_to_all(expert_result, 'expert', split_axis=2, concat_axis=1, tile...  11.9 us
    all_to_all x1, waiting for transfers between devices, on_device(): lax.all_to_all(expert_result, 'expert', split_axis=2, concat_axis=1, tile...  8.04 us
    ppermute x16, waiting for transfers between devices, shift_first(): return lax.ppermute(value, ('attn', 'expert'), ring_pairs(step, False))  3.59 us
  transfers between devices with their start and end apart: 33, of which 9 were waited for; matrix products, arithmetic and copies ran while one was open for 3% of the time, Pallas kernels for 14%

profile of v3, /device:TPU:1, one launch (start us, length us, event | category | flops | bytes accessed | tf_op | source)
XLA Modules:
  0.0 151.2 jit_solution(15766936598245970708)
XLA Ops:
  6.9 15.4 %all-gather = bf16[512,896]{1,0:T(8,128)(2,1)S(1)} all-gather(bf16[64,896]{1,0:T(8,128)(2,1)S(1)} %concatenate.40), channel_id=2, replica_groups=mesh['attn'=16,'expert'=8] {'expert'}, dimensions={0}, use_global_device_ids=true | all-gather | bytes 1032192 | tf_op jit(solution)/shard_map/all_gather | solution.py:217
  26.3 2.7 %collective-permute-start.1 = (bf16[16,6144]{1,0:T(8,128)(2,1)S(1)}, bf16[16,6144]{1,0:T(8,128)(2,1)S(1)}, u32[]{:S(2)}, u32[]{:S(2)}) collective-permute-start(bf16[16,6144]{1,0:T(8,128)(2,1)S(1)} %get-tuple-element.36), channel_id=1, source_target_pairs={{0,96},{1,25},{2,98},{3,27},{4,100},{5,29},{6,102},{7,31},{8,104},... | collective-permute-start | bytes 589832 | tf_op jit(solution)/shard_map/ppermute | solution.py:38
  29.8 2.7 %collective-permute-start.7 = (bf16[8,6144]{1,0:T(8,128)(2,1)S(1)}, bf16[8,6144]{1,0:T(8,128)(2,1)S(1)}, u32[]{:S(2)}, u32[]{:S(2)}) collective-permute-start(bf16[8,6144]{1,0:T(8,128)(2,1)S(1)} %slice.234), channel_id=1, source_target_pairs={{0,96},{1,25},{2,98},{3,27},{4,100},{5,29},{6,102},{7,31},{8,104},... | collective-permute-start | bytes 294920 | tf_op jit(solution)/shard_map/ppermute | solution.py:38
  32.6 2.7 %collective-permute-start.3 = (bf16[8,6144]{1,0:T(8,128)(2,1)S(1)}, bf16[8,6144]{1,0:T(8,128)(2,1)S(1)}, u32[]{:S(2)}, u32[]{:S(2)}) collective-permute-start(bf16[8,6144]{1,0:T(8,128)(2,1)S(1)} %slice.231), channel_id=1, source_target_pairs={{0,96},{1,25},{2,98},{3,27},{4,100},{5,29},{6,102},{7,31},{8,104},... | collective-permute-start | bytes 294920 | tf_op jit(solution)/shard_map/ppermute | solution.py:38
  39.5 2.7 %collective-permute-start.9 = (bf16[64,6144]{1,0:T(8,128)(2,1)S(1)}, bf16[64,6144]{1,0:T(8,128)(2,1)S(1)}, u32[]{:S(2)}, u32[]{:S(2)}) collective-permute-start(bf16[64,6144]{1,0:T(8,128)(2,1)S(1)} %constant_dynamic-update-slice_fusion.refs_0_), channel_id=1, source_target_pairs={{0,24},{1,97},{2,26},{3,99},{4,28},{5,101},{6,30},{7,103},{8,0},{9... | collective-permute-start | bytes 2359304 | tf_op jit(solution)/shard_map/ppermute | solution.py:42
  42.2 6.8 %collective-permute-done.12.refs_0_ = bf16[64,6144]{1,0:T(8,128)(2,1)S(1)} collective-permute-done((bf16[64,6144]{1,0:T(8,128)(2,1)S(1)}, bf16[64,6144]{1,0:T(8,128)(2,1)S(1)}, u32[]{:S(2)}, u32[]{:S(2)}) %collective-permute-start.12) | collective-permute-done | bytes 786464 | tf_op jit(solution)/shard_map/ppermute | solution.py:42
  49.1 2.8 %collective-permute-start.15 = (bf16[32,6144]{1,0:T(8,128)(2,1)S(1)}, bf16[32,6144]{1,0:T(8,128)(2,1)S(1)}, u32[]{:S(2)}, u32[]{:S(2)}) collective-permute-start(bf16[32,6144]{1,0:T(8,128)(2,1)S(1)} %slice.240), channel_id=1, source_target_pairs={{0,24},{1,97},{2,26},{3,99},{4,28},{5,101},{6,30},{7,103},{8,0},{9... | collective-permute-start | bytes 1179656 | tf_op jit(solution)/shard_map/ppermute | solution.py:42
  51.9 5.5 %collective-permute-done.8.refs_0_ = bf16[64,6144]{1,0:T(8,128)(2,1)S(1)} collective-permute-done((bf16[64,6144]{1,0:T(8,128)(2,1)S(1)}, bf16[64,6144]{1,0:T(8,128)(2,1)S(1)}, u32[]{:S(2)}, u32[]{:S(2)}) %collective-permute-start.8) | collective-permute-done | bytes 786464 | tf_op jit(solution)/shard_map/ppermute | solution.py:42
  57.6 3.0 %collective-permute-start.11 = (bf16[32,6144]{1,0:T(8,128)(2,1)S(1)}, bf16[32,6144]{1,0:T(8,128)(2,1)S(1)}, u32[]{:S(2)}, u32[]{:S(2)}) collective-permute-start(bf16[32,6144]{1,0:T(8,128)(2,1)S(1)} %slice.238), channel_id=1, source_target_pairs={{0,24},{1,97},{2,26},{3,99},{4,28},{5,101},{6,30},{7,103},{8,0},{9... | collective-permute-start | bytes 1179656 | tf_op jit(solution)/shard_map/ppermute | solution.py:42
  60.6 6.9 %shard_map.130 = bf16[128,6144]{1,0:T(8,128)(2,1)S(1)} custom-call(bf16[64,6144]{1,0:T(8,128)(2,1)S(1)} %collective-permute-done.12.refs_0_, bf16[64,6144]{1,0:T(8,128)(2,1)S(1)} %collective-permute-done.14.refs_1_, bf16[1,6144,512]{2,1,0:T(8,128)(2,1)} %refs_2_.5, bf16[1,6144,512]{2,1,0:T(8,128)(2,1)} %refs_3_.5, bf16[1,512,6144]{2,1,0:T(8,128)(2,1)} %refs_4_.7), custom_call_target="tpu_custom_call" | custom-call | flops 2415919104 | bytes 22020096 | tf_op jit(solution)/shard_map/pallas_call | solution.py:119
  67.5 6.9 %shard_map.128 = bf16[128,6144]{1,0:T(8,128)(2,1)S(1)} custom-call(bf16[64,6144]{1,0:T(8,128)(2,1)S(1)} %collective-permute-done.8.refs_0_, bf16[64,6144]{1,0:T(8,128)(2,1)S(1)} %collective-permute-done.9.refs_1_, bf16[1,6144,512]{2,1,0:T(8,128)(2,1)} %refs_2_.5, bf16[1,6144,512]{2,1,0:T(8,128)(2,1)} %refs_3_.5, bf16[1,512,6144]{2,1,0:T(8,128)(2,1)} %refs_4_.7), custom_call_target="tpu_custom_call" | custom-call | flops 2415919104 | bytes 22020096 | tf_op jit(solution)/shard_map/pallas_call | solution.py:119
  74.5 6.9 %shard_map.129 = bf16[128,6144]{1,0:T(8,128)(2,1)S(1)} custom-call(bf16[32,6144]{1,0:T(8,128)(2,1)S(1)} %collective-permute-done.10.refs_0_, bf16[32,6144]{1,0:T(8,128)(2,1)S(1)} %collective-permute-done.11.refs_1_, bf16[32,6144]{1,0:T(8,128)(2,1)S(1)} %collective-permute-done.13.refs_2_, bf16[32,6144]{1,0:T(8,128)(2,1)S(1)} %collective-permute-done.15.refs_3_, ...), custom_call_target="tpu_custom_call" | custom-call | flops 2415919104 | bytes 22020096 | tf_op jit(solution)/shard_map/pallas_call | solution.py:119
  81.7 2.7 %collective-permute-start.26 = (bf16[32,6144]{1,0:T(8,128)(2,1)S(1)}, bf16[32,6144]{1,0:T(8,128)(2,1)S(1)}, u32[]{:S(2)}, u32[]{:S(2)}) collective-permute-start(bf16[32,6144]{1,0:T(8,128)(2,1)S(1)} %get-tuple-element.12), channel_id=1, source_target_pairs={{0,24},{1,97},{2,26},{3,99},{4,28},{5,101},{6,30},{7,103},{8,0},{9... | collective-permute-start | bytes 1179656 | tf_op jit(solution)/shard_map/ppermute | solution.py:42
  84.5 2.7 %collective-permute-start.18 = (bf16[32,6144]{1,0:T(8,128)(2,1)S(1)}, bf16[32,6144]{1,0:T(8,128)(2,1)S(1)}, u32[]{:S(2)}, u32[]{:S(2)}) collective-permute-start(bf16[32,6144]{1,0:T(8,128)(2,1)S(1)} %get-tuple-element.14), channel_id=1, source_target_pairs={{0,24},{1,97},{2,26},{3,99},{4,28},{5,101},{6,30},{7,103},{8,0},{9... | collective-permute-start | bytes 1179656 | tf_op jit(solution)/shard_map/ppermute | solution.py:42
  91.9 2.7 %collective-permute-start.27 = (bf16[64,6144]{1,0:T(8,128)(2,1)}, bf16[64,6144]{1,0:T(8,128)(2,1)}, u32[]{:S(2)}, u32[]{:S(2)}) collective-permute-start(bf16[64,6144]{1,0:T(8,128)(2,1)} %pad_maximum_fusion.3), channel_id=1, source_target_pairs={{0,24},{1,97},{2,26},{3,99},{4,28},{5,101},{6,30},{7,103},{8,0},{9... | collective-permute-start | bytes 2359304 | tf_op jit(solution)/shard_map/ppermute | solution.py:42
  96.7 2.7 %collective-permute-start.19 = (bf16[64,6144]{1,0:T(8,128)(2,1)}, bf16[64,6144]{1,0:T(8,128)(2,1)}, u32[]{:S(2)}, u32[]{:S(2)}) collective-permute-start(bf16[64,6144]{1,0:T(8,128)(2,1)} %pad_maximum_fusion.1), channel_id=1, source_target_pairs={{0,24},{1,97},{2,26},{3,99},{4,28},{5,101},{6,30},{7,103},{8,0},{9... | collective-permute-start | bytes 2359304 | tf_op jit(solution)/shard_map/ppermute | solution.py:42
  100.6 6.9 %shard_map.127 = bf16[128,6144]{1,0:T(8,128)(2,1)S(1)} custom-call(bf16[64,6144]{1,0:T(8,128)(2,1)S(1)} %constant_dynamic-update-slice_fusion.refs_0_, bf16[64,6144]{1,0:T(8,128)(2,1)S(1)} %copy-done.2, bf16[1,6144,512]{2,1,0:T(8,128)(2,1)} %refs_2_.5, bf16[1,6144,512]{2,1,0:T(8,128)(2,1)} %refs_3_.5, bf16[1,512,6144]{2,1,0:T(8,128)(2,1)} %refs_4_.7), custom_call_target="tpu_custom_call" | custom-call | flops 2415919104 | bytes 22020096 | tf_op jit(solution)/shard_map/pallas_call | solution.py:119
  107.6 4.5 %collective-permute-done.17 = bf16[64,6144]{1,0:T(8,128)(2,1)} collective-permute-done((bf16[64,6144]{1,0:T(8,128)(2,1)}, bf16[64,6144]{1,0:T(8,128)(2,1)}, u32[]{:S(2)}, u32[]{:S(2)}) %collective-permute-start.17) | collective-permute-done | bytes 786464 | tf_op jit(solution)/shard_map/ppermute | solution.py:42
  114.9 2.7 %collective-permute-start.22 = (bf16[8,6144]{1,0:T(8,128)(2,1)S(1)}, bf16[8,6144]{1,0:T(8,128)(2,1)S(1)}, u32[]{:S(2)}, u32[]{:S(2)}) collective-permute-start(bf16[8,6144]{1,0:T(8,128)(2,1)S(1)} %get-tuple-element.24), channel_id=1, source_target_pairs={{0,96},{1,25},{2,98},{3,27},{4,100},{5,29},{6,102},{7,31},{8,104},... | collective-permute-start | bytes 294920 | tf_op jit(solution)/shard_map/ppermute | solution.py:38
  120.6 2.7 %collective-permute-start.23 = (bf16[16,6144]{1,0:T(8,128)(2,1)S(1)}, bf16[16,6144]{1,0:T(8,128)(2,1)S(1)}, u32[]{:S(2)}, u32[]{:S(2)}) collective-permute-start(bf16[16,6144]{1,0:T(8,128)(2,1)S(1)} %pad_maximum_fusion.6), channel_id=1, source_target_pairs={{0,96},{1,25},{2,98},{3,27},{4,100},{5,29},{6,102},{7,31},{8,104},... | collective-permute-start | bytes 589832 | tf_op jit(solution)/shard_map/ppermute | solution.py:38
  123.5 2.7 %collective-permute-start.31 = (bf16[16,6144]{1,0:T(8,128)(2,1)S(1)}, bf16[16,6144]{1,0:T(8,128)(2,1)S(1)}, u32[]{:S(2)}, u32[]{:S(2)}) collective-permute-start(bf16[16,6144]{1,0:T(8,128)(2,1)S(1)} %pad_maximum_fusion.8), channel_id=1, source_target_pairs={{0,96},{1,25},{2,98},{3,27},{4,100},{5,29},{6,102},{7,31},{8,104},... | collective-permute-start | bytes 589832 | tf_op jit(solution)/shard_map/ppermute | solution.py:38
  126.3 2.8 %collective-permute-done.29 = bf16[16,6144]{1,0:T(8,128)(2,1)S(1)} collective-permute-done((bf16[16,6144]{1,0:T(8,128)(2,1)S(1)}, bf16[16,6144]{1,0:T(8,128)(2,1)S(1)}, u32[]{:S(2)}, u32[]{:S(2)}) %collective-permute-start.29) | collective-permute-done | bytes 196640 | tf_op jit(solution)/shard_map/ppermute | solution.py:38
  130.2 11.9 %all-to-all-start = ((bf16[32,1,8,768]{3,0,1,2:T(8,128)(2,1)}), bf16[32,1,8,768]{3,0,1,2:T(8,128)(2,1)S(1)}, u32[]{:S(2)}, u32[]{:S(2)}) async-start(bf16[32,1,8,768]{3,0,1,2:T(8,128)(2,1)} %copy.58), calls=%async_computation | async-start | bytes 786432 | tf_op jit(solution)/shard_map/all_to_all | solution.py:284
  142.1 8.0 %all-to-all-done = bf16[32,1,8,768]{3,0,1,2:T(8,128)(2,1)S(1)} async-done(((bf16[32,1,8,768]{3,0,1,2:T(8,128)(2,1)}), bf16[32,1,8,768]{3,0,1,2:T(8,128)(2,1)S(1)}, u32[]{:S(2)}, u32[]{:S(2)}) %all-to-all-start) | async-done | bytes 393248 | tf_op jit(solution)/shard_map/all_to_all | solution.py:284
  (142 shorter events, 32.7 us)
Async XLA Ops:
  23.5 6.1 %collective-permute-start.4 = (bf16[16,6144]{1,0:T(8,128)(2,1)S(1)}, bf16[16,6144]{1,0:T(8,128)(2,1)S(1)}, u32[]{:S(2)}, u32[]{:S(2)}) collective-permute-start(bf16[16,6144]{1,0:T(8,128)(2,1)S(1)} %get-tuple-element.33), channel_id=1, source_target_pairs={{0,32},{1,9},{2,34},{3,11},{4,36},{5,13},{6,38},{7,15},{8,40},{9,1... | collective-permute-start | bytes 589832 | tf_op jit(solution)/shard_map/ppermute | solution.py:38
  26.3 6.2 %collective-permute-start = (bf16[16,6144]{1,0:T(8,128)(2,1)S(1)}, bf16[16,6144]{1,0:T(8,128)(2,1)S(1)}, u32[]{:S(2)}, u32[]{:S(2)}) collective-permute-start(bf16[16,6144]{1,0:T(8,128)(2,1)S(1)} %get-tuple-element.36), channel_id=1, source_target_pairs={{0,32},{1,9},{2,34},{3,11},{4,36},{5,13},{6,38},{7,15},{8,40},{9,1... | collective-permute-start | bytes 589832 | tf_op jit(solution)/shard_map/ppermute | solution.py:38
  26.3 6.3 %collective-permute-start.1 = (bf16[16,6144]{1,0:T(8,128)(2,1)S(1)}, bf16[16,6144]{1,0:T(8,128)(2,1)S(1)}, u32[]{:S(2)}, u32[]{:S(2)}) collective-permute-start(bf16[16,6144]{1,0:T(8,128)(2,1)S(1)} %get-tuple-element.36), channel_id=1, source_target_pairs={{0,96},{1,25},{2,98},{3,27},{4,100},{5,29},{6,102},{7,31},{8,104},... | collective-permute-start | bytes 589832 | tf_op jit(solution)/shard_map/ppermute | solution.py:38
  32.5 6.9 %collective-permute-start.2 = (bf16[8,6144]{1,0:T(8,128)(2,1)S(1)}, bf16[8,6144]{1,0:T(8,128)(2,1)S(1)}, u32[]{:S(2)}, u32[]{:S(2)}) collective-permute-start(bf16[8,6144]{1,0:T(8,128)(2,1)S(1)} %slice.230), channel_id=1, source_target_pairs={{0,32},{1,9},{2,34},{3,11},{4,36},{5,13},{6,38},{7,15},{8,40},{9,1... | collective-permute-start | bytes 294920 | tf_op jit(solution)/shard_map/ppermute | solution.py:38
  32.6 6.8 %collective-permute-start.3 = (bf16[8,6144]{1,0:T(8,128)(2,1)S(1)}, bf16[8,6144]{1,0:T(8,128)(2,1)S(1)}, u32[]{:S(2)}, u32[]{:S(2)}) collective-permute-start(bf16[8,6144]{1,0:T(8,128)(2,1)S(1)} %slice.231), channel_id=1, source_target_pairs={{0,96},{1,25},{2,98},{3,27},{4,100},{5,29},{6,102},{7,31},{8,104},... | collective-permute-start | bytes 294920 | tf_op jit(solution)/shard_map/ppermute | solution.py:38
  35.5 13.5 %collective-permute-start.12 = (bf16[64,6144]{1,0:T(8,128)(2,1)S(1)}, bf16[64,6144]{1,0:T(8,128)(2,1)S(1)}, u32[]{:S(2)}, u32[]{:S(2)}) collective-permute-start(bf16[64,6144]{1,0:T(8,128)(2,1)S(1)} %constant_dynamic-update-slice_fusion.5.refs_1_), channel_id=1, source_target_pairs={{0,8},{1,33},{2,10},{3,35},{4,12},{5,37},{6,14},{7,39},{8,16},{9,4... | collective-permute-start | bytes 2359304 | tf_op jit(solution)/shard_map/ppermute | solution.py:42
  36.9 12.2 %collective-permute-start.14 = (bf16[64,6144]{1,0:T(8,128)(2,1)S(1)}, bf16[64,6144]{1,0:T(8,128)(2,1)S(1)}, u32[]{:S(2)}, u32[]{:S(2)}) collective-permute-start(bf16[64,6144]{1,0:T(8,128)(2,1)S(1)} %constant_dynamic-update-slice_fusion.5.refs_1_), channel_id=1, source_target_pairs={{0,24},{1,97},{2,26},{3,99},{4,28},{5,101},{6,30},{7,103},{8,0},{9... | collective-permute-start | bytes 2359304 | tf_op jit(solution)/shard_map/ppermute | solution.py:42
  39.4 18.0 %collective-permute-start.8 = (bf16[64,6144]{1,0:T(8,128)(2,1)S(1)}, bf16[64,6144]{1,0:T(8,128)(2,1)S(1)}, u32[]{:S(2)}, u32[]{:S(2)}) collective-permute-start(bf16[64,6144]{1,0:T(8,128)(2,1)S(1)} %constant_dynamic-update-slice_fusion.refs_0_), channel_id=1, source_target_pairs={{0,8},{1,33},{2,10},{3,35},{4,12},{5,37},{6,14},{7,39},{8,16},{9,4... | collective-permute-start | bytes 2359304 | tf_op jit(solution)/shard_map/ppermute | solution.py:42
  39.5 18.0 %collective-permute-start.9 = (bf16[64,6144]{1,0:T(8,128)(2,1)S(1)}, bf16[64,6144]{1,0:T(8,128)(2,1)S(1)}, u32[]{:S(2)}, u32[]{:S(2)}) collective-permute-start(bf16[64,6144]{1,0:T(8,128)(2,1)S(1)} %constant_dynamic-update-slice_fusion.refs_0_), channel_id=1, source_target_pairs={{0,24},{1,97},{2,26},{3,99},{4,28},{5,101},{6,30},{7,103},{8,0},{9... | collective-permute-start | bytes 2359304 | tf_op jit(solution)/shard_map/ppermute | solution.py:42
  49.0 25.5 %collective-permute-start.13 = (bf16[32,6144]{1,0:T(8,128)(2,1)S(1)}, bf16[32,6144]{1,0:T(8,128)(2,1)S(1)}, u32[]{:S(2)}, u32[]{:S(2)}) collective-permute-start(bf16[32,6144]{1,0:T(8,128)(2,1)S(1)} %slice.239), channel_id=1, source_target_pairs={{0,8},{1,33},{2,10},{3,35},{4,12},{5,37},{6,14},{7,39},{8,16},{9,4... | collective-permute-start | bytes 1179656 | tf_op jit(solution)/shard_map/ppermute | solution.py:42
  49.1 25.4 %collective-permute-start.15 = (bf16[32,6144]{1,0:T(8,128)(2,1)S(1)}, bf16[32,6144]{1,0:T(8,128)(2,1)S(1)}, u32[]{:S(2)}, u32[]{:S(2)}) collective-permute-start(bf16[32,6144]{1,0:T(8,128)(2,1)S(1)} %slice.240), channel_id=1, source_target_pairs={{0,24},{1,97},{2,26},{3,99},{4,28},{5,101},{6,30},{7,103},{8,0},{9... | collective-permute-start | bytes 1179656 | tf_op jit(solution)/shard_map/ppermute | solution.py:42
  57.4 17.1 %collective-permute-start.10 = (bf16[32,6144]{1,0:T(8,128)(2,1)S(1)}, bf16[32,6144]{1,0:T(8,128)(2,1)S(1)}, u32[]{:S(2)}, u32[]{:S(2)}) collective-permute-start(bf16[32,6144]{1,0:T(8,128)(2,1)S(1)} %slice.237), channel_id=1, source_target_pairs={{0,8},{1,33},{2,10},{3,35},{4,12},{5,37},{6,14},{7,39},{8,16},{9,4... | collective-permute-start | bytes 1179656 | tf_op jit(solution)/shard_map/ppermute | solution.py:42
  57.6 16.9 %collective-permute-start.11 = (bf16[32,6144]{1,0:T(8,128)(2,1)S(1)}, bf16[32,6144]{1,0:T(8,128)(2,1)S(1)}, u32[]{:S(2)}, u32[]{:S(2)}) collective-permute-start(bf16[32,6144]{1,0:T(8,128)(2,1)S(1)} %slice.238), channel_id=1, source_target_pairs={{0,24},{1,97},{2,26},{3,99},{4,28},{5,101},{6,30},{7,103},{8,0},{9... | collective-permute-start | bytes 1179656 | tf_op jit(solution)/shard_map/ppermute | solution.py:42
  81.6 8.2 %collective-permute-start.24 = (bf16[32,6144]{1,0:T(8,128)(2,1)S(1)}, bf16[32,6144]{1,0:T(8,128)(2,1)S(1)}, u32[]{:S(2)}, u32[]{:S(2)}) collective-permute-start(bf16[32,6144]{1,0:T(8,128)(2,1)S(1)} %get-tuple-element.13), channel_id=1, source_target_pairs={{0,8},{1,33},{2,10},{3,35},{4,12},{5,37},{6,14},{7,39},{8,16},{9,4... | collective-permute-start | bytes 1179656 | tf_op jit(solution)/shard_map/ppermute | solution.py:42
  81.7 8.1 %collective-permute-start.26 = (bf16[32,6144]{1,0:T(8,128)(2,1)S(1)}, bf16[32,6144]{1,0:T(8,128)(2,1)S(1)}, u32[]{:S(2)}, u32[]{:S(2)}) collective-permute-start(bf16[32,6144]{1,0:T(8,128)(2,1)S(1)} %get-tuple-element.12), channel_id=1, source_target_pairs={{0,24},{1,97},{2,26},{3,99},{4,28},{5,101},{6,30},{7,103},{8,0},{9... | collective-permute-start | bytes 1179656 | tf_op jit(solution)/shard_map/ppermute | solution.py:42
  84.4 10.2 %collective-permute-start.16 = (bf16[32,6144]{1,0:T(8,128)(2,1)S(1)}, bf16[32,6144]{1,0:T(8,128)(2,1)S(1)}, u32[]{:S(2)}, u32[]{:S(2)}) collective-permute-start(bf16[32,6144]{1,0:T(8,128)(2,1)S(1)} %get-tuple-element.11), channel_id=1, source_target_pairs={{0,8},{1,33},{2,10},{3,35},{4,12},{5,37},{6,14},{7,39},{8,16},{9,4... | collective-permute-start | bytes 1179656 | tf_op jit(solution)/shard_map/ppermute | solution.py:42
  84.5 10.1 %collective-permute-start.18 = (bf16[32,6144]{1,0:T(8,128)(2,1)S(1)}, bf16[32,6144]{1,0:T(8,128)(2,1)S(1)}, u32[]{:S(2)}, u32[]{:S(2)}) collective-permute-start(bf16[32,6144]{1,0:T(8,128)(2,1)S(1)} %get-tuple-element.14), channel_id=1, source_target_pairs={{0,24},{1,97},{2,26},{3,99},{4,28},{5,101},{6,30},{7,103},{8,0},{9... | collective-permute-start | bytes 1179656 | tf_op jit(solution)/shard_map/ppermute | solution.py:42
  90.9 16.6 %collective-permute-start.25 = (bf16[64,6144]{1,0:T(8,128)(2,1)}, bf16[64,6144]{1,0:T(8,128)(2,1)}, u32[]{:S(2)}, u32[]{:S(2)}) collective-permute-start(bf16[64,6144]{1,0:T(8,128)(2,1)} %pad_maximum_fusion.2), channel_id=1, source_target_pairs={{0,8},{1,33},{2,10},{3,35},{4,12},{5,37},{6,14},{7,39},{8,16},{9,4... | collective-permute-start | bytes 2359304 | tf_op jit(solution)/shard_map/ppermute | solution.py:42
  91.9 15.7 %collective-permute-start.27 = (bf16[64,6144]{1,0:T(8,128)(2,1)}, bf16[64,6144]{1,0:T(8,128)(2,1)}, u32[]{:S(2)}, u32[]{:S(2)}) collective-permute-start(bf16[64,6144]{1,0:T(8,128)(2,1)} %pad_maximum_fusion.3), channel_id=1, source_target_pairs={{0,24},{1,97},{2,26},{3,99},{4,28},{5,101},{6,30},{7,103},{8,0},{9... | collective-permute-start | bytes 2359304 | tf_op jit(solution)/shard_map/ppermute | solution.py:42
  95.7 16.3 %collective-permute-start.17 = (bf16[64,6144]{1,0:T(8,128)(2,1)}, bf16[64,6144]{1,0:T(8,128)(2,1)}, u32[]{:S(2)}, u32[]{:S(2)}) collective-permute-start(bf16[64,6144]{1,0:T(8,128)(2,1)} %pad_maximum_fusion), channel_id=1, source_target_pairs={{0,8},{1,33},{2,10},{3,35},{4,12},{5,37},{6,14},{7,39},{8,16},{9,4... | collective-permute-start | bytes 2359304 | tf_op jit(solution)/shard_map/ppermute | solution.py:42
  96.7 15.6 %collective-permute-start.19 = (bf16[64,6144]{1,0:T(8,128)(2,1)}, bf16[64,6144]{1,0:T(8,128)(2,1)}, u32[]{:S(2)}, u32[]{:S(2)}) collective-permute-start(bf16[64,6144]{1,0:T(8,128)(2,1)} %pad_maximum_fusion.1), channel_id=1, source_target_pairs={{0,24},{1,97},{2,26},{3,99},{4,28},{5,101},{6,30},{7,103},{8,0},{9... | collective-permute-start | bytes 2359304 | tf_op jit(solution)/shard_map/ppermute | solution.py:42
  120.5 5.8 %collective-permute-start.21 = (bf16[16,6144]{1,0:T(8,128)(2,1)S(1)}, bf16[16,6144]{1,0:T(8,128)(2,1)S(1)}, u32[]{:S(2)}, u32[]{:S(2)}) collective-permute-start(bf16[16,6144]{1,0:T(8,128)(2,1)S(1)} %pad_maximum_fusion.5), channel_id=1, source_target_pairs={{0,32},{1,9},{2,34},{3,11},{4,36},{5,13},{6,38},{7,15},{8,40},{9,1... | collective-permute-start | bytes 589832 | tf_op jit(solution)/shard_map/ppermute | solution.py:38
  123.4 5.8 %collective-permute-start.29 = (bf16[16,6144]{1,0:T(8,128)(2,1)S(1)}, bf16[16,6144]{1,0:T(8,128)(2,1)S(1)}, u32[]{:S(2)}, u32[]{:S(2)}) collective-permute-start(bf16[16,6144]{1,0:T(8,128)(2,1)S(1)} %pad_maximum_fusion.7), channel_id=1, source_target_pairs={{0,32},{1,9},{2,34},{3,11},{4,36},{5,13},{6,38},{7,15},{8,40},{9,1... | collective-permute-start | bytes 589832 | tf_op jit(solution)/shard_map/ppermute | solution.py:38
  130.2 19.9 %all-to-all-start = ((bf16[32,1,8,768]{3,0,1,2:T(8,128)(2,1)}), bf16[32,1,8,768]{3,0,1,2:T(8,128)(2,1)S(1)}, u32[]{:S(2)}, u32[]{:S(2)}) async-start(bf16[32,1,8,768]{3,0,1,2:T(8,128)(2,1)} %copy.58), calls=%async_computation | async-start | bytes 786432 | tf_op jit(solution)/shard_map/all_to_all | solution.py:284
  (17 other events, 100.2 us)

commit v4 on v3

--- a/solution.py
+++ b/solution.py
@@ -12,8 +12,6 @@
 E = 8
 CAP = 32
 SIDE = 4
-CHAINS = 2
-CHAIN_ROWS = CAP // CHAINS
 
 
 EPSILON = 1e-05
@@ -54,25 +52,14 @@
     return (one.astype(jnp.float32) + other.astype(jnp.float32)).astype(jnp.bfloat16)
 
 
-def ring_sum(behind, own, ahead, far_low, far_high, shift):
-    half = far_low.shape[0]
-    got_low = shift(far_low, 1)
-    got_high = shift(far_high, -1)
-    up = jnp.concatenate([add_rounded(ahead[:half], got_low), ahead[half:]], axis=0)
-    down = jnp.concatenate([behind[:half], add_rounded(behind[half:], got_high)], axis=0)
-    from_behind = shift(up, 1)
-    from_ahead = shift(down, -1)
-    return (
-        own.astype(jnp.float32) + from_behind.astype(jnp.float32) + from_ahead.astype(jnp.float32)
-    )
-
-
 CHUNKS = 4
 
 
 def feed_kernel(count, *refs):
     row_refs = refs[:count]
-    gate_hbm, up_hbm, down_hbm, out_ref, rows, gate, up, down, ready = refs[count:]
+    gate_hbm, up_hbm, down_hbm = refs[count : count + 3]
+    out_refs = refs[count + 3 : 2 * count + 3]
+    rows, gate, up, down, ready = refs[2 * count + 3 :]
     width, hidden = gate.shape
     depth = width // CHUNKS
     copies = []
@@ -108,9 +95,13 @@
     active = (jax.nn.silu(gate_sum) * up_sum).astype(jnp.bfloat16)
     for k in range(CHUNKS):
         copies[2 * CHUNKS + k].wait()
-        out_ref[:, k * depth : (k + 1) * depth] = jnp.dot(
+        partial = jnp.dot(
             active, down[:, k * depth : (k + 1) * depth], preferred_element_type=jnp.float32
         ).astype(jnp.bfloat16)
+        at = 0
+        for ref in out_refs:
+            ref[:, k * depth : (k + 1) * depth] = partial[at : at + ref.shape[0]]
+            at += ref.shape[0]
 
 
 def feed(row_arrays, w_gate, w_up, w_down):
@@ -120,8 +111,8 @@
         functools.partial(feed_kernel, len(row_arrays)),
         in_specs=[pl.BlockSpec(memory_space=pltpu.VMEM)] * len(row_arrays)
         + [pl.BlockSpec(memory_space=pltpu.HBM)] * 3,
-        out_specs=pl.BlockSpec(memory_space=pltpu.VMEM),
-        out_shape=jax.ShapeDtypeStruct((count, width), jnp.bfloat16),
+        out_specs=[pl.BlockSpec(memory_space=pltpu.VMEM)] * len(row_arrays),
+        out_shape=[jax.ShapeDtypeStruct(array.shape, jnp.bfloat16) for array in row_arrays],
         scratch_shapes=[
             pltpu.VMEM((count, width), jnp.bfloat16),
             pltpu.VMEM((width, hidden), jnp.bfloat16),
@@ -138,13 +129,26 @@
     )(*row_arrays, w_gate, w_up, w_down)
 
 
-def gather_ring(block, shift):
-    half = block.shape[0] // 2
-    near_up = shift(block, 1)
-    near_down = shift(block, -1)
-    far_low = shift(near_up[:half], 1)
-    far_high = shift(near_down[half:], -1)
-    return block, near_up, near_down, far_low, far_high
+def spread_near(block, shift):
+    return shift(block, 1), shift(block, -1)
+
+
+def spread_far(near_up, near_down, shift):
+    half = near_up.shape[0] // 2
+    return shift(near_up[:half], 1), shift(near_down[half:], -1)
+
+
+def halves_added(ahead, behind, far_low, far_high, shift):
+    half = far_low.shape[0]
+    got_low, got_high = shift(far_low, 1), shift(far_high, -1)
+    up = ahead.at[:half].set(add_rounded(ahead[:half], got_low))
+    down = behind.at[half:].set(add_rounded(behind[half:], got_high))
+    return up, down
+
+
+def add_three(own, one, other):
+    total = own.astype(jnp.float32) + one.astype(jnp.float32) + other.astype(jnp.float32)
+    return total.astype(jnp.bfloat16)
 
 
 def on_device(
@@ -248,37 +252,38 @@
     outgoing = (outgoing * own_scale).astype(jnp.bfloat16)
 
     weights = (w_gate, w_up, w_down)
-    lines = []
-    for chain in range(CHAINS):
-        slab = outgoing[chain * CHAIN_ROWS : (chain + 1) * CHAIN_ROWS]
-        line = jnp.concatenate(gather_ring(slab, shift_first), axis=0)
-        lines.append(gather_ring(line, shift_second))
-    part_own = feed([line[0] for line in lines], *weights)
-    part_near = [feed([line[1], line[2]], *weights) for line in lines]
-    part_far = feed([piece for line in lines for piece in line[3:]], *weights)
-    results = []
-    for chain in range(CHAINS):
-        count = SIDE * CHAIN_ROWS
-        line_sum = ring_sum(
-            part_near[chain][:count],
-            part_own[chain * count : (chain + 1) * count],
-            part_near[chain][count:],
-            part_far[chain * count : chain * count + count // 2],
-            part_far[chain * count + count // 2 : (chain + 1) * count],
-            shift_second,
-        ).astype(jnp.bfloat16)
-        row = CHAIN_ROWS
-        results.append(
-            ring_sum(
-                line_sum[row : 2 * row],
-                line_sum[:row],
-                line_sum[2 * row : 3 * row],
-                line_sum[3 * row : 3 * row + row // 2],
-                line_sum[3 * row + row // 2 :],
-                shift_first,
-            ).astype(jnp.bfloat16)
-        )
-    expert_result = jnp.concatenate(results, axis=0)
+    near_up, near_down = spread_near(outgoing, shift_first)
+    far_low, far_high = spread_far(near_up, near_down, shift_first)
+    one = jnp.concatenate([outgoing, near_up], axis=0)
+    two = jnp.concatenate([near_down, far_low, far_high], axis=0)
+    one_near = spread_near(one, shift_second)
+    two_near = spread_near(two, shift_second)
+    one_far = spread_far(*one_near, shift_second)
+    one_near_part = feed(one_near, *weights)
+    two_near, one_near_part = lax.optimization_barrier((two_near, one_near_part))
+    two_far = spread_far(*two_near, shift_second)
+    two_near_part = feed(two_near, *weights)
+    two_far, two_near_part = lax.optimization_barrier((two_far, two_near_part))
+    far_part = feed([*one_far, *two_far], *weights)
+
+    two_up, two_down = halves_added(
+        two_near_part[1], two_near_part[0], far_part[2], far_part[3], shift_second
+    )
+    one_up, one_down = halves_added(
+        one_near_part[1], one_near_part[0], far_part[0], far_part[1], shift_second
+    )
+    one, two = lax.optimization_barrier((one, two, one_up, one_down, two_up, two_down))[:2]
+    one_own, two_own = feed([one, two], *weights)
+    two_sum = add_three(two_own, shift_second(two_up, 1), shift_second(two_down, -1))
+    one_sum = add_three(one_own, shift_second(one_up, 1), shift_second(one_down, -1))
+    up, down = halves_added(
+        two_sum[:CAP],
+        one_sum[CAP:],
+        two_sum[CAP : CAP + CAP // 2],
+        two_sum[CAP + CAP // 2 :],
+        shift_first,
+    )
+    expert_result = add_three(one_sum[:CAP], shift_first(up, 1), shift_first(down, -1))
 
     expert_result = expert_result.reshape(CAP, 1, expert_devices, width_local)
     returned = lax.all_to_all(expert_result, "expert", split_axis=2, concat_axis=1, tiled=True)

time: 152 us -> 157 us (1.033)
  waiting for transfers between devices: 31.3 us -> 61.3 us
  starting transfers between devices: 57.4 us -> 37.4 us
  other arithmetic: 10.4 us -> 7.08 us
    ppermute x16 -> x8, waiting for transfers between devices: 3.59 us -> 29.6 us  [shift_first(): return lax.ppermute(value, ('attn', 'expert'), ring_pairs(step, False))]
    ppermute x16 -> x8, starting transfers between devices: 22.1 us -> 7.08 us  [shift_first(): return lax.ppermute(value, ('attn', 'expert'), ring_pairs(step, False))]
    ppermute x16, starting transfers between devices: 23.4 us -> 16.4 us  [shift_second(): return lax.ppermute(value, ('attn', 'expert'), ring_pairs(step, True))]
    ppermute x16, waiting for transfers between devices: 19.6 us -> 23.7 us  [shift_second(): return lax.ppermute(value, ('attn', 'expert'), ring_pairs(step, True))]
    concatenate x9 -> x1, other arithmetic: 3.88 us -> 0.05 us  [on_device(): one = jnp.concatenate([outgoing, near_up], axis=0)]
    all_to_all x1, starting transfers between devices: 11.9 us -> 13.9 us  [on_device(): lax.all_to_all(expert_result, 'expert', split_axis=2, concat_axis=1, tile...]
    scatter x0 -> x6, other arithmetic: none -> 1.82 us  [the longest x3 1.25 us: halves_added(): up = ahead.at[:half].set(add_rounded(ahead[:half], got_low))]
    convert_element_type x7 -> x3, other arithmetic: 3.16 us -> 1.82 us  [add_three(): return total.astype(jnp.bfloat16)]
  transfers between devices with their start and end apart: 33 -> 25, of which waited for: 9 -> 16; matrix products, arithmetic and copies ran while one was open for 3% -> 2% of each run, Pallas kernels for 14% -> 13%
where the time goes in v4:
time: 157 us
  waiting for transfers between devices  61.3 us (39%)
  starting transfers between devices  37.4 us (24%)
  Pallas kernels  27.7 us (18%)
  blocking collectives  15.4 us (10%)
  other arithmetic  7.08 us (5%)
  matrix products  3.86 us (2%)
  local copies, waits for them, and re-layouts  3.82 us (2%)
    ppermute x8, waiting for transfers between devices, shift_first(): return lax.ppermute(value, ('attn', 'expert'), ring_pairs(step, False))  29.6 us
    pallas_call x4, Pallas kernels, feed(): pl.pallas_call(functools.partial(feed_kernel, len(row_arrays)), in_specs=...  27.7 us
    ppermute x16, waiting for transfers between devices, shift_second(): return lax.ppermute(value, ('attn', 'expert'), ring_pairs(step, True))  23.7 us
    ppermute x16, starting transfers between devices, shift_second(): return lax.ppermute(value, ('attn', 'expert'), ring_pairs(step, True))  16.4 us
    all_gather x1, blocking collectives, on_device(): gathered = lax.all_gather(payload, 'expert', axis=0)  15.4 us
    all_to_all x1, starting transfers between devices, on_device(): lax.all_to_all(expert_result, 'expert', split_axis=2, concat_axis=1, tile...  13.9 us
    all_to_all x1, waiting for transfers between devices, on_device(): lax.all_to_all(expert_result, 'expert', split_axis=2, concat_axis=1, tile...  8.04 us
    ppermute x8, starting transfers between devices, shift_first(): return lax.ppermute(value, ('attn', 'expert'), ring_pairs(step, False))  7.08 us
  transfers between devices with their start and end apart: 25, of which 16 were waited for; matrix products, arithmetic and copies ran while one was open for 2% of the time, Pallas kernels for 13%

profile of v4, /device:TPU:1, one launch (start us, length us, event | category | flops | bytes accessed | tf_op | source)
XLA Modules:
  0.0 157.0 jit_solution(14674842810971075089)
XLA Ops:
  7.2 15.4 %all-gather = bf16[512,896]{1,0:T(8,128)(2,1)S(1)} all-gather(bf16[64,896]{1,0:T(8,128)(2,1)S(1)} %concatenate.25), channel_id=2, replica_groups=mesh['attn'=16,'expert'=8] {'expert'}, dimensions={0}, use_global_device_ids=true | all-gather | bytes 1032192 | tf_op jit(solution)/shard_map/all_gather | solution.py:221
  24.8 1.5 collective-permute-start.1
  26.2 5.5 %collective-permute-done = bf16[32,6144]{1,0:T(8,128)(2,1)S(1)} collective-permute-done((bf16[32,6144]{1,0:T(8,128)(2,1)S(1)}, bf16[32,6144]{1,0:T(8,128)(2,1)S(1)}, u32[]{:S(2)}, u32[]{:S(2)}) %collective-permute-start) | collective-permute-done | bytes 393248 | tf_op jit(solution)/shard_map/ppermute | solution.py:36
  31.7 3.8 %collective-permute-start.7 = (bf16[64,6144]{1,0:T(8,128)(2,1)S(1)}, bf16[64,6144]{1,0:T(8,128)(2,1)S(1)}, u32[]{:S(2)}, u32[]{:S(2)}) collective-permute-start(bf16[64,6144]{1,0:T(8,128)(2,1)S(1)} %pad_maximum_fusion.refs_0_), channel_id=1, source_target_pairs={{0,24},{1,97},{2,26},{3,99},{4,28},{5,101},{6,30},{7,103},{8,0},{9... | collective-permute-start | bytes 2359304 | tf_op jit(solution)/shard_map/ppermute | solution.py:40
  37.2 7.9 %collective-permute-done.2 = bf16[16,6144]{1,0:T(8,128)(2,1)S(1)} collective-permute-done((bf16[16,6144]{1,0:T(8,128)(2,1)S(1)}, bf16[16,6144]{1,0:T(8,128)(2,1)S(1)}, u32[]{:S(2)}, u32[]{:S(2)}) %collective-permute-start.2) | collective-permute-done | bytes 196640 | tf_op jit(solution)/shard_map/ppermute | solution.py:36
  45.2 2.8 %collective-permute-start.5 = (bf16[64,6144]{1,0:T(8,128)(2,1)S(1)}, bf16[64,6144]{1,0:T(8,128)(2,1)S(1)}, u32[]{:S(2)}, u32[]{:S(2)}) collective-permute-start(bf16[64,6144]{1,0:T(8,128)(2,1)S(1)} %constant_dynamic-update-slice_fusion.refs_1_), channel_id=1, source_target_pairs={{0,24},{1,97},{2,26},{3,99},{4,28},{5,101},{6,30},{7,103},{8,0},{9... | collective-permute-start | bytes 2359304 | tf_op jit(solution)/shard_map/ppermute | solution.py:40
  47.9 2.1 %collective-permute-done.6.refs_0_ = bf16[64,6144]{1,0:T(8,128)(2,1)S(1)} collective-permute-done((bf16[64,6144]{1,0:T(8,128)(2,1)S(1)}, bf16[64,6144]{1,0:T(8,128)(2,1)S(1)}, u32[]{:S(2)}, u32[]{:S(2)}) %collective-permute-start.6) | collective-permute-done | bytes 786464 | tf_op jit(solution)/shard_map/ppermute | solution.py:40
  50.0 6.9 %shard_map.127 = (bf16[64,6144]{1,0:T(8,128)(2,1)S(1)}, bf16[64,6144]{1,0:T(8,128)(2,1)S(1)}) custom-call(bf16[64,6144]{1,0:T(8,128)(2,1)S(1)} %collective-permute-done.6.refs_0_, bf16[64,6144]{1,0:T(8,128)(2,1)S(1)} %collective-permute-done.7.refs_1_, bf16[1,6144,512]{2,1,0:T(8,128)(2,1)} %refs_2_.5, bf16[1,6144,512]{2,1,0:T(8,128)(2,1)} %refs_3_.5, ...), custom_call_target="tpu_custom_call" | custom-call | flops 2415919104 | bytes 22020096 | tf_op jit(solution)/shard_map/pallas_call | solution.py:110
  56.9 3.3 %collective-permute-done.4.refs_0_ = bf16[64,6144]{1,0:T(8,128)(2,1)S(1)} collective-permute-done((bf16[64,6144]{1,0:T(8,128)(2,1)S(1)}, bf16[64,6144]{1,0:T(8,128)(2,1)S(1)}, u32[]{:S(2)}, u32[]{:S(2)}) %collective-permute-start.4) | collective-permute-done | bytes 786464 | tf_op jit(solution)/shard_map/ppermute | solution.py:40
  63.7 6.9 %shard_map.128 = (bf16[64,6144]{1,0:T(8,128)(2,1)S(1)}, bf16[64,6144]{1,0:T(8,128)(2,1)S(1)}) custom-call(bf16[64,6144]{1,0:T(8,128)(2,1)S(1)} %collective-permute-done.4.refs_0_, bf16[64,6144]{1,0:T(8,128)(2,1)S(1)} %collective-permute-done.5.refs_1_, bf16[1,6144,512]{2,1,0:T(8,128)(2,1)} %refs_2_.5, bf16[1,6144,512]{2,1,0:T(8,128)(2,1)} %refs_3_.5, ...), custom_call_target="tpu_custom_call" | custom-call | flops 2415919104 | bytes 22020096 | tf_op jit(solution)/shard_map/pallas_call | solution.py:110
  72.8 6.9 %shard_map.129 = (bf16[32,6144]{1,0:T(8,128)(2,1)S(1)}, bf16[32,6144]{1,0:T(8,128)(2,1)S(1)}, bf16[32,6144]{1,0:T(8,128)(2,1)S(1)}, bf16[32,6144]{1,0:T(8,128)(2,1)S(1)}) custom-call(bf16[32,6144]{1,0:T(8,128)(2,1)S(1)} %collective-permute-done.8.refs_0_, bf16[32,6144]{1,0:T(8,128)(2,1)S(1)} %collective-permute-done.9.refs_1_, ...), custom_call_target="tpu_custom_call" | custom-call | flops 2415919104 | bytes 22020096 | tf_op jit(solution)/shard_map/pallas_call | solution.py:110
  81.3 1.6 collective-permute-start.13
  82.9 3.6 %collective-permute-done.15 = bf16[32,6144]{1,0:T(8,128)(2,1)S(1)} collective-permute-done((bf16[32,6144]{1,0:T(8,128)(2,1)S(1)}, bf16[32,6144]{1,0:T(8,128)(2,1)S(1)}, u32[]{:S(2)}, u32[]{:S(2)}) %collective-permute-start.15) | collective-permute-done | bytes 393248 | tf_op jit(solution)/shard_map/ppermute | solution.py:40
  86.7 1.6 %collective-permute-start.19 = (bf16[64,6144]{1,0:T(8,128)(2,1)S(1)}, bf16[64,6144]{1,0:T(8,128)(2,1)S(1)}, u32[]{:S(2)}, u32[]{:S(2)}) collective-permute-start(bf16[64,6144]{1,0:T(8,128)(2,1)S(1)} %fusion.20), channel_id=1, source_target_pairs={{0,24},{1,97},{2,26},{3,99},{4,28},{5,101},{6,30},{7,103},{8,0},{9... | collective-permute-start | bytes 2359304 | tf_op jit(solution)/shard_map/ppermute | solution.py:40
  88.4 4.2 %collective-permute-done.14 = bf16[32,6144]{1,0:T(8,128)(2,1)S(1)} collective-permute-done((bf16[32,6144]{1,0:T(8,128)(2,1)S(1)}, bf16[32,6144]{1,0:T(8,128)(2,1)S(1)}, u32[]{:S(2)}, u32[]{:S(2)}) %collective-permute-start.14) | collective-permute-done | bytes 393248 | tf_op jit(solution)/shard_map/ppermute | solution.py:40
  93.7 6.9 %shard_map.130 = (bf16[64,6144]{1,0:T(8,128)(2,1)S(1)}, bf16[64,6144]{1,0:T(8,128)(2,1)S(1)}) custom-call(bf16[64,6144]{1,0:T(8,128)(2,1)S(1)} %pad_maximum_fusion.refs_0_, bf16[64,6144]{1,0:T(8,128)(2,1)S(1)} %constant_dynamic-update-slice_fusion.refs_1_, bf16[1,6144,512]{2,1,0:T(8,128)(2,1)} %refs_2_.5, bf16[1,6144,512]{2,1,0:T(8,128)(2,1)} %refs_3_.5, ...), custom_call_target="tpu_custom_call" | custom-call | flops 2415919104 | bytes 22020096 | tf_op jit(solution)/shard_map/pallas_call | solution.py:110
  100.6 4.8 %collective-permute-done.18 = bf16[64,6144]{1,0:T(8,128)(2,1)S(1)} collective-permute-done((bf16[64,6144]{1,0:T(8,128)(2,1)S(1)}, bf16[64,6144]{1,0:T(8,128)(2,1)S(1)}, u32[]{:S(2)}, u32[]{:S(2)}) %collective-permute-start.18) | collective-permute-done | bytes 786464 | tf_op jit(solution)/shard_map/ppermute | solution.py:40
  108.1 5.6 %collective-permute-done.20 = bf16[16,6144]{1,0:T(8,128)(2,1)S(1)} collective-permute-done((bf16[16,6144]{1,0:T(8,128)(2,1)S(1)}, bf16[16,6144]{1,0:T(8,128)(2,1)S(1)}, u32[]{:S(2)}, u32[]{:S(2)}) %collective-permute-start.20) | collective-permute-done | bytes 196640 | tf_op jit(solution)/shard_map/ppermute | solution.py:36
  114.5 2.2 %collective-permute-done.17 = bf16[64,6144]{1,0:T(8,128)(2,1)S(1)} collective-permute-done((bf16[64,6144]{1,0:T(8,128)(2,1)S(1)}, bf16[64,6144]{1,0:T(8,128)(2,1)S(1)}, u32[]{:S(2)}, u32[]{:S(2)}) %collective-permute-start.17) | collective-permute-done | bytes 786464 | tf_op jit(solution)/shard_map/ppermute | solution.py:40
  118.4 2.4 %collective-permute-done.22 = bf16[16,6144]{1,0:T(8,128)(2,1)S(1)} collective-permute-done((bf16[16,6144]{1,0:T(8,128)(2,1)S(1)}, bf16[16,6144]{1,0:T(8,128)(2,1)S(1)}, u32[]{:S(2)}, u32[]{:S(2)}) %collective-permute-start.22) | collective-permute-done | bytes 196640 | tf_op jit(solution)/shard_map/ppermute | solution.py:36
  120.9 2.6 %collective-permute-start.23 = (bf16[32,6144]{1,0:T(8,128)(2,1)S(1)}, bf16[32,6144]{1,0:T(8,128)(2,1)}, u32[]{:S(2)}, u32[]{:S(2)}) collective-permute-start(bf16[32,6144]{1,0:T(8,128)(2,1)S(1)} %fusion.25), channel_id=1, source_target_pairs={{0,96},{1,25},{2,98},{3,27},{4,100},{5,29},{6,102},{7,31},{8,104},... | collective-permute-start | bytes 1179656 | tf_op jit(solution)/shard_map/ppermute | solution.py:36
  123.6 7.9 %collective-permute-done.21 = bf16[32,6144]{1,0:T(8,128)(2,1)} collective-permute-done((bf16[32,6144]{1,0:T(8,128)(2,1)}, bf16[32,6144]{1,0:T(8,128)(2,1)}, u32[]{:S(2)}, u32[]{:S(2)}) %collective-permute-start.21) | collective-permute-done | bytes 393248 | tf_op jit(solution)/shard_map/ppermute | solution.py:36
  133.9 13.9 %all-to-all-start = ((bf16[32,1,8,768]{3,0,1,2:T(8,128)(2,1)}), bf16[32,1,8,768]{3,0,1,2:T(8,128)(2,1)S(1)}, u32[]{:S(2)}, u32[]{:S(2)}) async-start(bf16[32,1,8,768]{3,0,1,2:T(8,128)(2,1)} %copy.58), calls=%async_computation | async-start | bytes 786432 | tf_op jit(solution)/shard_map/all_to_all | solution.py:289
  147.8 8.0 %all-to-all-done = bf16[32,1,8,768]{3,0,1,2:T(8,128)(2,1)S(1)} async-done(((bf16[32,1,8,768]{3,0,1,2:T(8,128)(2,1)}), bf16[32,1,8,768]{3,0,1,2:T(8,128)(2,1)S(1)}, u32[]{:S(2)}, u32[]{:S(2)}) %all-to-all-start) | async-done | bytes 393248 | tf_op jit(solution)/shard_map/all_to_all | solution.py:289
  (106 shorter events, 28.2 us)
Async XLA Ops:
  23.5 8.2 %collective-permute-start = (bf16[32,6144]{1,0:T(8,128)(2,1)S(1)}, bf16[32,6144]{1,0:T(8,128)(2,1)S(1)}, u32[]{:S(2)}, u32[]{:S(2)}) collective-permute-start(bf16[32,6144]{1,0:T(8,128)(2,1)S(1)} %multiply_convert_fusion), channel_id=1, source_target_pairs={{0,32},{1,9},{2,34},{3,11},{4,36},{5,13},{6,38},{7,15},{8,40},{9,1... | collective-permute-start | bytes 1179656 | tf_op jit(solution)/shard_map/ppermute | solution.py:36
  24.8 10.8 %collective-permute-start.1 = (bf16[32,6144]{1,0:T(8,128)(2,1)S(1)}, bf16[32,6144]{1,0:T(8,128)(2,1)S(1)}, u32[]{:S(2)}, u32[]{:S(2)}) collective-permute-start(bf16[32,6144]{1,0:T(8,128)(2,1)S(1)} %multiply_convert_fusion), channel_id=1, source_target_pairs={{0,96},{1,25},{2,98},{3,27},{4,100},{5,29},{6,102},{7,31},{8,104},... | collective-permute-start | bytes 1179656 | tf_op jit(solution)/shard_map/ppermute | solution.py:36
  31.7 16.2 %collective-permute-start.7 = (bf16[64,6144]{1,0:T(8,128)(2,1)S(1)}, bf16[64,6144]{1,0:T(8,128)(2,1)S(1)}, u32[]{:S(2)}, u32[]{:S(2)}) collective-permute-start(bf16[64,6144]{1,0:T(8,128)(2,1)S(1)} %pad_maximum_fusion.refs_0_), channel_id=1, source_target_pairs={{0,24},{1,97},{2,26},{3,99},{4,28},{5,101},{6,30},{7,103},{8,0},{9... | collective-permute-start | bytes 2359304 | tf_op jit(solution)/shard_map/ppermute | solution.py:40
  35.6 14.5 %collective-permute-start.6 = (bf16[64,6144]{1,0:T(8,128)(2,1)S(1)}, bf16[64,6144]{1,0:T(8,128)(2,1)S(1)}, u32[]{:S(2)}, u32[]{:S(2)}) collective-permute-start(bf16[64,6144]{1,0:T(8,128)(2,1)S(1)} %pad_maximum_fusion.refs_0_), channel_id=1, source_target_pairs={{0,8},{1,33},{2,10},{3,35},{4,12},{5,37},{6,14},{7,39},{8,16},{9,4... | collective-permute-start | bytes 2359304 | tf_op jit(solution)/shard_map/ppermute | solution.py:40
  35.6 9.6 %collective-permute-start.3 = (bf16[16,6144]{1,0:T(8,128)(2,1)S(1)}, bf16[16,6144]{1,0:T(8,128)(2,1)S(1)}, u32[]{:S(2)}, u32[]{:S(2)}) collective-permute-start(bf16[16,6144]{1,0:T(8,128)(2,1)S(1)} %slice.226), channel_id=1, source_target_pairs={{0,96},{1,25},{2,98},{3,27},{4,100},{5,29},{6,102},{7,31},{8,104},... | collective-permute-start | bytes 589832 | tf_op jit(solution)/shard_map/ppermute | solution.py:36
  36.9 8.2 %collective-permute-start.2 = (bf16[16,6144]{1,0:T(8,128)(2,1)S(1)}, bf16[16,6144]{1,0:T(8,128)(2,1)S(1)}, u32[]{:S(2)}, u32[]{:S(2)}) collective-permute-start(bf16[16,6144]{1,0:T(8,128)(2,1)S(1)} %slice.225), channel_id=1, source_target_pairs={{0,32},{1,9},{2,34},{3,11},{4,36},{5,13},{6,38},{7,15},{8,40},{9,1... | collective-permute-start | bytes 589832 | tf_op jit(solution)/shard_map/ppermute | solution.py:36
  45.2 11.8 %collective-permute-start.5 = (bf16[64,6144]{1,0:T(8,128)(2,1)S(1)}, bf16[64,6144]{1,0:T(8,128)(2,1)S(1)}, u32[]{:S(2)}, u32[]{:S(2)}) collective-permute-start(bf16[64,6144]{1,0:T(8,128)(2,1)S(1)} %constant_dynamic-update-slice_fusion.refs_1_), channel_id=1, source_target_pairs={{0,24},{1,97},{2,26},{3,99},{4,28},{5,101},{6,30},{7,103},{8,0},{9... | collective-permute-start | bytes 2359304 | tf_op jit(solution)/shard_map/ppermute | solution.py:40
  47.9 12.3 %collective-permute-start.4 = (bf16[64,6144]{1,0:T(8,128)(2,1)S(1)}, bf16[64,6144]{1,0:T(8,128)(2,1)S(1)}, u32[]{:S(2)}, u32[]{:S(2)}) collective-permute-start(bf16[64,6144]{1,0:T(8,128)(2,1)S(1)} %constant_dynamic-update-slice_fusion.refs_1_), channel_id=1, source_target_pairs={{0,8},{1,33},{2,10},{3,35},{4,12},{5,37},{6,14},{7,39},{8,16},{9,4... | collective-permute-start | bytes 2359304 | tf_op jit(solution)/shard_map/ppermute | solution.py:40
  60.4 10.3 %collective-permute-start.11 = (bf16[32,6144]{1,0:T(8,128)(2,1)S(1)}, bf16[32,6144]{1,0:T(8,128)(2,1)S(1)}, u32[]{:S(2)}, u32[]{:S(2)}) collective-permute-start(bf16[32,6144]{1,0:T(8,128)(2,1)S(1)} %slice.205), channel_id=1, source_target_pairs={{0,24},{1,97},{2,26},{3,99},{4,28},{5,101},{6,30},{7,103},{8,0},{9... | collective-permute-start | bytes 1179656 | tf_op jit(solution)/shard_map/ppermute | solution.py:40
  60.4 10.2 %collective-permute-start.10 = (bf16[32,6144]{1,0:T(8,128)(2,1)S(1)}, bf16[32,6144]{1,0:T(8,128)(2,1)S(1)}, u32[]{:S(2)}, u32[]{:S(2)}) collective-permute-start(bf16[32,6144]{1,0:T(8,128)(2,1)S(1)} %slice.204), channel_id=1, source_target_pairs={{0,8},{1,33},{2,10},{3,35},{4,12},{5,37},{6,14},{7,39},{8,16},{9,4... | collective-permute-start | bytes 1179656 | tf_op jit(solution)/shard_map/ppermute | solution.py:40
  61.9 9.6 %collective-permute-start.9 = (bf16[32,6144]{1,0:T(8,128)(2,1)S(1)}, bf16[32,6144]{1,0:T(8,128)(2,1)S(1)}, u32[]{:S(2)}, u32[]{:S(2)}) collective-permute-start(bf16[32,6144]{1,0:T(8,128)(2,1)S(1)} %slice.228), channel_id=1, source_target_pairs={{0,24},{1,97},{2,26},{3,99},{4,28},{5,101},{6,30},{7,103},{8,0},{9... | collective-permute-start | bytes 1179656 | tf_op jit(solution)/shard_map/ppermute | solution.py:40
  63.3 9.5 %collective-permute-start.8 = (bf16[32,6144]{1,0:T(8,128)(2,1)S(1)}, bf16[32,6144]{1,0:T(8,128)(2,1)S(1)}, u32[]{:S(2)}, u32[]{:S(2)}) collective-permute-start(bf16[32,6144]{1,0:T(8,128)(2,1)S(1)} %slice.227), channel_id=1, source_target_pairs={{0,8},{1,33},{2,10},{3,35},{4,12},{5,37},{6,14},{7,39},{8,16},{9,4... | collective-permute-start | bytes 1179656 | tf_op jit(solution)/shard_map/ppermute | solution.py:40
  79.8 6.7 %collective-permute-start.15 = (bf16[32,6144]{1,0:T(8,128)(2,1)S(1)}, bf16[32,6144]{1,0:T(8,128)(2,1)S(1)}, u32[]{:S(2)}, u32[]{:S(2)}) collective-permute-start(bf16[32,6144]{1,0:T(8,128)(2,1)S(1)} %get-tuple-element.112), channel_id=1, source_target_pairs={{0,24},{1,97},{2,26},{3,99},{4,28},{5,101},{6,30},{7,103},{8,0},{9... | collective-permute-start | bytes 1179656 | tf_op jit(solution)/shard_map/ppermute | solution.py:40
  80.2 12.9 %collective-permute-start.12 = (bf16[32,6144]{1,0:T(8,128)(2,1)S(1)}, bf16[32,6144]{1,0:T(8,128)(2,1)S(1)}, u32[]{:S(2)}, u32[]{:S(2)}) collective-permute-start(bf16[32,6144]{1,0:T(8,128)(2,1)S(1)} %get-tuple-element.106), channel_id=1, source_target_pairs={{0,8},{1,33},{2,10},{3,35},{4,12},{5,37},{6,14},{7,39},{8,16},{9,4... | collective-permute-start | bytes 1179656 | tf_op jit(solution)/shard_map/ppermute | solution.py:40
  81.3 12.1 %collective-permute-start.13 = (bf16[32,6144]{1,0:T(8,128)(2,1)S(1)}, bf16[32,6144]{1,0:T(8,128)(2,1)S(1)}, u32[]{:S(2)}, u32[]{:S(2)}) collective-permute-start(bf16[32,6144]{1,0:T(8,128)(2,1)S(1)} %get-tuple-element.108), channel_id=1, source_target_pairs={{0,24},{1,97},{2,26},{3,99},{4,28},{5,101},{6,30},{7,103},{8,0},{9... | collective-permute-start | bytes 1179656 | tf_op jit(solution)/shard_map/ppermute | solution.py:40
  82.9 9.7 %collective-permute-start.14 = (bf16[32,6144]{1,0:T(8,128)(2,1)S(1)}, bf16[32,6144]{1,0:T(8,128)(2,1)S(1)}, u32[]{:S(2)}, u32[]{:S(2)}) collective-permute-start(bf16[32,6144]{1,0:T(8,128)(2,1)S(1)} %get-tuple-element.110), channel_id=1, source_target_pairs={{0,8},{1,33},{2,10},{3,35},{4,12},{5,37},{6,14},{7,39},{8,16},{9,4... | collective-permute-start | bytes 1179656 | tf_op jit(solution)/shard_map/ppermute | solution.py:40
  86.7 13.8 %collective-permute-start.19 = (bf16[64,6144]{1,0:T(8,128)(2,1)S(1)}, bf16[64,6144]{1,0:T(8,128)(2,1)S(1)}, u32[]{:S(2)}, u32[]{:S(2)}) collective-permute-start(bf16[64,6144]{1,0:T(8,128)(2,1)S(1)} %fusion.20), channel_id=1, source_target_pairs={{0,24},{1,97},{2,26},{3,99},{4,28},{5,101},{6,30},{7,103},{8,0},{9... | collective-permute-start | bytes 2359304 | tf_op jit(solution)/shard_map/ppermute | solution.py:40
  92.8 12.6 %collective-permute-start.18 = (bf16[64,6144]{1,0:T(8,128)(2,1)S(1)}, bf16[64,6144]{1,0:T(8,128)(2,1)S(1)}, u32[]{:S(2)}, u32[]{:S(2)}) collective-permute-start(bf16[64,6144]{1,0:T(8,128)(2,1)S(1)} %fusion.19), channel_id=1, source_target_pairs={{0,8},{1,33},{2,10},{3,35},{4,12},{5,37},{6,14},{7,39},{8,16},{9,4... | collective-permute-start | bytes 2359304 | tf_op jit(solution)/shard_map/ppermute | solution.py:40
  105.8 8.0 %collective-permute-start.20 = (bf16[16,6144]{1,0:T(8,128)(2,1)S(1)}, bf16[16,6144]{1,0:T(8,128)(2,1)S(1)}, u32[]{:S(2)}, u32[]{:S(2)}) collective-permute-start(bf16[16,6144]{1,0:T(8,128)(2,1)S(1)} %slice.232), channel_id=1, source_target_pairs={{0,32},{1,9},{2,34},{3,11},{4,36},{5,13},{6,38},{7,15},{8,40},{9,1... | collective-permute-start | bytes 589832 | tf_op jit(solution)/shard_map/ppermute | solution.py:36
  105.8 10.9 %collective-permute-start.17 = (bf16[64,6144]{1,0:T(8,128)(2,1)S(1)}, bf16[64,6144]{1,0:T(8,128)(2,1)S(1)}, u32[]{:S(2)}, u32[]{:S(2)}) collective-permute-start(bf16[64,6144]{1,0:T(8,128)(2,1)S(1)} %fusion.18), channel_id=1, source_target_pairs={{0,24},{1,97},{2,26},{3,99},{4,28},{5,101},{6,30},{7,103},{8,0},{9... | collective-permute-start | bytes 2359304 | tf_op jit(solution)/shard_map/ppermute | solution.py:40
  105.9 12.1 %collective-permute-start.16 = (bf16[64,6144]{1,0:T(8,128)(2,1)S(1)}, bf16[64,6144]{1,0:T(8,128)(2,1)S(1)}, u32[]{:S(2)}, u32[]{:S(2)}) collective-permute-start(bf16[64,6144]{1,0:T(8,128)(2,1)S(1)} %fusion.17), channel_id=1, source_target_pairs={{0,8},{1,33},{2,10},{3,35},{4,12},{5,37},{6,14},{7,39},{8,16},{9,4... | collective-permute-start | bytes 2359304 | tf_op jit(solution)/shard_map/ppermute | solution.py:40
  118.4 13.2 %collective-permute-start.21 = (bf16[32,6144]{1,0:T(8,128)(2,1)}, bf16[32,6144]{1,0:T(8,128)(2,1)}, u32[]{:S(2)}, u32[]{:S(2)}) collective-permute-start(bf16[32,6144]{1,0:T(8,128)(2,1)} %get-tuple-element.119), channel_id=1, source_target_pairs={{0,32},{1,9},{2,34},{3,11},{4,36},{5,13},{6,38},{7,15},{8,40},{9,1... | collective-permute-start | bytes 1179656 | tf_op jit(solution)/shard_map/ppermute | solution.py:36
  120.9 10.8 %collective-permute-start.23 = (bf16[32,6144]{1,0:T(8,128)(2,1)S(1)}, bf16[32,6144]{1,0:T(8,128)(2,1)}, u32[]{:S(2)}, u32[]{:S(2)}) collective-permute-start(bf16[32,6144]{1,0:T(8,128)(2,1)S(1)} %fusion.25), channel_id=1, source_target_pairs={{0,96},{1,25},{2,98},{3,27},{4,100},{5,29},{6,102},{7,31},{8,104},... | collective-permute-start | bytes 1179656 | tf_op jit(solution)/shard_map/ppermute | solution.py:36
  133.9 22.0 %all-to-all-start = ((bf16[32,1,8,768]{3,0,1,2:T(8,128)(2,1)}), bf16[32,1,8,768]{3,0,1,2:T(8,128)(2,1)S(1)}, u32[]{:S(2)}, u32[]{:S(2)}) async-start(bf16[32,1,8,768]{3,0,1,2:T(8,128)(2,1)} %copy.58), calls=%async_computation | async-start | bytes 786432 | tf_op jit(solution)/shard_map/all_to_all | solution.py:289
  (7 other events, 16.7 us)

commit v5 on v4

--- a/solution.py
+++ b/solution.py
@@ -53,29 +53,48 @@
 
 
 CHUNKS = 4
+LOAD_VMEM = 24 * 1024 * 1024
+FEED_VMEM = 28 * 1024 * 1024
+
+
+def load_kernel(*refs):
+    sources, targets, ready = refs[:3], refs[3:6], refs[6]
+    copies = []
+    for index, (source, target) in enumerate(zip(sources, targets)):
+        part = source.shape[1] // CHUNKS
+        for k in range(CHUNKS):
+            where = pl.ds(k * part, part)
+            copies.append(
+                pltpu.make_async_copy(
+                    source.at[:, where, :], target.at[:, where, :], ready.at[index, k]
+                )
+            )
+    for copy in copies:
+        copy.start()
+    for copy in copies:
+        copy.wait()
+
+
+def load(*arrays):
+    size = sum(array.size * 2 for array in arrays)
+    return pl.pallas_call(
+        load_kernel,
+        in_specs=[pl.BlockSpec(memory_space=pltpu.HBM)] * 3,
+        out_specs=[pl.BlockSpec(memory_space=pltpu.VMEM)] * 3,
+        out_shape=[jax.ShapeDtypeStruct(array.shape, array.dtype) for array in arrays],
+        scratch_shapes=[pltpu.SemaphoreType.DMA((3, CHUNKS))],
+        compiler_params=pltpu.CompilerParams(vmem_limit_bytes=LOAD_VMEM),
+        cost_estimate=pl.CostEstimate(flops=0, bytes_accessed=size, transcendentals=0),
+    )(*arrays)
 
 
 def feed_kernel(count, *refs):
     row_refs = refs[:count]
-    gate_hbm, up_hbm, down_hbm = refs[count : count + 3]
+    gate, up, down = refs[count : count + 3]
     out_refs = refs[count + 3 : 2 * count + 3]
-    rows, gate, up, down, ready = refs[2 * count + 3 :]
-    width, hidden = gate.shape
+    rows = refs[-1]
+    width, hidden = gate.shape[1:]
     depth = width // CHUNKS
-    copies = []
-    for k in range(CHUNKS):
-        part = pl.ds(k * depth, depth)
-        copies.append(
-            pltpu.make_async_copy(gate_hbm.at[0, part, :], gate.at[part, :], ready.at[0, k])
-        )
-        copies.append(pltpu.make_async_copy(up_hbm.at[0, part, :], up.at[part, :], ready.at[1, k]))
-    for k in range(CHUNKS):
-        part = pl.ds(k * depth, depth)
-        copies.append(
-            pltpu.make_async_copy(down_hbm.at[0, :, part], down.at[:, part], ready.at[2, k])
-        )
-    for copy in copies:
-        copy.start()
     at = 0
     for ref in row_refs:
         rows[at : at + ref.shape[0], :] = ref[...]
@@ -84,19 +103,16 @@
     up_sum = jnp.zeros((rows.shape[0], hidden), jnp.float32)
     for k in range(CHUNKS):
         part = rows[:, k * depth : (k + 1) * depth]
-        copies[2 * k].wait()
         gate_sum += jnp.dot(
-            part, gate[k * depth : (k + 1) * depth, :], preferred_element_type=jnp.float32
+            part, gate[0, k * depth : (k + 1) * depth, :], preferred_element_type=jnp.float32
         )
-        copies[2 * k + 1].wait()
         up_sum += jnp.dot(
-            part, up[k * depth : (k + 1) * depth, :], preferred_element_type=jnp.float32
+            part, up[0, k * depth : (k + 1) * depth, :], preferred_element_type=jnp.float32
         )
     active = (jax.nn.silu(gate_sum) * up_sum).astype(jnp.bfloat16)
     for k in range(CHUNKS):
-        copies[2 * CHUNKS + k].wait()
         partial = jnp.dot(
-            active, down[:, k * depth : (k + 1) * depth], preferred_element_type=jnp.float32
+            active, down[0, :, k * depth : (k + 1) * depth], preferred_element_type=jnp.float32
         ).astype(jnp.bfloat16)
         at = 0
         for ref in out_refs:
@@ -109,21 +125,14 @@
     width, hidden = w_gate.shape[1:]
     return pl.pallas_call(
         functools.partial(feed_kernel, len(row_arrays)),
-        in_specs=[pl.BlockSpec(memory_space=pltpu.VMEM)] * len(row_arrays)
-        + [pl.BlockSpec(memory_space=pltpu.HBM)] * 3,
+        in_specs=[pl.BlockSpec(memory_space=pltpu.VMEM)] * (len(row_arrays) + 3),
         out_specs=[pl.BlockSpec(memory_space=pltpu.VMEM)] * len(row_arrays),
         out_shape=[jax.ShapeDtypeStruct(array.shape, jnp.bfloat16) for array in row_arrays],
-        scratch_shapes=[
-            pltpu.VMEM((count, width), jnp.bfloat16),
-            pltpu.VMEM((width, hidden), jnp.bfloat16),
-            pltpu.VMEM((width, hidden), jnp.bfloat16),
-            pltpu.VMEM((hidden, width), jnp.bfloat16),
-            pltpu.SemaphoreType.DMA((3, CHUNKS)),
-        ],
-        compiler_params=pltpu.CompilerParams(vmem_limit_bytes=46 * 1024 * 1024),
+        scratch_shapes=[pltpu.VMEM((count, width), jnp.bfloat16)],
+        compiler_params=pltpu.CompilerParams(vmem_limit_bytes=FEED_VMEM),
         cost_estimate=pl.CostEstimate(
             flops=6 * count * width * hidden,
-            bytes_accessed=6 * width * hidden + 4 * count * width,
+            bytes_accessed=4 * count * width,
             transcendentals=count * hidden,
         ),
     )(*row_arrays, w_gate, w_up, w_down)
@@ -251,9 +260,11 @@
     )
     outgoing = (outgoing * own_scale).astype(jnp.bfloat16)
 
-    weights = (w_gate, w_up, w_down)
     near_up, near_down = spread_near(outgoing, shift_first)
+    weights = load(w_gate, w_up, w_down)
+    near_up, near_down, weights = lax.optimization_barrier((near_up, near_down, weights))
     far_low, far_high = spread_far(near_up, near_down, shift_first)
+    outgoing, far_low, far_high = lax.optimization_barrier((outgoing, far_low, far_high))
     one = jnp.concatenate([outgoing, near_up], axis=0)
     two = jnp.concatenate([near_down, far_low, far_high], axis=0)
     one_near = spread_near(one, shift_second)
@@ -262,6 +273,7 @@
     one_near_part = feed(one_near, *weights)
     two_near, one_near_part = lax.optimization_barrier((two_near, one_near_part))
     two_far = spread_far(*two_near, shift_second)
+    two_near, one_far = lax.optimization_barrier((two_near, one_far))
     two_near_part = feed(two_near, *weights)
     two_far, two_near_part = lax.optimization_barrier((two_far, two_near_part))
     far_part = feed([*one_far, *two_far], *weights)

time: 157 us -> 153 us (0.975)
  Pallas kernels: 27.7 us -> 16.1 us
  waiting for transfers between devices: 61.3 us -> 67.5 us
  starting transfers between devices: 37.4 us -> 39.6 us
    pallas_call x4, Pallas kernels: 27.7 us -> 10.9 us  [feed(): pl.pallas_call(functools.partial(feed_kernel, len(row_arrays)), in_specs=...]
    ppermute x16, waiting for transfers between devices: 23.7 us -> 36.3 us  [shift_second(): return lax.ppermute(value, ('attn', 'expert'), ring_pairs(step, True))]
    ppermute x8, waiting for transfers between devices: 29.6 us -> 23.2 us  [shift_first(): return lax.ppermute(value, ('attn', 'expert'), ring_pairs(step, False))]
    pallas_call x0 -> x1, Pallas kernels: none -> 5.15 us  [load(): pl.pallas_call(load_kernel, in_specs=[pl.BlockSpec(memory_space=pltpu.HBM...]
  transfers between devices with their start and end apart: 25 -> 25, of which waited for: 16 -> 19; matrix products, arithmetic and copies ran while one was open for 2% -> 1% of each run, Pallas kernels for 13% -> 9%
where the time goes in v5:
time: 153 us; the launch traced here: 152 us
  waiting for transfers between devices  67.5 us (44%)
  starting transfers between devices  39.6 us (26%)
  Pallas kernels  16.1 us (11%)
  blocking collectives  15.5 us (10%)
  other arithmetic  6.38 us (4%)
  matrix products  3.86 us (3%)
  local copies, waits for them, and re-layouts  3.05 us (2%)
    ppermute x16, waiting for transfers between devices, shift_second(): return lax.ppermute(value, ('attn', 'expert'), ring_pairs(step, True))  36.3 us
    ppermute x8, waiting for transfers between devices, shift_first(): return lax.ppermute(value, ('attn', 'expert'), ring_pairs(step, False))  23.2 us
    ppermute x16, starting transfers between devices, shift_second(): return lax.ppermute(value, ('attn', 'expert'), ring_pairs(step, True))  17.7 us
    all_gather x1, blocking collectives, on_device(): gathered = lax.all_gather(payload, 'expert', axis=0)  15.5 us
    all_to_all x1, starting transfers between devices, on_device(): lax.all_to_all(expert_result, 'expert', split_axis=2, concat_axis=1, tile...  13.7 us
    pallas_call x4, Pallas kernels, feed(): pl.pallas_call(functools.partial(feed_kernel, len(row_arrays)), in_specs=...  10.9 us
    ppermute x8, starting transfers between devices, shift_first(): return lax.ppermute(value, ('attn', 'expert'), ring_pairs(step, False))  8.14 us
    all_to_all x1, waiting for transfers between devices, on_device(): lax.all_to_all(expert_result, 'expert', split_axis=2, concat_axis=1, tile...  8.04 us
  transfers between devices with their start and end apart: 25, of which 19 were waited for; matrix products, arithmetic and copies ran while one was open for 1% of the time, Pallas kernels for 9%

profile of v5, /device:TPU:1, one launch (start us, length us, event | category | flops | bytes accessed | tf_op | source)
XLA Modules:
  0.0 152.4 jit_solution(1680785049799637337)
XLA Ops:
  7.1 15.5 %all-gather = bf16[512,896]{1,0:T(8,128)(2,1)S(1)} all-gather(bf16[64,896]{1,0:T(8,128)(2,1)S(1)} %concatenate.25), channel_id=2, replica_groups=mesh['attn'=16,'expert'=8] {'expert'}, dimensions={0}, use_global_device_ids=true | all-gather | bytes 1032192 | tf_op jit(solution)/shard_map/all_gather | solution.py:230
  26.1 5.2 %shard_map.127 = (bf16[1,6144,512]{2,1,0:T(8,128)(2,1)S(1)}, bf16[1,6144,512]{2,1,0:T(8,128)(2,1)S(1)}, bf16[1,512,6144]{2,1,0:T(8,128)(2,1)S(1)}) custom-call(bf16[1,6144,512]{2,1,0:T(8,128)(2,1)S(1)} %copy-done.2, bf16[1,6144,512]{2,1,0:T(8,128)(2,1)} %refs_1_.1, bf16[1,512,6144]{2,1,0:T(8,128)(2,1)} %refs_2_.1), custom_call_target="tpu_custom_call" | custom-call | bytes 18874368 | tf_op jit(solution)/shard_map/pallas_call | solution.py:80
  31.2 3.0 %collective-permute-done = bf16[32,6144]{1,0:T(8,128)(2,1)S(1)} collective-permute-done((bf16[32,6144]{1,0:T(8,128)(2,1)S(1)}, bf16[32,6144]{1,0:T(8,128)(2,1)S(1)}, u32[]{:S(2)}, u32[]{:S(2)}) %collective-permute-start) | collective-permute-done | bytes 393248 | tf_op jit(solution)/shard_map/ppermute | solution.py:36
  35.8 3.0 %collective-permute-done.3 = bf16[16,6144]{1,0:T(8,128)(2,1)S(1)} collective-permute-done((bf16[16,6144]{1,0:T(8,128)(2,1)S(1)}, bf16[16,6144]{1,0:T(8,128)(2,1)S(1)}, u32[]{:S(2)}, u32[]{:S(2)}) %collective-permute-start.3) | collective-permute-done | bytes 196640 | tf_op jit(solution)/shard_map/ppermute | solution.py:36
  40.2 3.7 %collective-permute-start.7 = (bf16[64,6144]{1,0:T(8,128)(2,1)S(1)}, bf16[64,6144]{1,0:T(8,128)(2,1)S(1)}, u32[]{:S(2)}, u32[]{:S(2)}) collective-permute-start(bf16[64,6144]{1,0:T(8,128)(2,1)S(1)} %constant_dynamic-update-slice_fusion.refs_0_), channel_id=1, source_target_pairs={{0,24},{1,97},{2,26},{3,99},{4,28},{5,101},{6,30},{7,103},{8,0},{9... | collective-permute-start | bytes 2359304 | tf_op jit(solution)/shard_map/ppermute | solution.py:40
  44.0 2.7 %collective-permute-start.5 = (bf16[64,6144]{1,0:T(8,128)(2,1)S(1)}, bf16[64,6144]{1,0:T(8,128)(2,1)S(1)}, u32[]{:S(2)}, u32[]{:S(2)}) collective-permute-start(bf16[64,6144]{1,0:T(8,128)(2,1)S(1)} %constant_dynamic-update-slice_fusion.2.refs_1_), channel_id=1, source_target_pairs={{0,24},{1,97},{2,26},{3,99},{4,28},{5,101},{6,30},{7,103},{8,0},{9... | collective-permute-start | bytes 2359304 | tf_op jit(solution)/shard_map/ppermute | solution.py:40
  46.7 6.1 %collective-permute-done.7.refs_1_ = bf16[64,6144]{1,0:T(8,128)(2,1)S(1)} collective-permute-done((bf16[64,6144]{1,0:T(8,128)(2,1)S(1)}, bf16[64,6144]{1,0:T(8,128)(2,1)S(1)}, u32[]{:S(2)}, u32[]{:S(2)}) %collective-permute-start.7) | collective-permute-done | bytes 786464 | tf_op jit(solution)/shard_map/ppermute | solution.py:40
  52.9 3.5 %collective-permute-start.9 = (bf16[32,6144]{1,0:T(8,128)(2,1)S(1)}, bf16[32,6144]{1,0:T(8,128)(2,1)S(1)}, u32[]{:S(2)}, u32[]{:S(2)}) collective-permute-start(bf16[32,6144]{1,0:T(8,128)(2,1)S(1)} %slice.226), channel_id=1, source_target_pairs={{0,24},{1,97},{2,26},{3,99},{4,28},{5,101},{6,30},{7,103},{8,0},{9... | collective-permute-start | bytes 1179656 | tf_op jit(solution)/shard_map/ppermute | solution.py:40
  56.5 2.7 %shard_map.128 = (bf16[64,6144]{1,0:T(8,128)(2,1)S(1)}, bf16[64,6144]{1,0:T(8,128)(2,1)S(1)}) custom-call(bf16[64,6144]{1,0:T(8,128)(2,1)S(1)} %collective-permute-done.6.refs_0_, bf16[64,6144]{1,0:T(8,128)(2,1)S(1)} %collective-permute-done.7.refs_1_, bf16[1,6144,512]{2,1,0:T(8,128)(2,1)S(1)} %get-tuple-element.120.refs_2_.refs_4_, ...), custom_call_target="tpu_custom_call" | custom-call | flops 2415919104 | bytes 3145728 | tf_op jit(solution)/shard_map/pallas_call | solution.py:126
  61.3 3.4 %collective-permute-done.4.refs_0_ = bf16[64,6144]{1,0:T(8,128)(2,1)S(1)} collective-permute-done((bf16[64,6144]{1,0:T(8,128)(2,1)S(1)}, bf16[64,6144]{1,0:T(8,128)(2,1)S(1)}, u32[]{:S(2)}, u32[]{:S(2)}) %collective-permute-start.4) | collective-permute-done | bytes 786464 | tf_op jit(solution)/shard_map/ppermute | solution.py:40
  66.3 2.6 %collective-permute-done.8.refs_0_ = bf16[32,6144]{1,0:T(8,128)(2,1)S(1)} collective-permute-done((bf16[32,6144]{1,0:T(8,128)(2,1)S(1)}, bf16[32,6144]{1,0:T(8,128)(2,1)S(1)}, u32[]{:S(2)}, u32[]{:S(2)}) %collective-permute-start.8) | collective-permute-done | bytes 393248 | tf_op jit(solution)/shard_map/ppermute | solution.py:40
  68.9 2.7 %shard_map.129 = (bf16[64,6144]{1,0:T(8,128)(2,1)S(1)}, bf16[64,6144]{1,0:T(8,128)(2,1)S(1)}) custom-call(bf16[64,6144]{1,0:T(8,128)(2,1)S(1)} %collective-permute-done.4.refs_0_, bf16[64,6144]{1,0:T(8,128)(2,1)S(1)} %collective-permute-done.5.refs_1_, bf16[1,6144,512]{2,1,0:T(8,128)(2,1)S(1)} %get-tuple-element.120.refs_2_.refs_4_, ...), custom_call_target="tpu_custom_call" | custom-call | flops 2415919104 | bytes 3145728 | tf_op jit(solution)/shard_map/pallas_call | solution.py:126
  72.9 2.7 %shard_map.130 = (bf16[32,6144]{1,0:T(8,128)(2,1)S(1)}, bf16[32,6144]{1,0:T(8,128)(2,1)S(1)}, bf16[32,6144]{1,0:T(8,128)(2,1)S(1)}, bf16[32,6144]{1,0:T(8,128)(2,1)S(1)}) custom-call(bf16[32,6144]{1,0:T(8,128)(2,1)S(1)} %collective-permute-done.8.refs_0_, bf16[32,6144]{1,0:T(8,128)(2,1)S(1)} %collective-permute-done.9.refs_1_, ...), custom_call_target="tpu_custom_call" | custom-call | flops 2415919104 | bytes 3145728 | tf_op jit(solution)/shard_map/pallas_call | solution.py:126
  78.7 3.7 %collective-permute-done.15 = bf16[32,6144]{1,0:T(8,128)(2,1)S(1)} collective-permute-done((bf16[32,6144]{1,0:T(8,128)(2,1)S(1)}, bf16[32,6144]{1,0:T(8,128)(2,1)S(1)}, u32[]{:S(2)}, u32[]{:S(2)}) %collective-permute-start.15) | collective-permute-done | bytes 393248 | tf_op jit(solution)/shard_map/ppermute | solution.py:40
  84.1 4.2 %collective-permute-done.14 = bf16[32,6144]{1,0:T(8,128)(2,1)S(1)} collective-permute-done((bf16[32,6144]{1,0:T(8,128)(2,1)S(1)}, bf16[32,6144]{1,0:T(8,128)(2,1)S(1)}, u32[]{:S(2)}, u32[]{:S(2)}) %collective-permute-start.14) | collective-permute-done | bytes 393248 | tf_op jit(solution)/shard_map/ppermute | solution.py:40
  89.2 2.7 %shard_map.131 = (bf16[64,6144]{1,0:T(8,128)(2,1)S(1)}, bf16[64,6144]{1,0:T(8,128)(2,1)S(1)}) custom-call(bf16[64,6144]{1,0:T(8,128)(2,1)S(1)} %constant_dynamic-update-slice_fusion.refs_0_, bf16[64,6144]{1,0:T(8,128)(2,1)S(1)} %constant_dynamic-update-slice_fusion.2.refs_1_, bf16[1,6144,512]{2,1,0:T(8,128)(2,1)S(1)} %get-tuple-element.120.refs_2_.refs_4_, ...), custom_call_target="tpu_custom_call" | custom-call | flops 2415919104 | bytes 3145728 | tf_op jit(solution)/shard_map/pallas_call | solution.py:126
  92.0 3.3 %collective-permute-done.19 = bf16[64,6144]{1,0:T(8,128)(2,1)S(1)} collective-permute-done((bf16[64,6144]{1,0:T(8,128)(2,1)S(1)}, bf16[64,6144]{1,0:T(8,128)(2,1)S(1)}, u32[]{:S(2)}, u32[]{:S(2)}) %collective-permute-start.19) | collective-permute-done | bytes 786464 | tf_op jit(solution)/shard_map/ppermute | solution.py:40
  95.3 5.7 %collective-permute-done.18 = bf16[64,6144]{1,0:T(8,128)(2,1)S(1)} collective-permute-done((bf16[64,6144]{1,0:T(8,128)(2,1)S(1)}, bf16[64,6144]{1,0:T(8,128)(2,1)S(1)}, u32[]{:S(2)}, u32[]{:S(2)}) %collective-permute-start.18) | collective-permute-done | bytes 786464 | tf_op jit(solution)/shard_map/ppermute | solution.py:40
  102.9 6.6 %collective-permute-done.20 = bf16[16,6144]{1,0:T(8,128)(2,1)S(1)} collective-permute-done((bf16[16,6144]{1,0:T(8,128)(2,1)S(1)}, bf16[16,6144]{1,0:T(8,128)(2,1)S(1)}, u32[]{:S(2)}, u32[]{:S(2)}) %collective-permute-start.20) | collective-permute-done | bytes 196640 | tf_op jit(solution)/shard_map/ppermute | solution.py:36
  109.7 2.6 %collective-permute-done.17 = bf16[64,6144]{1,0:T(8,128)(2,1)S(1)} collective-permute-done((bf16[64,6144]{1,0:T(8,128)(2,1)S(1)}, bf16[64,6144]{1,0:T(8,128)(2,1)S(1)}, u32[]{:S(2)}, u32[]{:S(2)}) %collective-permute-start.17) | collective-permute-done | bytes 786464 | tf_op jit(solution)/shard_map/ppermute | solution.py:40
  115.2 3.8 %collective-permute-start.23 = (bf16[32,6144]{1,0:T(8,128)(2,1)S(1)}, bf16[32,6144]{1,0:T(8,128)(2,1)}, u32[]{:S(2)}, u32[]{:S(2)}) collective-permute-start(bf16[32,6144]{1,0:T(8,128)(2,1)S(1)} %fusion.25), channel_id=1, source_target_pairs={{0,96},{1,25},{2,98},{3,27},{4,100},{5,29},{6,102},{7,31},{8,104},... | collective-permute-start | bytes 1179656 | tf_op jit(solution)/shard_map/ppermute | solution.py:36
  119.1 8.2 %collective-permute-done.21 = bf16[32,6144]{1,0:T(8,128)(2,1)S(1)} collective-permute-done((bf16[32,6144]{1,0:T(8,128)(2,1)S(1)}, bf16[32,6144]{1,0:T(8,128)(2,1)S(1)}, u32[]{:S(2)}, u32[]{:S(2)}) %collective-permute-start.21) | collective-permute-done | bytes 393248 | tf_op jit(solution)/shard_map/ppermute | solution.py:36
  129.5 13.7 %all-to-all-start = ((bf16[32,1,8,768]{3,0,1,2:T(8,128)(2,1)}), bf16[32,1,8,768]{3,0,1,2:T(8,128)(2,1)S(1)}, u32[]{:S(2)}, u32[]{:S(2)}) async-start(bf16[32,1,8,768]{3,0,1,2:T(8,128)(2,1)} %copy.58), calls=%async_computation | async-start | bytes 786432 | tf_op jit(solution)/shard_map/all_to_all | solution.py:301
  143.3 8.0 %all-to-all-done = bf16[32,1,8,768]{3,0,1,2:T(8,128)(2,1)S(1)} async-done(((bf16[32,1,8,768]{3,0,1,2:T(8,128)(2,1)}), bf16[32,1,8,768]{3,0,1,2:T(8,128)(2,1)S(1)}, u32[]{:S(2)}, u32[]{:S(2)}) %all-to-all-start) | async-done | bytes 393248 | tf_op jit(solution)/shard_map/all_to_all | solution.py:301
  (112 shorter events, 32.4 us)
Async XLA Ops:
  23.5 7.7 %collective-permute-start.1 = (bf16[32,6144]{1,0:T(8,128)(2,1)S(1)}, bf16[32,6144]{1,0:T(8,128)(2,1)S(1)}, u32[]{:S(2)}, u32[]{:S(2)}) collective-permute-start(bf16[32,6144]{1,0:T(8,128)(2,1)S(1)} %multiply_convert_fusion), channel_id=1, source_target_pairs={{0,96},{1,25},{2,98},{3,27},{4,100},{5,29},{6,102},{7,31},{8,104},... | collective-permute-start | bytes 1179656 | tf_op jit(solution)/shard_map/ppermute | solution.py:36
  26.1 8.1 %collective-permute-start = (bf16[32,6144]{1,0:T(8,128)(2,1)S(1)}, bf16[32,6144]{1,0:T(8,128)(2,1)S(1)}, u32[]{:S(2)}, u32[]{:S(2)}) collective-permute-start(bf16[32,6144]{1,0:T(8,128)(2,1)S(1)} %multiply_convert_fusion), channel_id=1, source_target_pairs={{0,32},{1,9},{2,34},{3,11},{4,36},{5,13},{6,38},{7,15},{8,40},{9,1... | collective-permute-start | bytes 1179656 | tf_op jit(solution)/shard_map/ppermute | solution.py:36
  34.3 5.8 %collective-permute-start.2 = (bf16[16,6144]{1,0:T(8,128)(2,1)S(1)}, bf16[16,6144]{1,0:T(8,128)(2,1)S(1)}, u32[]{:S(2)}, u32[]{:S(2)}) collective-permute-start(bf16[16,6144]{1,0:T(8,128)(2,1)S(1)} %slice.199), channel_id=1, source_target_pairs={{0,32},{1,9},{2,34},{3,11},{4,36},{5,13},{6,38},{7,15},{8,40},{9,1... | collective-permute-start | bytes 589832 | tf_op jit(solution)/shard_map/ppermute | solution.py:36
  40.2 12.7 %collective-permute-start.7 = (bf16[64,6144]{1,0:T(8,128)(2,1)S(1)}, bf16[64,6144]{1,0:T(8,128)(2,1)S(1)}, u32[]{:S(2)}, u32[]{:S(2)}) collective-permute-start(bf16[64,6144]{1,0:T(8,128)(2,1)S(1)} %constant_dynamic-update-slice_fusion.refs_0_), channel_id=1, source_target_pairs={{0,24},{1,97},{2,26},{3,99},{4,28},{5,101},{6,30},{7,103},{8,0},{9... | collective-permute-start | bytes 2359304 | tf_op jit(solution)/shard_map/ppermute | solution.py:40
  43.9 12.4 %collective-permute-start.6 = (bf16[64,6144]{1,0:T(8,128)(2,1)S(1)}, bf16[64,6144]{1,0:T(8,128)(2,1)S(1)}, u32[]{:S(2)}, u32[]{:S(2)}) collective-permute-start(bf16[64,6144]{1,0:T(8,128)(2,1)S(1)} %constant_dynamic-update-slice_fusion.refs_0_), channel_id=1, source_target_pairs={{0,8},{1,33},{2,10},{3,35},{4,12},{5,37},{6,14},{7,39},{8,16},{9,4... | collective-permute-start | bytes 2359304 | tf_op jit(solution)/shard_map/ppermute | solution.py:40
  44.0 17.3 %collective-permute-start.5 = (bf16[64,6144]{1,0:T(8,128)(2,1)S(1)}, bf16[64,6144]{1,0:T(8,128)(2,1)S(1)}, u32[]{:S(2)}, u32[]{:S(2)}) collective-permute-start(bf16[64,6144]{1,0:T(8,128)(2,1)S(1)} %constant_dynamic-update-slice_fusion.2.refs_1_), channel_id=1, source_target_pairs={{0,24},{1,97},{2,26},{3,99},{4,28},{5,101},{6,30},{7,103},{8,0},{9... | collective-permute-start | bytes 2359304 | tf_op jit(solution)/shard_map/ppermute | solution.py:40
  46.7 18.0 %collective-permute-start.4 = (bf16[64,6144]{1,0:T(8,128)(2,1)S(1)}, bf16[64,6144]{1,0:T(8,128)(2,1)S(1)}, u32[]{:S(2)}, u32[]{:S(2)}) collective-permute-start(bf16[64,6144]{1,0:T(8,128)(2,1)S(1)} %constant_dynamic-update-slice_fusion.2.refs_1_), channel_id=1, source_target_pairs={{0,8},{1,33},{2,10},{3,35},{4,12},{5,37},{6,14},{7,39},{8,16},{9,4... | collective-permute-start | bytes 2359304 | tf_op jit(solution)/shard_map/ppermute | solution.py:40
  52.9 13.4 %collective-permute-start.9 = (bf16[32,6144]{1,0:T(8,128)(2,1)S(1)}, bf16[32,6144]{1,0:T(8,128)(2,1)S(1)}, u32[]{:S(2)}, u32[]{:S(2)}) collective-permute-start(bf16[32,6144]{1,0:T(8,128)(2,1)S(1)} %slice.226), channel_id=1, source_target_pairs={{0,24},{1,97},{2,26},{3,99},{4,28},{5,101},{6,30},{7,103},{8,0},{9... | collective-permute-start | bytes 1179656 | tf_op jit(solution)/shard_map/ppermute | solution.py:40
  56.4 12.5 %collective-permute-start.8 = (bf16[32,6144]{1,0:T(8,128)(2,1)S(1)}, bf16[32,6144]{1,0:T(8,128)(2,1)S(1)}, u32[]{:S(2)}, u32[]{:S(2)}) collective-permute-start(bf16[32,6144]{1,0:T(8,128)(2,1)S(1)} %slice.225), channel_id=1, source_target_pairs={{0,8},{1,33},{2,10},{3,35},{4,12},{5,37},{6,14},{7,39},{8,16},{9,4... | collective-permute-start | bytes 1179656 | tf_op jit(solution)/shard_map/ppermute | solution.py:40
  64.8 7.0 %collective-permute-start.11 = (bf16[32,6144]{1,0:T(8,128)(2,1)S(1)}, bf16[32,6144]{1,0:T(8,128)(2,1)S(1)}, u32[]{:S(2)}, u32[]{:S(2)}) collective-permute-start(bf16[32,6144]{1,0:T(8,128)(2,1)S(1)} %slice.205), channel_id=1, source_target_pairs={{0,24},{1,97},{2,26},{3,99},{4,28},{5,101},{6,30},{7,103},{8,0},{9... | collective-permute-start | bytes 1179656 | tf_op jit(solution)/shard_map/ppermute | solution.py:40
  64.8 8.1 %collective-permute-start.10 = (bf16[32,6144]{1,0:T(8,128)(2,1)S(1)}, bf16[32,6144]{1,0:T(8,128)(2,1)S(1)}, u32[]{:S(2)}, u32[]{:S(2)}) collective-permute-start(bf16[32,6144]{1,0:T(8,128)(2,1)S(1)} %slice.204), channel_id=1, source_target_pairs={{0,8},{1,33},{2,10},{3,35},{4,12},{5,37},{6,14},{7,39},{8,16},{9,4... | collective-permute-start | bytes 1179656 | tf_op jit(solution)/shard_map/ppermute | solution.py:40
  75.7 6.7 %collective-permute-start.15 = (bf16[32,6144]{1,0:T(8,128)(2,1)S(1)}, bf16[32,6144]{1,0:T(8,128)(2,1)S(1)}, u32[]{:S(2)}, u32[]{:S(2)}) collective-permute-start(bf16[32,6144]{1,0:T(8,128)(2,1)S(1)} %get-tuple-element.142), channel_id=1, source_target_pairs={{0,24},{1,97},{2,26},{3,99},{4,28},{5,101},{6,30},{7,103},{8,0},{9... | collective-permute-start | bytes 1179656 | tf_op jit(solution)/shard_map/ppermute | solution.py:40
  75.9 12.7 %collective-permute-start.12 = (bf16[32,6144]{1,0:T(8,128)(2,1)S(1)}, bf16[32,6144]{1,0:T(8,128)(2,1)S(1)}, u32[]{:S(2)}, u32[]{:S(2)}) collective-permute-start(bf16[32,6144]{1,0:T(8,128)(2,1)S(1)} %get-tuple-element.136), channel_id=1, source_target_pairs={{0,8},{1,33},{2,10},{3,35},{4,12},{5,37},{6,14},{7,39},{8,16},{9,4... | collective-permute-start | bytes 1179656 | tf_op jit(solution)/shard_map/ppermute | solution.py:40
  77.2 11.7 %collective-permute-start.13 = (bf16[32,6144]{1,0:T(8,128)(2,1)S(1)}, bf16[32,6144]{1,0:T(8,128)(2,1)S(1)}, u32[]{:S(2)}, u32[]{:S(2)}) collective-permute-start(bf16[32,6144]{1,0:T(8,128)(2,1)S(1)} %get-tuple-element.138), channel_id=1, source_target_pairs={{0,24},{1,97},{2,26},{3,99},{4,28},{5,101},{6,30},{7,103},{8,0},{9... | collective-permute-start | bytes 1179656 | tf_op jit(solution)/shard_map/ppermute | solution.py:40
  78.6 9.7 %collective-permute-start.14 = (bf16[32,6144]{1,0:T(8,128)(2,1)S(1)}, bf16[32,6144]{1,0:T(8,128)(2,1)S(1)}, u32[]{:S(2)}, u32[]{:S(2)}) collective-permute-start(bf16[32,6144]{1,0:T(8,128)(2,1)S(1)} %get-tuple-element.140), channel_id=1, source_target_pairs={{0,8},{1,33},{2,10},{3,35},{4,12},{5,37},{6,14},{7,39},{8,16},{9,4... | collective-permute-start | bytes 1179656 | tf_op jit(solution)/shard_map/ppermute | solution.py:40
  82.6 12.7 %collective-permute-start.19 = (bf16[64,6144]{1,0:T(8,128)(2,1)S(1)}, bf16[64,6144]{1,0:T(8,128)(2,1)S(1)}, u32[]{:S(2)}, u32[]{:S(2)}) collective-permute-start(bf16[64,6144]{1,0:T(8,128)(2,1)S(1)} %fusion.20), channel_id=1, source_target_pairs={{0,24},{1,97},{2,26},{3,99},{4,28},{5,101},{6,30},{7,103},{8,0},{9... | collective-permute-start | bytes 2359304 | tf_op jit(solution)/shard_map/ppermute | solution.py:40
  88.5 12.4 %collective-permute-start.18 = (bf16[64,6144]{1,0:T(8,128)(2,1)S(1)}, bf16[64,6144]{1,0:T(8,128)(2,1)S(1)}, u32[]{:S(2)}, u32[]{:S(2)}) collective-permute-start(bf16[64,6144]{1,0:T(8,128)(2,1)S(1)} %fusion.19), channel_id=1, source_target_pairs={{0,8},{1,33},{2,10},{3,35},{4,12},{5,37},{6,14},{7,39},{8,16},{9,4... | collective-permute-start | bytes 2359304 | tf_op jit(solution)/shard_map/ppermute | solution.py:40
  101.3 8.3 %collective-permute-start.20 = (bf16[16,6144]{1,0:T(8,128)(2,1)S(1)}, bf16[16,6144]{1,0:T(8,128)(2,1)S(1)}, u32[]{:S(2)}, u32[]{:S(2)}) collective-permute-start(bf16[16,6144]{1,0:T(8,128)(2,1)S(1)} %slice.230), channel_id=1, source_target_pairs={{0,32},{1,9},{2,34},{3,11},{4,36},{5,13},{6,38},{7,15},{8,40},{9,1... | collective-permute-start | bytes 589832 | tf_op jit(solution)/shard_map/ppermute | solution.py:36
  101.3 10.9 %collective-permute-start.17 = (bf16[64,6144]{1,0:T(8,128)(2,1)S(1)}, bf16[64,6144]{1,0:T(8,128)(2,1)S(1)}, u32[]{:S(2)}, u32[]{:S(2)}) collective-permute-start(bf16[64,6144]{1,0:T(8,128)(2,1)S(1)} %fusion.18), channel_id=1, source_target_pairs={{0,24},{1,97},{2,26},{3,99},{4,28},{5,101},{6,30},{7,103},{8,0},{9... | collective-permute-start | bytes 2359304 | tf_op jit(solution)/shard_map/ppermute | solution.py:40
  101.4 12.1 %collective-permute-start.16 = (bf16[64,6144]{1,0:T(8,128)(2,1)S(1)}, bf16[64,6144]{1,0:T(8,128)(2,1)S(1)}, u32[]{:S(2)}, u32[]{:S(2)}) collective-permute-start(bf16[64,6144]{1,0:T(8,128)(2,1)S(1)} %fusion.17), channel_id=1, source_target_pairs={{0,8},{1,33},{2,10},{3,35},{4,12},{5,37},{6,14},{7,39},{8,16},{9,4... | collective-permute-start | bytes 2359304 | tf_op jit(solution)/shard_map/ppermute | solution.py:40
  109.6 5.5 %collective-permute-start.22 = (bf16[16,6144]{1,0:T(8,128)(2,1)S(1)}, bf16[16,6144]{1,0:T(8,128)(2,1)S(1)}, u32[]{:S(2)}, u32[]{:S(2)}) collective-permute-start(bf16[16,6144]{1,0:T(8,128)(2,1)S(1)} %get-tuple-element.150), channel_id=1, source_target_pairs={{0,96},{1,25},{2,98},{3,27},{4,100},{5,29},{6,102},{7,31},{8,104},... | collective-permute-start | bytes 589832 | tf_op jit(solution)/shard_map/ppermute | solution.py:36
  113.9 13.4 %collective-permute-start.21 = (bf16[32,6144]{1,0:T(8,128)(2,1)S(1)}, bf16[32,6144]{1,0:T(8,128)(2,1)S(1)}, u32[]{:S(2)}, u32[]{:S(2)}) collective-permute-start(bf16[32,6144]{1,0:T(8,128)(2,1)S(1)} %get-tuple-element.149), channel_id=1, source_target_pairs={{0,32},{1,9},{2,34},{3,11},{4,36},{5,13},{6,38},{7,15},{8,40},{9,1... | collective-permute-start | bytes 1179656 | tf_op jit(solution)/shard_map/ppermute | solution.py:36
  115.2 12.1 %collective-permute-start.23 = (bf16[32,6144]{1,0:T(8,128)(2,1)S(1)}, bf16[32,6144]{1,0:T(8,128)(2,1)}, u32[]{:S(2)}, u32[]{:S(2)}) collective-permute-start(bf16[32,6144]{1,0:T(8,128)(2,1)S(1)} %fusion.25), channel_id=1, source_target_pairs={{0,96},{1,25},{2,98},{3,27},{4,100},{5,29},{6,102},{7,31},{8,104},... | collective-permute-start | bytes 1179656 | tf_op jit(solution)/shard_map/ppermute | solution.py:36
  129.5 21.8 %all-to-all-start = ((bf16[32,1,8,768]{3,0,1,2:T(8,128)(2,1)}), bf16[32,1,8,768]{3,0,1,2:T(8,128)(2,1)S(1)}, u32[]{:S(2)}, u32[]{:S(2)}) async-start(bf16[32,1,8,768]{3,0,1,2:T(8,128)(2,1)} %copy.58), calls=%async_computation | async-start | bytes 786432 | tf_op jit(solution)/shard_map/all_to_all | solution.py:301
  (9 other events, 60.0 us)

commit v6 on v5

--- a/solution.py
+++ b/solution.py
@@ -15,6 +15,8 @@
 
 
 EPSILON = 1e-05
+CHAINS = 2
+CHAIN_ROWS = CAP // CHAINS
 
 
 def ring_pairs(step, second):
@@ -54,7 +56,7 @@
 
 CHUNKS = 4
 LOAD_VMEM = 24 * 1024 * 1024
-FEED_VMEM = 28 * 1024 * 1024
+FEED_VMEM = 16 * 1024 * 1024
 
 
 def load_kernel(*refs):
@@ -260,42 +262,39 @@
     )
     outgoing = (outgoing * own_scale).astype(jnp.bfloat16)
 
-    near_up, near_down = spread_near(outgoing, shift_first)
-    weights = load(w_gate, w_up, w_down)
-    near_up, near_down, weights = lax.optimization_barrier((near_up, near_down, weights))
-    far_low, far_high = spread_far(near_up, near_down, shift_first)
-    outgoing, far_low, far_high = lax.optimization_barrier((outgoing, far_low, far_high))
-    one = jnp.concatenate([outgoing, near_up], axis=0)
-    two = jnp.concatenate([near_down, far_low, far_high], axis=0)
-    one_near = spread_near(one, shift_second)
-    two_near = spread_near(two, shift_second)
-    one_far = spread_far(*one_near, shift_second)
-    one_near_part = feed(one_near, *weights)
-    two_near, one_near_part = lax.optimization_barrier((two_near, one_near_part))
-    two_far = spread_far(*two_near, shift_second)
-    two_near, one_far = lax.optimization_barrier((two_near, one_far))
-    two_near_part = feed(two_near, *weights)
-    two_far, two_near_part = lax.optimization_barrier((two_far, two_near_part))
-    far_part = feed([*one_far, *two_far], *weights)
-
-    two_up, two_down = halves_added(
-        two_near_part[1], two_near_part[0], far_part[2], far_part[3], shift_second
-    )
-    one_up, one_down = halves_added(
-        one_near_part[1], one_near_part[0], far_part[0], far_part[1], shift_second
-    )
-    one, two = lax.optimization_barrier((one, two, one_up, one_down, two_up, two_down))[:2]
-    one_own, two_own = feed([one, two], *weights)
-    two_sum = add_three(two_own, shift_second(two_up, 1), shift_second(two_down, -1))
-    one_sum = add_three(one_own, shift_second(one_up, 1), shift_second(one_down, -1))
-    up, down = halves_added(
-        two_sum[:CAP],
-        one_sum[CAP:],
-        two_sum[CAP : CAP + CAP // 2],
-        two_sum[CAP + CAP // 2 :],
-        shift_first,
-    )
-    expert_result = add_three(one_sum[:CAP], shift_first(up, 1), shift_first(down, -1))
+    lines = []
+    for chain in range(CHAINS):
+        slab = outgoing[chain * CHAIN_ROWS : (chain + 1) * CHAIN_ROWS]
+        near = spread_near(slab, shift_first)
+        lines.append(jnp.concatenate([slab, *near, *spread_far(*near, shift_first)], axis=0))
+    weights = lax.optimization_barrier((w_gate, w_up, w_down, *lines))[:3]
+    weights = load(*weights)
+    own_parts = feed(lines, *weights)
+    nears = [spread_near(line, shift_second) for line in lines]
+    nears[0], own_parts = lax.optimization_barrier((nears[0], own_parts))
+    first_part = feed(nears[0], *weights)
+    nears[1], first_part = lax.optimization_barrier((nears[1], first_part))
+    fars = [spread_far(*near, shift_second) for near in nears]
+    nears[1], fars[0] = lax.optimization_barrier((nears[1], fars[0]))
+    near_parts = [first_part, feed(nears[1], *weights)]
+    fars, near_parts = lax.optimization_barrier((fars, near_parts))
+    far_part = feed([piece for far in fars for piece in far], *weights)
+
+    results = []
+    for chain in range(CHAINS):
+        behind, ahead = near_parts[chain]
+        far = far_part[2 * chain : 2 * chain + 2]
+        up, down = halves_added(ahead, behind, *far, shift_second)
+        line_sum = add_three(own_parts[chain], shift_second(up, 1), shift_second(down, -1))
+        behind = line_sum[CHAIN_ROWS : 2 * CHAIN_ROWS]
+        ahead = line_sum[2 * CHAIN_ROWS : 3 * CHAIN_ROWS]
+        middle = 3 * CHAIN_ROWS + CHAIN_ROWS // 2
+        far_low, far_high = line_sum[3 * CHAIN_ROWS : middle], line_sum[middle:]
+        up, down = halves_added(ahead, behind, far_low, far_high, shift_first)
+        results.append(
+            add_three(line_sum[:CHAIN_ROWS], shift_first(up, 1), shift_first(down, -1))
+        )
+    expert_result = jnp.concatenate(results, axis=0)
 
     expert_result = expert_result.reshape(CAP, 1, expert_devices, width_local)
     returned = lax.all_to_all(expert_result, "expert", split_axis=2, concat_axis=1, tiled=True)

time: 153 us -> 156 us (1.020)
  waiting for transfers between devices: 67.5 us -> 47.2 us
  starting transfers between devices: 39.6 us -> 54.1 us
  local copies, waits for them, and re-layouts: 3.05 us -> 9.08 us
  other arithmetic: 6.38 us -> 8.54 us
    ppermute x8 -> x16, waiting for transfers between devices: 23.2 us -> 9.64 us  [shift_first(): return lax.ppermute(value, ('attn', 'expert'), ring_pairs(step, False))]
    ppermute x8 -> x16, starting transfers between devices: 8.14 us -> 18.3 us  [shift_first(): return lax.ppermute(value, ('attn', 'expert'), ring_pairs(step, False))]
    ppermute x16, waiting for transfers between devices: 36.3 us -> 29.5 us  [shift_second(): return lax.ppermute(value, ('attn', 'expert'), ring_pairs(step, True))]
    unnamed x21 -> x36, local copies, waits for them, and re-layouts: 0.23 us -> 5.64 us
    all_to_all x1, starting transfers between devices: 13.7 us -> 17.9 us  [on_device(): lax.all_to_all(expert_result, 'expert', split_axis=2, concat_axis=1, tile...]
    scatter x3 -> x4, other arithmetic: 0.57 us -> 2.26 us  [halves_added(): down = behind.at[half:].set(add_rounded(behind[half:], got_high))]
    scatter x3 -> x4, other arithmetic: 0.57 us -> 2.14 us  [halves_added(): up = ahead.at[:half].set(add_rounded(ahead[:half], got_low))]
  transfers between devices with their start and end apart: 25 -> 33, of which waited for: 19 -> 16; matrix products, arithmetic and copies ran while one was open for 1% -> 4% of each run, Pallas kernels for 9% -> 9%
where the time goes in v6:
time: 156 us
  starting transfers between devices  54.1 us (35%)
  waiting for transfers between devices  47.2 us (30%)
  Pallas kernels  16.8 us (11%)
  blocking collectives  15.4 us (10%)
  local copies, waits for them, and re-layouts  9.08 us (6%)
  other arithmetic  8.54 us (5%)
  matrix products  3.86 us (2%)
    ppermute x16, waiting for transfers between devices, shift_second(): return lax.ppermute(value, ('attn', 'expert'), ring_pairs(step, True))  29.5 us
    ppermute x16, starting transfers between devices, shift_first(): return lax.ppermute(value, ('attn', 'expert'), ring_pairs(step, False))  18.3 us
    ppermute x16, starting transfers between devices, shift_second(): return lax.ppermute(value, ('attn', 'expert'), ring_pairs(step, True))  17.9 us
    all_to_all x1, starting transfers between devices, on_device(): lax.all_to_all(expert_result, 'expert', split_axis=2, concat_axis=1, tile...  17.9 us
    all_gather x1, blocking collectives, on_device(): gathered = lax.all_gather(payload, 'expert', axis=0)  15.4 us
    pallas_call x4, Pallas kernels, feed(): pl.pallas_call(functools.partial(feed_kernel, len(row_arrays)), in_specs=...  11.7 us
    ppermute x16, waiting for transfers between devices, shift_first(): return lax.ppermute(value, ('attn', 'expert'), ring_pairs(step, False))  9.64 us
    all_to_all x1, waiting for transfers between devices, on_device(): lax.all_to_all(expert_result, 'expert', split_axis=2, concat_axis=1, tile...  8.04 us
  transfers between devices with their start and end apart: 33, of which 16 were waited for; matrix products, arithmetic and copies ran while one was open for 4% of the time, Pallas kernels for 9%

profile of v6, /device:TPU:1, one launch (start us, length us, event | category | flops | bytes accessed | tf_op | source)
XLA Modules:
  0.0 155.6 jit_solution(1948056919739943786)
XLA Ops:
  7.4 15.4 %all-gather = bf16[512,896]{1,0:T(8,128)(2,1)S(1)} all-gather(bf16[64,896]{1,0:T(8,128)(2,1)S(1)} %concatenate.32), channel_id=2, replica_groups=mesh['attn'=16,'expert'=8] {'expert'}, dimensions={0}, use_global_device_ids=true | all-gather | bytes 1032192 | tf_op jit(solution)/shard_map/all_gather | solution.py:232
  23.8 2.5 %collective-permute-start.1 = (bf16[16,6144]{1,0:T(8,128)(2,1)S(1)}, bf16[16,6144]{1,0:T(8,128)(2,1)S(1)}, u32[]{:S(2)}, u32[]{:S(2)}) collective-permute-start(bf16[16,6144]{1,0:T(8,128)(2,1)S(1)} %get-tuple-element.183), channel_id=1, source_target_pairs={{0,96},{1,25},{2,98},{3,27},{4,100},{5,29},{6,102},{7,31},{8,104},... | collective-permute-start | bytes 589832 | tf_op jit(solution)/shard_map/ppermute | solution.py:38
  26.3 2.7 %collective-permute-start.7 = (bf16[16,6144]{1,0:T(8,128)(2,1)S(1)}, bf16[16,6144]{1,0:T(8,128)(2,1)S(1)}, u32[]{:S(2)}, u32[]{:S(2)}) collective-permute-start(bf16[16,6144]{1,0:T(8,128)(2,1)S(1)} %get-tuple-element.186), channel_id=1, source_target_pairs={{0,96},{1,25},{2,98},{3,27},{4,100},{5,29},{6,102},{7,31},{8,104},... | collective-permute-start | bytes 589832 | tf_op jit(solution)/shard_map/ppermute | solution.py:38
  29.0 3.1 %collective-permute-start.3 = (bf16[8,6144]{1,0:T(8,128)(2,1)S(1)}, bf16[8,6144]{1,0:T(8,128)(2,1)S(1)}, u32[]{:S(2)}, u32[]{:S(2)}) collective-permute-start(bf16[8,6144]{1,0:T(8,128)(2,1)S(1)} %slice.307), channel_id=1, source_target_pairs={{0,96},{1,25},{2,98},{3,27},{4,100},{5,29},{6,102},{7,31},{8,104},... | collective-permute-start | bytes 294920 | tf_op jit(solution)/shard_map/ppermute | solution.py:38
  32.3 2.8 %collective-permute-start.9 = (bf16[8,6144]{1,0:T(8,128)(2,1)S(1)}, bf16[8,6144]{1,0:T(8,128)(2,1)S(1)}, u32[]{:S(2)}, u32[]{:S(2)}) collective-permute-start(bf16[8,6144]{1,0:T(8,128)(2,1)S(1)} %slice.310), channel_id=1, source_target_pairs={{0,96},{1,25},{2,98},{3,27},{4,100},{5,29},{6,102},{7,31},{8,104},... | collective-permute-start | bytes 294920 | tf_op jit(solution)/shard_map/ppermute | solution.py:38
  37.2 3.8 %collective-permute-start.5 = (bf16[64,6144]{1,0:T(8,128)(2,1)S(1)}, bf16[64,6144]{1,0:T(8,128)(2,1)S(1)}, u32[]{:S(2)}, u32[]{:S(2)}) collective-permute-start(bf16[64,6144]{1,0:T(8,128)(2,1)S(1)} %constant_dynamic-update-slice_fusion.refs_0_), channel_id=1, source_target_pairs={{0,24},{1,97},{2,26},{3,99},{4,28},{5,101},{6,30},{7,103},{8,0},{9... | collective-permute-start | bytes 2359304 | tf_op jit(solution)/shard_map/ppermute | solution.py:42
  41.1 2.8 %collective-permute-start.11 = (bf16[64,6144]{1,0:T(8,128)(2,1)S(1)}, bf16[64,6144]{1,0:T(8,128)(2,1)S(1)}, u32[]{:S(2)}, u32[]{:S(2)}) collective-permute-start(bf16[64,6144]{1,0:T(8,128)(2,1)S(1)} %constant_dynamic-update-slice_fusion.5.refs_1_), channel_id=1, source_target_pairs={{0,24},{1,97},{2,26},{3,99},{4,28},{5,101},{6,30},{7,103},{8,0},{9... | collective-permute-start | bytes 2359304 | tf_op jit(solution)/shard_map/ppermute | solution.py:42
  43.9 2.8 %copy-done.2 = bf16[1,6144,512]{2,1,0:T(8,128)(2,1)S(1)} copy-done((bf16[1,6144,512]{2,1,0:T(8,128)(2,1)S(1)}, bf16[1,6144,512]{2,1,0:T(8,128)(2,1)}, u32[]{:S(2)}) %copy-start.2) | copy-done | bytes 6291480
  46.7 5.2 %shard_map.127 = (bf16[1,6144,512]{2,1,0:T(8,128)(2,1)S(1)}, bf16[1,6144,512]{2,1,0:T(8,128)(2,1)S(1)}, bf16[1,512,6144]{2,1,0:T(8,128)(2,1)S(1)}) custom-call(bf16[1,6144,512]{2,1,0:T(8,128)(2,1)S(1)} %copy-done.2, bf16[1,6144,512]{2,1,0:T(8,128)(2,1)} %refs_1_, bf16[1,512,6144]{2,1,0:T(8,128)(2,1)} %refs_2_), custom_call_target="tpu_custom_call" | custom-call | bytes 18874368 | tf_op jit(solution)/shard_map/pallas_call | solution.py:82
  51.8 2.7 %shard_map.128 = (bf16[64,6144]{1,0:T(8,128)(2,1)S(1)}, bf16[64,6144]{1,0:T(8,128)(2,1)S(1)}) custom-call(bf16[64,6144]{1,0:T(8,128)(2,1)S(1)} %constant_dynamic-update-slice_fusion.refs_0_, bf16[64,6144]{1,0:T(8,128)(2,1)S(1)} %constant_dynamic-update-slice_fusion.5.refs_1_, bf16[1,6144,512]{2,1,0:T(8,128)(2,1)S(1)} %get-tuple-element.140.refs_2_.refs_4_, ...), custom_call_target="tpu_custom_call" | custom-call | flops 2415919104 | bytes 3145728 | tf_op jit(solution)/shard_map/pallas_call | solution.py:128
  54.7 2.7 %collective-permute-start.13 = (bf16[32,6144]{1,0:T(8,128)(2,1)S(1)}, bf16[32,6144]{1,0:T(8,128)(2,1)S(1)}, u32[]{:S(2)}, u32[]{:S(2)}) collective-permute-start(bf16[32,6144]{1,0:T(8,128)(2,1)S(1)} %slice.275), channel_id=1, source_target_pairs={{0,24},{1,97},{2,26},{3,99},{4,28},{5,101},{6,30},{7,103},{8,0},{9... | collective-permute-start | bytes 1179656 | tf_op jit(solution)/shard_map/ppermute | solution.py:42
  57.4 2.7 %shard_map.129 = (bf16[64,6144]{1,0:T(8,128)(2,1)S(1)}, bf16[64,6144]{1,0:T(8,128)(2,1)S(1)}) custom-call(bf16[64,6144]{1,0:T(8,128)(2,1)S(1)} %collective-permute-done.4.refs_0_, bf16[64,6144]{1,0:T(8,128)(2,1)S(1)} %collective-permute-done.5.refs_1_, bf16[1,6144,512]{2,1,0:T(8,128)(2,1)S(1)} %get-tuple-element.140.refs_2_.refs_4_, ...), custom_call_target="tpu_custom_call" | custom-call | flops 2415919104 | bytes 3145728 | tf_op jit(solution)/shard_map/pallas_call | solution.py:128
  63.4 2.3 %collective-permute-done.12.refs_0_ = bf16[32,6144]{1,0:T(8,128)(2,1)S(1)} collective-permute-done((bf16[32,6144]{1,0:T(8,128)(2,1)S(1)}, bf16[32,6144]{1,0:T(8,128)(2,1)S(1)}, u32[]{:S(2)}, u32[]{:S(2)}) %collective-permute-start.12) | collective-permute-done | bytes 393248 | tf_op jit(solution)/shard_map/ppermute | solution.py:42
  65.7 2.7 %shard_map.130 = (bf16[64,6144]{1,0:T(8,128)(2,1)S(1)}, bf16[64,6144]{1,0:T(8,128)(2,1)S(1)}) custom-call(bf16[64,6144]{1,0:T(8,128)(2,1)S(1)} %collective-permute-done.10.refs_0_, bf16[64,6144]{1,0:T(8,128)(2,1)S(1)} %collective-permute-done.11.refs_1_, bf16[1,6144,512]{2,1,0:T(8,128)(2,1)S(1)} %get-tuple-element.140.refs_2_.refs_4_, ...), custom_call_target="tpu_custom_call" | custom-call | flops 2415919104 | bytes 3145728 | tf_op jit(solution)/shard_map/pallas_call | solution.py:128
  70.8 3.5 %shard_map.131 = (bf16[32,6144]{1,0:T(8,128)(2,1)S(1)}, bf16[32,6144]{1,0:T(8,128)(2,1)S(1)}, bf16[32,6144]{1,0:T(8,128)(2,1)S(1)}, bf16[32,6144]{1,0:T(8,128)(2,1)}) custom-call(bf16[32,6144]{1,0:T(8,128)(2,1)S(1)} %collective-permute-done.12.refs_0_, bf16[32,6144]{1,0:T(8,128)(2,1)S(1)} %collective-permute-done.13.refs_1_, ...), custom_call_target="tpu_custom_call" | custom-call | flops 2415919104 | bytes 3145728 | tf_op jit(solution)/shard_map/pallas_call | solution.py:128
  80.3 2.5 %collective-permute-done.26 = bf16[32,6144]{1,0:T(8,128)(2,1)} collective-permute-done((bf16[32,6144]{1,0:T(8,128)(2,1)}, bf16[32,6144]{1,0:T(8,128)(2,1)}, u32[]{:S(2)}, u32[]{:S(2)}) %collective-permute-start.26) | collective-permute-done | bytes 393248 | tf_op jit(solution)/shard_map/ppermute | solution.py:42
  85.9 3.8 %collective-permute-done.24 = bf16[32,6144]{1,0:T(8,128)(2,1)S(1)} collective-permute-done((bf16[32,6144]{1,0:T(8,128)(2,1)}, bf16[32,6144]{1,0:T(8,128)(2,1)S(1)}, u32[]{:S(2)}, u32[]{:S(2)}) %collective-permute-start.24) | collective-permute-done | bytes 393248 | tf_op jit(solution)/shard_map/ppermute | solution.py:42
  92.0 2.5 %collective-permute-start.19 = (bf16[64,6144]{1,0:T(8,128)(2,1)S(1)}, bf16[64,6144]{1,0:T(8,128)(2,1)S(1)}, u32[]{:S(2)}, u32[]{:S(2)}) collective-permute-start(bf16[64,6144]{1,0:T(8,128)(2,1)S(1)} %fusion.18), channel_id=1, source_target_pairs={{0,24},{1,97},{2,26},{3,99},{4,28},{5,101},{6,30},{7,103},{8,0},{9... | collective-permute-start | bytes 2359304 | tf_op jit(solution)/shard_map/ppermute | solution.py:42
  96.1 8.0 %collective-permute-done.25 = bf16[64,6144]{1,0:T(8,128)(2,1)S(1)} collective-permute-done((bf16[64,6144]{1,0:T(8,128)(2,1)}, bf16[64,6144]{1,0:T(8,128)(2,1)S(1)}, u32[]{:S(2)}, u32[]{:S(2)}) %collective-permute-start.25) | collective-permute-done | bytes 786464 | tf_op jit(solution)/shard_map/ppermute | solution.py:42
  104.7 7.8 %collective-permute-done.17 = bf16[64,6144]{1,0:T(8,128)(2,1)S(1)} collective-permute-done((bf16[64,6144]{1,0:T(8,128)(2,1)S(1)}, bf16[64,6144]{1,0:T(8,128)(2,1)S(1)}, u32[]{:S(2)}, u32[]{:S(2)}) %collective-permute-start.17) | collective-permute-done | bytes 786464 | tf_op jit(solution)/shard_map/ppermute | solution.py:42
  113.0 2.7 %collective-permute-start.30 = (bf16[8,6144]{1,0:T(8,128)(2,1)S(1)}, bf16[8,6144]{1,0:T(8,128)(2,1)S(1)}, u32[]{:S(2)}, u32[]{:S(2)}) collective-permute-start(bf16[8,6144]{1,0:T(8,128)(2,1)S(1)} %get-tuple-element.180), channel_id=1, source_target_pairs={{0,96},{1,25},{2,98},{3,27},{4,100},{5,29},{6,102},{7,31},{8,104},... | collective-permute-start | bytes 294920 | tf_op jit(solution)/shard_map/ppermute | solution.py:38
  115.7 3.3 %collective-permute-done.20 = bf16[8,6144]{1,0:T(8,128)(2,1)S(1)} collective-permute-done((bf16[8,6144]{1,0:T(8,128)(2,1)S(1)}, bf16[8,6144]{1,0:T(8,128)(2,1)S(1)}, u32[]{:S(2)}, u32[]{:S(2)}) %collective-permute-start.20) | collective-permute-done | bytes 98336 | tf_op jit(solution)/shard_map/ppermute | solution.py:38
  128.5 17.9 %all-to-all-start = ((bf16[32,1,8,768]{3,0,1,2:T(8,128)(2,1)}), bf16[32,1,8,768]{3,0,1,2:T(8,128)(2,1)S(1)}, u32[]{:S(2)}, u32[]{:S(2)}) async-start(bf16[32,1,8,768]{3,0,1,2:T(8,128)(2,1)} %copy.58), calls=%async_computation | async-start | bytes 786432 | tf_op jit(solution)/shard_map/all_to_all | solution.py:300
  146.4 8.0 %all-to-all-done = bf16[32,1,8,768]{3,0,1,2:T(8,128)(2,1)S(1)} async-done(((bf16[32,1,8,768]{3,0,1,2:T(8,128)(2,1)}), bf16[32,1,8,768]{3,0,1,2:T(8,128)(2,1)S(1)}, u32[]{:S(2)}, u32[]{:S(2)}) %all-to-all-start) | async-done | bytes 393248 | tf_op jit(solution)/shard_map/all_to_all | solution.py:300
  (151 shorter events, 40.7 us)
Async XLA Ops:
  29.0 8.2 %collective-permute-start.3 = (bf16[8,6144]{1,0:T(8,128)(2,1)S(1)}, bf16[8,6144]{1,0:T(8,128)(2,1)S(1)}, u32[]{:S(2)}, u32[]{:S(2)}) collective-permute-start(bf16[8,6144]{1,0:T(8,128)(2,1)S(1)} %slice.307), channel_id=1, source_target_pairs={{0,96},{1,25},{2,98},{3,27},{4,100},{5,29},{6,102},{7,31},{8,104},... | collective-permute-start | bytes 294920 | tf_op jit(solution)/shard_map/ppermute | solution.py:38
  32.3 8.8 %collective-permute-start.9 = (bf16[8,6144]{1,0:T(8,128)(2,1)S(1)}, bf16[8,6144]{1,0:T(8,128)(2,1)S(1)}, u32[]{:S(2)}, u32[]{:S(2)}) collective-permute-start(bf16[8,6144]{1,0:T(8,128)(2,1)S(1)} %slice.310), channel_id=1, source_target_pairs={{0,96},{1,25},{2,98},{3,27},{4,100},{5,29},{6,102},{7,31},{8,104},... | collective-permute-start | bytes 294920 | tf_op jit(solution)/shard_map/ppermute | solution.py:38
  37.2 17.4 %collective-permute-start.5 = (bf16[64,6144]{1,0:T(8,128)(2,1)S(1)}, bf16[64,6144]{1,0:T(8,128)(2,1)S(1)}, u32[]{:S(2)}, u32[]{:S(2)}) collective-permute-start(bf16[64,6144]{1,0:T(8,128)(2,1)S(1)} %constant_dynamic-update-slice_fusion.refs_0_), channel_id=1, source_target_pairs={{0,24},{1,97},{2,26},{3,99},{4,28},{5,101},{6,30},{7,103},{8,0},{9... | collective-permute-start | bytes 2359304 | tf_op jit(solution)/shard_map/ppermute | solution.py:42
  41.1 13.5 %collective-permute-start.4 = (bf16[64,6144]{1,0:T(8,128)(2,1)S(1)}, bf16[64,6144]{1,0:T(8,128)(2,1)S(1)}, u32[]{:S(2)}, u32[]{:S(2)}) collective-permute-start(bf16[64,6144]{1,0:T(8,128)(2,1)S(1)} %constant_dynamic-update-slice_fusion.refs_0_), channel_id=1, source_target_pairs={{0,8},{1,33},{2,10},{3,35},{4,12},{5,37},{6,14},{7,39},{8,16},{9,4... | collective-permute-start | bytes 2359304 | tf_op jit(solution)/shard_map/ppermute | solution.py:42
  41.1 19.1 %collective-permute-start.11 = (bf16[64,6144]{1,0:T(8,128)(2,1)S(1)}, bf16[64,6144]{1,0:T(8,128)(2,1)S(1)}, u32[]{:S(2)}, u32[]{:S(2)}) collective-permute-start(bf16[64,6144]{1,0:T(8,128)(2,1)S(1)} %constant_dynamic-update-slice_fusion.5.refs_1_), channel_id=1, source_target_pairs={{0,24},{1,97},{2,26},{3,99},{4,28},{5,101},{6,30},{7,103},{8,0},{9... | collective-permute-start | bytes 2359304 | tf_op jit(solution)/shard_map/ppermute | solution.py:42
  43.9 17.9 %collective-permute-start.10 = (bf16[64,6144]{1,0:T(8,128)(2,1)S(1)}, bf16[64,6144]{1,0:T(8,128)(2,1)S(1)}, u32[]{:S(2)}, u32[]{:S(2)}) collective-permute-start(bf16[64,6144]{1,0:T(8,128)(2,1)S(1)} %constant_dynamic-update-slice_fusion.5.refs_1_), channel_id=1, source_target_pairs={{0,8},{1,33},{2,10},{3,35},{4,12},{5,37},{6,14},{7,39},{8,16},{9,4... | collective-permute-start | bytes 2359304 | tf_op jit(solution)/shard_map/ppermute | solution.py:42
  54.7 8.8 %collective-permute-start.13 = (bf16[32,6144]{1,0:T(8,128)(2,1)S(1)}, bf16[32,6144]{1,0:T(8,128)(2,1)S(1)}, u32[]{:S(2)}, u32[]{:S(2)}) collective-permute-start(bf16[32,6144]{1,0:T(8,128)(2,1)S(1)} %slice.275), channel_id=1, source_target_pairs={{0,24},{1,97},{2,26},{3,99},{4,28},{5,101},{6,30},{7,103},{8,0},{9... | collective-permute-start | bytes 1179656 | tf_op jit(solution)/shard_map/ppermute | solution.py:42
  57.4 8.3 %collective-permute-start.12 = (bf16[32,6144]{1,0:T(8,128)(2,1)S(1)}, bf16[32,6144]{1,0:T(8,128)(2,1)S(1)}, u32[]{:S(2)}, u32[]{:S(2)}) collective-permute-start(bf16[32,6144]{1,0:T(8,128)(2,1)S(1)} %slice.274), channel_id=1, source_target_pairs={{0,8},{1,33},{2,10},{3,35},{4,12},{5,37},{6,14},{7,39},{8,16},{9,4... | collective-permute-start | bytes 1179656 | tf_op jit(solution)/shard_map/ppermute | solution.py:42
  61.9 7.0 %collective-permute-start.15 = (bf16[32,6144]{1,0:T(8,128)(2,1)S(1)}, bf16[32,6144]{1,0:T(8,128)(2,1)S(1)}, u32[]{:S(2)}, u32[]{:S(2)}) collective-permute-start(bf16[32,6144]{1,0:T(8,128)(2,1)S(1)} %slice.277), channel_id=1, source_target_pairs={{0,24},{1,97},{2,26},{3,99},{4,28},{5,101},{6,30},{7,103},{8,0},{9... | collective-permute-start | bytes 1179656 | tf_op jit(solution)/shard_map/ppermute | solution.py:42
  63.0 7.8 %collective-permute-start.14 = (bf16[32,6144]{1,0:T(8,128)(2,1)S(1)}, bf16[32,6144]{1,0:T(8,128)(2,1)S(1)}, u32[]{:S(2)}, u32[]{:S(2)}) collective-permute-start(bf16[32,6144]{1,0:T(8,128)(2,1)S(1)} %slice.276), channel_id=1, source_target_pairs={{0,8},{1,33},{2,10},{3,35},{4,12},{5,37},{6,14},{7,39},{8,16},{9,4... | collective-permute-start | bytes 1179656 | tf_op jit(solution)/shard_map/ppermute | solution.py:42
  75.8 6.9 %collective-permute-start.26 = (bf16[32,6144]{1,0:T(8,128)(2,1)}, bf16[32,6144]{1,0:T(8,128)(2,1)}, u32[]{:S(2)}, u32[]{:S(2)}) collective-permute-start(bf16[32,6144]{1,0:T(8,128)(2,1)} %get-tuple-element.172), channel_id=1, source_target_pairs={{0,24},{1,97},{2,26},{3,99},{4,28},{5,101},{6,30},{7,103},{8,0},{9... | collective-permute-start | bytes 1179656 | tf_op jit(solution)/shard_map/ppermute | solution.py:42
  77.4 17.2 %collective-permute-start.16 = (bf16[32,6144]{1,0:T(8,128)(2,1)S(1)}, bf16[32,6144]{1,0:T(8,128)(2,1)S(1)}, u32[]{:S(2)}, u32[]{:S(2)}) collective-permute-start(bf16[32,6144]{1,0:T(8,128)(2,1)S(1)} %get-tuple-element.165), channel_id=1, source_target_pairs={{0,8},{1,33},{2,10},{3,35},{4,12},{5,37},{6,14},{7,39},{8,16},{9,4... | collective-permute-start | bytes 1179656 | tf_op jit(solution)/shard_map/ppermute | solution.py:42
  78.8 13.0 %collective-permute-start.18 = (bf16[32,6144]{1,0:T(8,128)(2,1)}, bf16[32,6144]{1,0:T(8,128)(2,1)S(1)}, u32[]{:S(2)}, u32[]{:S(2)}) collective-permute-start(bf16[32,6144]{1,0:T(8,128)(2,1)} %copy-done.5), channel_id=1, source_target_pairs={{0,24},{1,97},{2,26},{3,99},{4,28},{5,101},{6,30},{7,103},{8,0},{9... | collective-permute-start | bytes 1179656 | tf_op jit(solution)/shard_map/ppermute | solution.py:42
  80.0 9.7 %collective-permute-start.24 = (bf16[32,6144]{1,0:T(8,128)(2,1)}, bf16[32,6144]{1,0:T(8,128)(2,1)S(1)}, u32[]{:S(2)}, u32[]{:S(2)}) collective-permute-start(bf16[32,6144]{1,0:T(8,128)(2,1)} %copy-done.6), channel_id=1, source_target_pairs={{0,8},{1,33},{2,10},{3,35},{4,12},{5,37},{6,14},{7,39},{8,16},{9,4... | collective-permute-start | bytes 1179656 | tf_op jit(solution)/shard_map/ppermute | solution.py:42
  84.7 11.3 %collective-permute-start.27 = (bf16[64,6144]{1,0:T(8,128)(2,1)}, bf16[64,6144]{1,0:T(8,128)(2,1)S(1)}, u32[]{:S(2)}, u32[]{:S(2)}) collective-permute-start(bf16[64,6144]{1,0:T(8,128)(2,1)} %fusion.20), channel_id=1, source_target_pairs={{0,24},{1,97},{2,26},{3,99},{4,28},{5,101},{6,30},{7,103},{8,0},{9... | collective-permute-start | bytes 2359304 | tf_op jit(solution)/shard_map/ppermute | solution.py:42
  91.5 12.6 %collective-permute-start.25 = (bf16[64,6144]{1,0:T(8,128)(2,1)}, bf16[64,6144]{1,0:T(8,128)(2,1)S(1)}, u32[]{:S(2)}, u32[]{:S(2)}) collective-permute-start(bf16[64,6144]{1,0:T(8,128)(2,1)} %fusion.19), channel_id=1, source_target_pairs={{0,8},{1,33},{2,10},{3,35},{4,12},{5,37},{6,14},{7,39},{8,16},{9,4... | collective-permute-start | bytes 2359304 | tf_op jit(solution)/shard_map/ppermute | solution.py:42
  92.0 12.7 %collective-permute-start.19 = (bf16[64,6144]{1,0:T(8,128)(2,1)S(1)}, bf16[64,6144]{1,0:T(8,128)(2,1)S(1)}, u32[]{:S(2)}, u32[]{:S(2)}) collective-permute-start(bf16[64,6144]{1,0:T(8,128)(2,1)S(1)} %fusion.18), channel_id=1, source_target_pairs={{0,24},{1,97},{2,26},{3,99},{4,28},{5,101},{6,30},{7,103},{8,0},{9... | collective-permute-start | bytes 2359304 | tf_op jit(solution)/shard_map/ppermute | solution.py:42
  94.8 17.7 %collective-permute-start.17 = (bf16[64,6144]{1,0:T(8,128)(2,1)S(1)}, bf16[64,6144]{1,0:T(8,128)(2,1)S(1)}, u32[]{:S(2)}, u32[]{:S(2)}) collective-permute-start(bf16[64,6144]{1,0:T(8,128)(2,1)S(1)} %fusion.17), channel_id=1, source_target_pairs={{0,8},{1,33},{2,10},{3,35},{4,12},{5,37},{6,14},{7,39},{8,16},{9,4... | collective-permute-start | bytes 2359304 | tf_op jit(solution)/shard_map/ppermute | solution.py:42
  104.4 8.5 %collective-permute-start.28 = (bf16[8,6144]{1,0:T(8,128)(2,1)S(1)}, bf16[8,6144]{1,0:T(8,128)(2,1)S(1)}, u32[]{:S(2)}, u32[]{:S(2)}) collective-permute-start(bf16[8,6144]{1,0:T(8,128)(2,1)S(1)} %slice.321), channel_id=1, source_target_pairs={{0,32},{1,9},{2,34},{3,11},{4,36},{5,13},{6,38},{7,15},{8,40},{9,1... | collective-permute-start | bytes 294920 | tf_op jit(solution)/shard_map/ppermute | solution.py:38
  112.9 6.2 %collective-permute-start.20 = (bf16[8,6144]{1,0:T(8,128)(2,1)S(1)}, bf16[8,6144]{1,0:T(8,128)(2,1)S(1)}, u32[]{:S(2)}, u32[]{:S(2)}) collective-permute-start(bf16[8,6144]{1,0:T(8,128)(2,1)S(1)} %slice.314), channel_id=1, source_target_pairs={{0,32},{1,9},{2,34},{3,11},{4,36},{5,13},{6,38},{7,15},{8,40},{9,1... | collective-permute-start | bytes 294920 | tf_op jit(solution)/shard_map/ppermute | solution.py:38
  113.0 7.6 %collective-permute-start.30 = (bf16[8,6144]{1,0:T(8,128)(2,1)S(1)}, bf16[8,6144]{1,0:T(8,128)(2,1)S(1)}, u32[]{:S(2)}, u32[]{:S(2)}) collective-permute-start(bf16[8,6144]{1,0:T(8,128)(2,1)S(1)} %get-tuple-element.180), channel_id=1, source_target_pairs={{0,96},{1,25},{2,98},{3,27},{4,100},{5,29},{6,102},{7,31},{8,104},... | collective-permute-start | bytes 294920 | tf_op jit(solution)/shard_map/ppermute | solution.py:38
  115.7 8.2 %collective-permute-start.29 = (bf16[16,6144]{1,0:T(8,128)(2,1)S(1)}, bf16[16,6144]{1,0:T(8,128)(2,1)S(1)}, u32[]{:S(2)}, u32[]{:S(2)}) collective-permute-start(bf16[16,6144]{1,0:T(8,128)(2,1)S(1)} %get-tuple-element.179), channel_id=1, source_target_pairs={{0,32},{1,9},{2,34},{3,11},{4,36},{5,13},{6,38},{7,15},{8,40},{9,1... | collective-permute-start | bytes 589832 | tf_op jit(solution)/shard_map/ppermute | solution.py:38
  119.1 6.8 %collective-permute-start.21 = (bf16[16,6144]{1,0:T(8,128)(2,1)S(1)}, bf16[16,6144]{1,0:T(8,128)(2,1)S(1)}, u32[]{:S(2)}, u32[]{:S(2)}) collective-permute-start(bf16[16,6144]{1,0:T(8,128)(2,1)S(1)} %get-tuple-element.175), channel_id=1, source_target_pairs={{0,32},{1,9},{2,34},{3,11},{4,36},{5,13},{6,38},{7,15},{8,40},{9,1... | collective-permute-start | bytes 589832 | tf_op jit(solution)/shard_map/ppermute | solution.py:38
  128.5 25.9 %all-to-all-start = ((bf16[32,1,8,768]{3,0,1,2:T(8,128)(2,1)}), bf16[32,1,8,768]{3,0,1,2:T(8,128)(2,1)S(1)}, u32[]{:S(2)}, u32[]{:S(2)}) async-start(bf16[32,1,8,768]{3,0,1,2:T(8,128)(2,1)} %copy.58), calls=%async_computation | async-start | bytes 786432 | tf_op jit(solution)/shard_map/all_to_all | solution.py:300
  (23 other events, 123.7 us)

commit v7 on v6

--- a/solution.py
+++ b/solution.py
@@ -15,8 +15,6 @@
 
 
 EPSILON = 1e-05
-CHAINS = 2
-CHAIN_ROWS = CAP // CHAINS
 
 
 def ring_pairs(step, second):
@@ -40,6 +38,17 @@
 
 def shift_second(value, step):
     return lax.ppermute(value, ("attn", "expert"), ring_pairs(step, True))
+
+
+def shift_y(value, step):
+    pairs = [
+        (y * 2 + core, (y + step) % SIDE * 2 + core) for y in range(SIDE) for core in range(2)
+    ]
+    return lax.ppermute(value, "expert", pairs)
+
+
+def swap_cores(value):
+    return lax.ppermute(value, "expert", [(index, index ^ 1) for index in range(E)])
 
 
 def split_three(value):
@@ -183,7 +192,6 @@
     cache_slots = key_cache.shape[2]
     head_size = key_cache.shape[3]
     group_size = query.shape[1] // (kv_local * head_size)
-    expert_devices = lax.axis_size("expert")
     score_scale = 1.0 / math.sqrt(head_size)
     queries = query.reshape(row_count, kv_local, group_size, head_size)
     scores = (
@@ -262,44 +270,44 @@
     )
     outgoing = (outgoing * own_scale).astype(jnp.bfloat16)
 
-    lines = []
-    for chain in range(CHAINS):
-        slab = outgoing[chain * CHAIN_ROWS : (chain + 1) * CHAIN_ROWS]
-        near = spread_near(slab, shift_first)
-        lines.append(jnp.concatenate([slab, *near, *spread_far(*near, shift_first)], axis=0))
-    weights = lax.optimization_barrier((w_gate, w_up, w_down, *lines))[:3]
+    near = spread_near(outgoing, shift_first)
+    line = jnp.concatenate([outgoing, *near, shift_first(outgoing, 2)], axis=0)
+    weights = lax.optimization_barrier((w_gate, w_up, w_down, line))[:3]
     weights = load(*weights)
-    own_parts = feed(lines, *weights)
-    nears = [spread_near(line, shift_second) for line in lines]
-    nears[0], own_parts = lax.optimization_barrier((nears[0], own_parts))
-    first_part = feed(nears[0], *weights)
-    nears[1], first_part = lax.optimization_barrier((nears[1], first_part))
-    fars = [spread_far(*near, shift_second) for near in nears]
-    nears[1], fars[0] = lax.optimization_barrier((nears[1], fars[0]))
-    near_parts = [first_part, feed(nears[1], *weights)]
-    fars, near_parts = lax.optimization_barrier((fars, near_parts))
-    far_part = feed([piece for far in fars for piece in far], *weights)
-
-    results = []
-    for chain in range(CHAINS):
-        behind, ahead = near_parts[chain]
-        far = far_part[2 * chain : 2 * chain + 2]
-        up, down = halves_added(ahead, behind, *far, shift_second)
-        line_sum = add_three(own_parts[chain], shift_second(up, 1), shift_second(down, -1))
-        behind = line_sum[CHAIN_ROWS : 2 * CHAIN_ROWS]
-        ahead = line_sum[2 * CHAIN_ROWS : 3 * CHAIN_ROWS]
-        middle = 3 * CHAIN_ROWS + CHAIN_ROWS // 2
-        far_low, far_high = line_sum[3 * CHAIN_ROWS : middle], line_sum[middle:]
-        up, down = halves_added(ahead, behind, far_low, far_high, shift_first)
-        results.append(
-            add_three(line_sum[:CHAIN_ROWS], shift_first(up, 1), shift_first(down, -1))
-        )
-    expert_result = jnp.concatenate(results, axis=0)
-
-    expert_result = expert_result.reshape(CAP, 1, expert_devices, width_local)
-    returned = lax.all_to_all(expert_result, "expert", split_axis=2, concat_axis=1, tiled=True)
-    flat_result = returned.reshape(CAP * E, width_local)
-    target_index = slot_index * E + expert_ids
+    line_near = spread_near(line, shift_second)
+    (own_part,) = feed([line], *weights)
+    line_near, own_part = lax.optimization_barrier((line_near, own_part))
+    line_far = spread_far(*line_near, shift_second)
+    behind_part, ahead_part = feed(line_near, *weights)
+    line_far, behind_part, ahead_part = lax.optimization_barrier(
+        (line_far, behind_part, ahead_part)
+    )
+    far_part = feed(line_far, *weights)
+
+    up, down = halves_added(ahead_part, behind_part, *far_part, shift_second)
+    line_sum = add_three(own_part, shift_second(up, 1), shift_second(down, -1))
+    parts = [line_sum[k * CAP : (k + 1) * CAP] for k in range(SIDE)]
+    expert_result = (
+        parts[0].astype(jnp.float32)
+        + shift_first(parts[1], -1).astype(jnp.float32)
+        + shift_first(parts[2], 1).astype(jnp.float32)
+        + shift_first(parts[3], 2).astype(jnp.float32)
+    ).astype(jnp.bfloat16)
+
+    core = own_expert % 2
+    row_y = own_expert // 2
+    slices = jnp.swapaxes(expert_result.reshape(CAP, SIDE, 2, width_local), 0, 1)
+    even, odd = slices[:, :, 0], slices[:, :, 1]
+    kept = jnp.where(core == 0, even, odd)
+    swapped = swap_cores(jnp.where(core == 0, odd, even))
+    pair = jnp.concatenate([kept, swapped], axis=1)
+    blocks = []
+    for step in range(SIDE):
+        block = lax.dynamic_index_in_dim(pair, (row_y + step) % SIDE, 0, keepdims=False)
+        blocks.append(block if step == 0 else shift_y(block, step))
+    flat_result = jnp.concatenate(blocks, axis=0)
+    away = (row_y - expert_ids // 2 + SIDE) % SIDE
+    target_index = (away * 2 + (expert_ids + core) % 2) * CAP + slot_index
     picker = (
         target_index[:, :, None] == lax.broadcasted_iota(jnp.int32, (1, 1, CAP * E), 2)
     ).astype(jnp.bfloat16)

time: 156 us -> 143 us (0.917)
  starting transfers between devices: 54.1 us -> 30.8 us
  waiting for transfers between devices: 47.2 us -> 64.5 us
  local copies, waits for them, and re-layouts: 9.08 us -> 5.41 us
  other arithmetic: 8.54 us -> 6.41 us
    all_to_all x1 -> x0, starting transfers between devices: 17.9 us -> none  [on_device(): lax.all_to_all(expert_result, 'expert', split_axis=2, concat_axis=1, tile...]
    ppermute x16 -> x6, starting transfers between devices: 18.3 us -> 7.61 us  [shift_first(): return lax.ppermute(value, ('attn', 'expert'), ring_pairs(step, False))]
    ppermute x0 -> x4, starting transfers between devices: none -> 10.6 us  [the longest x1 6.94 us: swap_cores(): lax.ppermute(value, 'expert', [(index, index ^ 1) for index in range(E)])]
    ppermute x16 -> x6, waiting for transfers between devices: 9.64 us -> 20.2 us  [shift_first(): return lax.ppermute(value, ('attn', 'expert'), ring_pairs(step, False))]
    ppermute x16 -> x8, waiting for transfers between devices: 29.5 us -> 38.8 us  [shift_second(): return lax.ppermute(value, ('attn', 'expert'), ring_pairs(step, True))]
    all_to_all x1 -> x0, waiting for transfers between devices: 8.04 us -> none  [on_device(): lax.all_to_all(expert_result, 'expert', split_axis=2, concat_axis=1, tile...]
    ppermute x0 -> x4, waiting for transfers between devices: none -> 5.58 us  [the longest x3 4.53 us: shift_y(): return lax.ppermute(value, 'expert', pairs)]
    ppermute x16 -> x8, starting transfers between devices: 17.9 us -> 12.6 us  [shift_second(): return lax.ppermute(value, ('attn', 'expert'), ring_pairs(step, True))]
  transfers between devices with their start and end apart: 33 -> 18, of which waited for: 16 -> 11; matrix products, arithmetic and copies ran while one was open for 4% -> 1% of each run, Pallas kernels for 9% -> 9%
where the time goes in v7:
time: 143 us; the launch traced here: 142 us
  waiting for transfers between devices  64.5 us (45%)
  starting transfers between devices  30.8 us (22%)
  Pallas kernels  15.7 us (11%)
  blocking collectives  15.4 us (11%)
  other arithmetic  6.41 us (4%)
  local copies, waits for them, and re-layouts  5.41 us (4%)
  matrix products  3.6 us (3%)
    ppermute x8, waiting for transfers between devices, shift_second(): return lax.ppermute(value, ('attn', 'expert'), ring_pairs(step, True))  38.8 us
    ppermute x6, waiting for transfers between devices, shift_first(): return lax.ppermute(value, ('attn', 'expert'), ring_pairs(step, False))  20.2 us
    all_gather x1, blocking collectives, on_device(): gathered = lax.all_gather(payload, 'expert', axis=0)  15.4 us
    ppermute x8, starting transfers between devices, shift_second(): return lax.ppermute(value, ('attn', 'expert'), ring_pairs(step, True))  12.6 us
    pallas_call x3, Pallas kernels, feed(): pl.pallas_call(functools.partial(feed_kernel, len(row_arrays)), in_specs=...  10.6 us
    ppermute x6, starting transfers between devices, shift_first(): return lax.ppermute(value, ('attn', 'expert'), ring_pairs(step, False))  7.61 us
    ppermute x1, starting transfers between devices, swap_cores(): lax.ppermute(value, 'expert', [(index, index ^ 1) for index in range(E)])  6.94 us
    pallas_call x1, Pallas kernels, load(): pl.pallas_call(load_kernel, in_specs=[pl.BlockSpec(memory_space=pltpu.HBM...  5.15 us
  transfers between devices with their start and end apart: 18, of which 11 were waited for; matrix products, arithmetic and copies ran while one was open for 1% of the time, Pallas kernels for 9%

profile of v7, /device:TPU:1, one launch (start us, length us, event | category | flops | bytes accessed | tf_op | source)
XLA Modules:
  0.0 142.2 jit_solution(15277509023954036682)
XLA Ops:
  7.2 15.4 %all-gather = bf16[512,896]{1,0:T(8,128)(2,1)S(1)} all-gather(bf16[64,896]{1,0:T(8,128)(2,1)S(1)} %concatenate.20), channel_id=2, replica_groups=mesh['attn'=16,'expert'=8] {'expert'}, dimensions={0}, use_global_device_ids=true | all-gather | bytes 1032192 | tf_op jit(solution)/shard_map/all_gather | solution.py:240
  26.3 1.5 %collective-permute-start.2 = (bf16[32,6144]{1,0:T(8,128)(2,1)S(1)}, bf16[32,6144]{1,0:T(8,128)(2,1)S(1)}, u32[]{:S(2)}, u32[]{:S(2)}) collective-permute-start(bf16[32,6144]{1,0:T(8,128)(2,1)S(1)} %multiply_convert_fusion), channel_id=1, source_target_pairs={{0,64},{1,17},{2,66},{3,19},{4,68},{5,21},{6,70},{7,23},{8,72},{9,... | collective-permute-start | bytes 1179656 | tf_op jit(solution)/shard_map/ppermute | solution.py:36
  27.8 3.9 %collective-permute-done = bf16[32,6144]{1,0:T(8,128)(2,1)S(1)} collective-permute-done((bf16[32,6144]{1,0:T(8,128)(2,1)S(1)}, bf16[32,6144]{1,0:T(8,128)(2,1)S(1)}, u32[]{:S(2)}, u32[]{:S(2)}) %collective-permute-start) | collective-permute-done | bytes 393248 | tf_op jit(solution)/shard_map/ppermute | solution.py:36
  31.7 5.2 %collective-permute-done.2 = bf16[32,6144]{1,0:T(8,128)(2,1)S(1)} collective-permute-done((bf16[32,6144]{1,0:T(8,128)(2,1)S(1)}, bf16[32,6144]{1,0:T(8,128)(2,1)S(1)}, u32[]{:S(2)}, u32[]{:S(2)}) %collective-permute-start.2) | collective-permute-done | bytes 393248 | tf_op jit(solution)/shard_map/ppermute | solution.py:36
  38.5 2.2 %collective-permute-start.4 = (bf16[128,6144]{1,0:T(8,128)(2,1)S(1)}, bf16[128,6144]{1,0:T(8,128)(2,1)S(1)}, u32[]{:S(2)}, u32[]{:S(2)}) collective-permute-start(bf16[128,6144]{1,0:T(8,128)(2,1)S(1)} %pad_maximum_fusion.refs_0_), channel_id=1, source_target_pairs={{0,24},{1,97},{2,26},{3,99},{4,28},{5,101},{6,30},{7,103},{8,0},{9... | collective-permute-start | bytes 4718600 | tf_op jit(solution)/shard_map/ppermute | solution.py:40
  40.7 2.8 %copy-done.2 = bf16[1,6144,512]{2,1,0:T(8,128)(2,1)S(1)} copy-done((bf16[1,6144,512]{2,1,0:T(8,128)(2,1)S(1)}, bf16[1,6144,512]{2,1,0:T(8,128)(2,1)}, u32[]{:S(2)}) %copy-start.2) | copy-done | bytes 6291480
  43.5 5.2 %shard_map.127 = (bf16[1,6144,512]{2,1,0:T(8,128)(2,1)S(1)}, bf16[1,6144,512]{2,1,0:T(8,128)(2,1)S(1)}, bf16[1,512,6144]{2,1,0:T(8,128)(2,1)S(1)}) custom-call(bf16[1,6144,512]{2,1,0:T(8,128)(2,1)S(1)} %copy-done.2, bf16[1,6144,512]{2,1,0:T(8,128)(2,1)} %refs_1_, bf16[1,512,6144]{2,1,0:T(8,128)(2,1)} %refs_2_), custom_call_target="tpu_custom_call" | custom-call | bytes 18874368 | tf_op jit(solution)/shard_map/pallas_call | solution.py:91
  48.6 2.7 %shard_map.128 = bf16[128,6144]{1,0:T(8,128)(2,1)S(1)} custom-call(bf16[128,6144]{1,0:T(8,128)(2,1)S(1)} %pad_maximum_fusion.refs_0_, bf16[1,6144,512]{2,1,0:T(8,128)(2,1)S(1)} %get-tuple-element.49.refs_1_.refs_2_, bf16[1,6144,512]{2,1,0:T(8,128)(2,1)S(1)} %get-tuple-element.50.refs_2_.refs_3_, bf16[1,512,6144]{2,1,0:T(8,128)(2,1)S(1)} %get-tuple-element.51.refs_3_.refs_4_), custom_call_target="tpu_custom_call" | custom-call | flops 2415919104 | bytes 3145728 | tf_op jit(solution)/shard_map/pallas_call | solution.py:137
  51.4 7.3 %collective-permute-done.3.refs_0_ = bf16[128,6144]{1,0:T(8,128)(2,1)S(1)} collective-permute-done((bf16[128,6144]{1,0:T(8,128)(2,1)S(1)}, bf16[128,6144]{1,0:T(8,128)(2,1)S(1)}, u32[]{:S(2)}, u32[]{:S(2)}) %collective-permute-start.3) | collective-permute-done | bytes 1572896 | tf_op jit(solution)/shard_map/ppermute | solution.py:40
  59.8 2.0 %collective-permute-start.6 = (bf16[64,6144]{1,0:T(8,128)(2,1)S(1)}, bf16[64,6144]{1,0:T(8,128)(2,1)S(1)}, u32[]{:S(2)}, u32[]{:S(2)}) collective-permute-start(bf16[64,6144]{1,0:T(8,128)(2,1)S(1)} %slice.109), channel_id=1, source_target_pairs={{0,24},{1,97},{2,26},{3,99},{4,28},{5,101},{6,30},{7,103},{8,0},{9... | collective-permute-start | bytes 2359304 | tf_op jit(solution)/shard_map/ppermute | solution.py:40
  61.9 5.1 %shard_map.129 = (bf16[128,6144]{1,0:T(8,128)(2,1)S(1)}, bf16[128,6144]{1,0:T(8,128)(2,1)S(1)}) custom-call(bf16[128,6144]{1,0:T(8,128)(2,1)S(1)} %collective-permute-done.3.refs_0_, bf16[128,6144]{1,0:T(8,128)(2,1)S(1)} %collective-permute-done.4.refs_1_, bf16[1,6144,512]{2,1,0:T(8,128)(2,1)S(1)} %get-tuple-element.49.refs_1_.refs_2_, ...), custom_call_target="tpu_custom_call" | custom-call | flops 4831838208 | bytes 6291456 | tf_op jit(solution)/shard_map/pallas_call | solution.py:137
  67.0 4.2 %collective-permute-done.5.refs_0_ = bf16[64,6144]{1,0:T(8,128)(2,1)S(1)} collective-permute-done((bf16[64,6144]{1,0:T(8,128)(2,1)S(1)}, bf16[64,6144]{1,0:T(8,128)(2,1)S(1)}, u32[]{:S(2)}, u32[]{:S(2)}) %collective-permute-start.5) | collective-permute-done | bytes 786464 | tf_op jit(solution)/shard_map/ppermute | solution.py:40
  71.2 2.7 %shard_map.130 = (bf16[64,6144]{1,0:T(8,128)(2,1)S(1)}, bf16[64,6144]{1,0:T(8,128)(2,1)S(1)}) custom-call(bf16[64,6144]{1,0:T(8,128)(2,1)S(1)} %collective-permute-done.5.refs_0_, bf16[64,6144]{1,0:T(8,128)(2,1)S(1)} %collective-permute-done.6.refs_1_, bf16[1,6144,512]{2,1,0:T(8,128)(2,1)S(1)} %get-tuple-element.49.refs_1_.refs_2_, ...), custom_call_target="tpu_custom_call" | custom-call | flops 2415919104 | bytes 3145728 | tf_op jit(solution)/shard_map/pallas_call | solution.py:137
  75.2 1.9 %collective-permute-start.9 = (bf16[64,6144]{1,0:T(8,128)(2,1)S(1)}, bf16[64,6144]{1,0:T(8,128)(2,1)S(1)}, u32[]{:S(2)}, u32[]{:S(2)}) collective-permute-start(bf16[64,6144]{1,0:T(8,128)(2,1)S(1)} %get-tuple-element.62), channel_id=1, source_target_pairs={{0,24},{1,97},{2,26},{3,99},{4,28},{5,101},{6,30},{7,103},{8,0},{9... | collective-permute-start | bytes 2359304 | tf_op jit(solution)/shard_map/ppermute | solution.py:40
  77.1 9.6 %collective-permute-done.7 = bf16[64,6144]{1,0:T(8,128)(2,1)S(1)} collective-permute-done((bf16[64,6144]{1,0:T(8,128)(2,1)S(1)}, bf16[64,6144]{1,0:T(8,128)(2,1)S(1)}, u32[]{:S(2)}, u32[]{:S(2)}) %collective-permute-start.7) | collective-permute-done | bytes 786464 | tf_op jit(solution)/shard_map/ppermute | solution.py:40
  87.6 2.7 %collective-permute-start.10 = (bf16[128,6144]{1,0:T(8,128)(2,1)S(1)}, bf16[128,6144]{1,0:T(8,128)(2,1)S(1)}, u32[]{:S(2)}, u32[]{:S(2)}) collective-permute-start(bf16[128,6144]{1,0:T(8,128)(2,1)S(1)} %fusion.17), channel_id=1, source_target_pairs={{0,24},{1,97},{2,26},{3,99},{4,28},{5,101},{6,30},{7,103},{8,0},{9... | collective-permute-start | bytes 4718600 | tf_op jit(solution)/shard_map/ppermute | solution.py:40
  90.3 17.6 %collective-permute-done.8 = bf16[128,6144]{1,0:T(8,128)(2,1)S(1)} collective-permute-done((bf16[128,6144]{1,0:T(8,128)(2,1)S(1)}, bf16[128,6144]{1,0:T(8,128)(2,1)S(1)}, u32[]{:S(2)}, u32[]{:S(2)}) %collective-permute-start.8) | collective-permute-done | bytes 1572896 | tf_op jit(solution)/shard_map/ppermute | solution.py:40
  108.8 2.1 %collective-permute-start.11 = (bf16[32,6144]{1,0:T(8,128)(2,1)S(1)}, bf16[32,6144]{1,0:T(8,128)(2,1)S(1)}, u32[]{:S(2)}, u32[]{:S(2)}) collective-permute-start(bf16[32,6144]{1,0:T(8,128)(2,1)S(1)} %get-tuple-element.65), channel_id=1, source_target_pairs={{0,96},{1,25},{2,98},{3,27},{4,100},{5,29},{6,102},{7,31},{8,104},... | collective-permute-start | bytes 1179656 | tf_op jit(solution)/shard_map/ppermute | solution.py:36
  112.2 9.2 %collective-permute-done.11 = bf16[32,6144]{1,0:T(8,128)(2,1)S(1)} collective-permute-done((bf16[32,6144]{1,0:T(8,128)(2,1)S(1)}, bf16[32,6144]{1,0:T(8,128)(2,1)S(1)}, u32[]{:S(2)}, u32[]{:S(2)}) %collective-permute-start.11) | collective-permute-done | bytes 393248 | tf_op jit(solution)/shard_map/ppermute | solution.py:36
  121.4 1.9 %collective-permute-done.12 = bf16[32,6144]{1,0:T(8,128)(2,1)} collective-permute-done((bf16[32,6144]{1,0:T(8,128)(2,1)S(1)}, bf16[32,6144]{1,0:T(8,128)(2,1)}, u32[]{:S(2)}, u32[]{:S(2)}) %collective-permute-start.12) | collective-permute-done | bytes 393248 | tf_op jit(solution)/shard_map/ppermute | solution.py:36
  125.0 6.9 %collective-permute-start.14 = (bf16[4,32,768]{2,1,0:T(8,128)(2,1)S(1)}, bf16[4,32,768]{2,1,0:T(8,128)(2,1)S(1)}, u32[]{:S(2)}, u32[]{:S(2)}) collective-permute-start(bf16[4,32,768]{2,1,0:T(8,128)(2,1)S(1)} %get-tuple-element.72), channel_id=1, source_target_pairs={{0,1},{1,0},{2,3},{3,2},{4,5},{5,4},{6,7},{7,6},{8,9},{9,8},{10,11... | collective-permute-start | bytes 589832 | tf_op jit(solution)/shard_map/ppermute | solution.py:51
  134.2 2.4 %collective-permute-start.16 = (bf16[64,768]{1,0:T(8,128)(2,1)S(1)}, bf16[64,768]{1,0:T(8,128)(2,1)S(1)}, u32[]{:S(2)}, u32[]{:S(2)}) collective-permute-start(bf16[64,768]{1,0:T(8,128)(2,1)S(1)} %get-tuple-element.70), channel_id=1, source_target_pairs={{0,4},{1,5},{2,6},{3,7},{4,0},{5,1},{6,2},{7,3},{8,12},{9,13},{10,... | collective-permute-start | bytes 294920 | tf_op jit(solution)/shard_map/ppermute | solution.py:47
  136.7 1.6 %collective-permute-done.15 = bf16[64,768]{1,0:T(8,128)(2,1)S(1)} collective-permute-done((bf16[64,768]{1,0:T(8,128)(2,1)S(1)}, bf16[64,768]{1,0:T(8,128)(2,1)S(1)}, u32[]{:S(2)}, u32[]{:S(2)}) %collective-permute-start.15) | collective-permute-done | bytes 98336 | tf_op jit(solution)/shard_map/ppermute | solution.py:47
  138.3 2.9 %collective-permute-done.16 = bf16[64,768]{1,0:T(8,128)(2,1)S(1)} collective-permute-done((bf16[64,768]{1,0:T(8,128)(2,1)S(1)}, bf16[64,768]{1,0:T(8,128)(2,1)S(1)}, u32[]{:S(2)}, u32[]{:S(2)}) %collective-permute-start.16) | collective-permute-done | bytes 98336 | tf_op jit(solution)/shard_map/ppermute | solution.py:47
  (84 shorter events, 22.8 us)
Async XLA Ops:
  0.0 3.7 %copy-start = (bf16[64,1,128,128]{3,2,1,0:T(8,128)(2,1)S(1)}, bf16[64,1,128,128]{3,2,1,0:T(8,128)(2,1)}, u32[]{:S(2)}) copy-start(bf16[64,1,128,128]{3,2,1,0:T(8,128)(2,1)} %param.19) | copy-start | bytes 6291460
  1.2 3.9 %copy-start.3 = (bf16[64,1,128,128]{3,2,1,0:T(8,128)(2,1)S(1)}, bf16[64,1,128,128]{3,2,1,0:T(8,128)(2,1)}, u32[]{:S(2)}) copy-start(bf16[64,1,128,128]{3,2,1,0:T(8,128)(2,1)} %param.20) | copy-start | bytes 6291460
  5.0 1.0 copy-start.5
  5.1 1.3 copy-start.7
  23.5 8.2 %collective-permute-start = (bf16[32,6144]{1,0:T(8,128)(2,1)S(1)}, bf16[32,6144]{1,0:T(8,128)(2,1)S(1)}, u32[]{:S(2)}, u32[]{:S(2)}) collective-permute-start(bf16[32,6144]{1,0:T(8,128)(2,1)S(1)} %multiply_convert_fusion), channel_id=1, source_target_pairs={{0,32},{1,9},{2,34},{3,11},{4,36},{5,13},{6,38},{7,15},{8,40},{9,1... | collective-permute-start | bytes 1179656 | tf_op jit(solution)/shard_map/ppermute | solution.py:36
  24.8 6.9 %collective-permute-start.1 = (bf16[32,6144]{1,0:T(8,128)(2,1)S(1)}, bf16[32,6144]{1,0:T(8,128)(2,1)S(1)}, u32[]{:S(2)}, u32[]{:S(2)}) collective-permute-start(bf16[32,6144]{1,0:T(8,128)(2,1)S(1)} %multiply_convert_fusion), channel_id=1, source_target_pairs={{0,96},{1,25},{2,98},{3,27},{4,100},{5,29},{6,102},{7,31},{8,104},... | collective-permute-start | bytes 1179656 | tf_op jit(solution)/shard_map/ppermute | solution.py:36
  26.3 10.7 %collective-permute-start.2 = (bf16[32,6144]{1,0:T(8,128)(2,1)S(1)}, bf16[32,6144]{1,0:T(8,128)(2,1)S(1)}, u32[]{:S(2)}, u32[]{:S(2)}) collective-permute-start(bf16[32,6144]{1,0:T(8,128)(2,1)S(1)} %multiply_convert_fusion), channel_id=1, source_target_pairs={{0,64},{1,17},{2,66},{3,19},{4,68},{5,21},{6,70},{7,23},{8,72},{9,... | collective-permute-start | bytes 1179656 | tf_op jit(solution)/shard_map/ppermute | solution.py:36
  37.1 21.6 %collective-permute-start.3 = (bf16[128,6144]{1,0:T(8,128)(2,1)S(1)}, bf16[128,6144]{1,0:T(8,128)(2,1)S(1)}, u32[]{:S(2)}, u32[]{:S(2)}) collective-permute-start(bf16[128,6144]{1,0:T(8,128)(2,1)S(1)} %pad_maximum_fusion.refs_0_), channel_id=1, source_target_pairs={{0,8},{1,33},{2,10},{3,35},{4,12},{5,37},{6,14},{7,39},{8,16},{9,4... | collective-permute-start | bytes 4718600 | tf_op jit(solution)/shard_map/ppermute | solution.py:40
  38.5 20.2 %collective-permute-start.4 = (bf16[128,6144]{1,0:T(8,128)(2,1)S(1)}, bf16[128,6144]{1,0:T(8,128)(2,1)S(1)}, u32[]{:S(2)}, u32[]{:S(2)}) collective-permute-start(bf16[128,6144]{1,0:T(8,128)(2,1)S(1)} %pad_maximum_fusion.refs_0_), channel_id=1, source_target_pairs={{0,24},{1,97},{2,26},{3,99},{4,28},{5,101},{6,30},{7,103},{8,0},{9... | collective-permute-start | bytes 4718600 | tf_op jit(solution)/shard_map/ppermute | solution.py:40
  40.7 2.8 %copy-start.2 = (bf16[1,6144,512]{2,1,0:T(8,128)(2,1)S(1)}, bf16[1,6144,512]{2,1,0:T(8,128)(2,1)}, u32[]{:S(2)}) copy-start(bf16[1,6144,512]{2,1,0:T(8,128)(2,1)} %refs_0_) | copy-start | bytes 18874372
  58.7 12.5 %collective-permute-start.5 = (bf16[64,6144]{1,0:T(8,128)(2,1)S(1)}, bf16[64,6144]{1,0:T(8,128)(2,1)S(1)}, u32[]{:S(2)}, u32[]{:S(2)}) collective-permute-start(bf16[64,6144]{1,0:T(8,128)(2,1)S(1)} %slice.108), channel_id=1, source_target_pairs={{0,8},{1,33},{2,10},{3,35},{4,12},{5,37},{6,14},{7,39},{8,16},{9,4... | collective-permute-start | bytes 2359304 | tf_op jit(solution)/shard_map/ppermute | solution.py:40
  59.8 11.4 %collective-permute-start.6 = (bf16[64,6144]{1,0:T(8,128)(2,1)S(1)}, bf16[64,6144]{1,0:T(8,128)(2,1)S(1)}, u32[]{:S(2)}, u32[]{:S(2)}) collective-permute-start(bf16[64,6144]{1,0:T(8,128)(2,1)S(1)} %slice.109), channel_id=1, source_target_pairs={{0,24},{1,97},{2,26},{3,99},{4,28},{5,101},{6,30},{7,103},{8,0},{9... | collective-permute-start | bytes 2359304 | tf_op jit(solution)/shard_map/ppermute | solution.py:40
  74.0 12.7 %collective-permute-start.7 = (bf16[64,6144]{1,0:T(8,128)(2,1)S(1)}, bf16[64,6144]{1,0:T(8,128)(2,1)S(1)}, u32[]{:S(2)}, u32[]{:S(2)}) collective-permute-start(bf16[64,6144]{1,0:T(8,128)(2,1)S(1)} %get-tuple-element.60), channel_id=1, source_target_pairs={{0,8},{1,33},{2,10},{3,35},{4,12},{5,37},{6,14},{7,39},{8,16},{9,4... | collective-permute-start | bytes 2359304 | tf_op jit(solution)/shard_map/ppermute | solution.py:40
  75.2 12.0 %collective-permute-start.9 = (bf16[64,6144]{1,0:T(8,128)(2,1)S(1)}, bf16[64,6144]{1,0:T(8,128)(2,1)S(1)}, u32[]{:S(2)}, u32[]{:S(2)}) collective-permute-start(bf16[64,6144]{1,0:T(8,128)(2,1)S(1)} %get-tuple-element.62), channel_id=1, source_target_pairs={{0,24},{1,97},{2,26},{3,99},{4,28},{5,101},{6,30},{7,103},{8,0},{9... | collective-permute-start | bytes 2359304 | tf_op jit(solution)/shard_map/ppermute | solution.py:40
  87.1 20.8 %collective-permute-start.8 = (bf16[128,6144]{1,0:T(8,128)(2,1)S(1)}, bf16[128,6144]{1,0:T(8,128)(2,1)S(1)}, u32[]{:S(2)}, u32[]{:S(2)}) collective-permute-start(bf16[128,6144]{1,0:T(8,128)(2,1)S(1)} %fusion.16), channel_id=1, source_target_pairs={{0,8},{1,33},{2,10},{3,35},{4,12},{5,37},{6,14},{7,39},{8,16},{9,4... | collective-permute-start | bytes 4718600 | tf_op jit(solution)/shard_map/ppermute | solution.py:40
  87.6 20.3 %collective-permute-start.10 = (bf16[128,6144]{1,0:T(8,128)(2,1)S(1)}, bf16[128,6144]{1,0:T(8,128)(2,1)S(1)}, u32[]{:S(2)}, u32[]{:S(2)}) collective-permute-start(bf16[128,6144]{1,0:T(8,128)(2,1)S(1)} %fusion.17), channel_id=1, source_target_pairs={{0,24},{1,97},{2,26},{3,99},{4,28},{5,101},{6,30},{7,103},{8,0},{9... | collective-permute-start | bytes 4718600 | tf_op jit(solution)/shard_map/ppermute | solution.py:40
  108.8 12.6 %collective-permute-start.11 = (bf16[32,6144]{1,0:T(8,128)(2,1)S(1)}, bf16[32,6144]{1,0:T(8,128)(2,1)S(1)}, u32[]{:S(2)}, u32[]{:S(2)}) collective-permute-start(bf16[32,6144]{1,0:T(8,128)(2,1)S(1)} %get-tuple-element.65), channel_id=1, source_target_pairs={{0,96},{1,25},{2,98},{3,27},{4,100},{5,29},{6,102},{7,31},{8,104},... | collective-permute-start | bytes 1179656 | tf_op jit(solution)/shard_map/ppermute | solution.py:36
  110.8 12.5 %collective-permute-start.12 = (bf16[32,6144]{1,0:T(8,128)(2,1)S(1)}, bf16[32,6144]{1,0:T(8,128)(2,1)}, u32[]{:S(2)}, u32[]{:S(2)}) collective-permute-start(bf16[32,6144]{1,0:T(8,128)(2,1)S(1)} %get-tuple-element.67), channel_id=1, source_target_pairs={{0,32},{1,9},{2,34},{3,11},{4,36},{5,13},{6,38},{7,15},{8,40},{9,1... | collective-permute-start | bytes 1179656 | tf_op jit(solution)/shard_map/ppermute | solution.py:36
  110.8 12.5 %collective-permute-start.13 = (bf16[32,6144]{1,0:T(8,128)(2,1)S(1)}, bf16[32,6144]{1,0:T(8,128)(2,1)}, u32[]{:S(2)}, u32[]{:S(2)}) collective-permute-start(bf16[32,6144]{1,0:T(8,128)(2,1)S(1)} %get-tuple-element.66), channel_id=1, source_target_pairs={{0,64},{1,17},{2,66},{3,19},{4,68},{5,21},{6,70},{7,23},{8,72},{9,... | collective-permute-start | bytes 1179656 | tf_op jit(solution)/shard_map/ppermute | solution.py:36
  125.0 8.0 %collective-permute-start.14 = (bf16[4,32,768]{2,1,0:T(8,128)(2,1)S(1)}, bf16[4,32,768]{2,1,0:T(8,128)(2,1)S(1)}, u32[]{:S(2)}, u32[]{:S(2)}) collective-permute-start(bf16[4,32,768]{2,1,0:T(8,128)(2,1)S(1)} %get-tuple-element.72), channel_id=1, source_target_pairs={{0,1},{1,0},{2,3},{3,2},{4,5},{5,4},{6,7},{7,6},{8,9},{9,8},{10,11... | collective-permute-start | bytes 589832 | tf_op jit(solution)/shard_map/ppermute | solution.py:51
  131.9 10.3 %copy-start.1 = (bf16[64,1,128,128]{3,2,1,0:T(8,128)(2,1)S(1)}, bf16[64,1,128,128]{3,2,1,0:T(8,128)(2,1)}, u32[]{:S(2)}) copy-start(bf16[64,1,128,128]{3,2,1,0:T(8,128)(2,1)} %param.19) | copy-start | bytes 6291460
  133.0 5.3 %collective-permute-start.15 = (bf16[64,768]{1,0:T(8,128)(2,1)S(1)}, bf16[64,768]{1,0:T(8,128)(2,1)S(1)}, u32[]{:S(2)}, u32[]{:S(2)}) collective-permute-start(bf16[64,768]{1,0:T(8,128)(2,1)S(1)} %get-tuple-element.69), channel_id=1, source_target_pairs={{0,2},{1,3},{2,4},{3,5},{4,6},{5,7},{6,0},{7,1},{8,10},{9,11},{10,... | collective-permute-start | bytes 294920 | tf_op jit(solution)/shard_map/ppermute | solution.py:47
  134.2 7.0 %collective-permute-start.16 = (bf16[64,768]{1,0:T(8,128)(2,1)S(1)}, bf16[64,768]{1,0:T(8,128)(2,1)S(1)}, u32[]{:S(2)}, u32[]{:S(2)}) collective-permute-start(bf16[64,768]{1,0:T(8,128)(2,1)S(1)} %get-tuple-element.70), channel_id=1, source_target_pairs={{0,4},{1,5},{2,6},{3,7},{4,0},{5,1},{6,2},{7,3},{8,12},{9,13},{10,... | collective-permute-start | bytes 294920 | tf_op jit(solution)/shard_map/ppermute | solution.py:47
  136.6 4.7 %collective-permute-start.17 = (bf16[64,768]{1,0:T(8,128)(2,1)S(1)}, bf16[64,768]{1,0:T(8,128)(2,1)S(1)}, u32[]{:S(2)}, u32[]{:S(2)}) collective-permute-start(bf16[64,768]{1,0:T(8,128)(2,1)S(1)} %get-tuple-element.71), channel_id=1, source_target_pairs={{0,6},{1,7},{2,0},{3,1},{4,2},{5,3},{6,4},{7,5},{8,14},{9,15},{10,... | collective-permute-start | bytes 294920 | tf_op jit(solution)/shard_map/ppermute | solution.py:47
  (2 other events, 1.9 us)

commit v8 on v7

--- a/solution.py
+++ b/solution.py
@@ -23,7 +23,7 @@
         for x in range(SIDE):
             for y in range(SIDE):
                 for core in range(2):
-                    along_z = (core == 0) != second
+                    along_z = (core == 1) != second
                     to_z = (z + step) % SIDE if along_z else z
                     to_x = x if along_z else (x + step) % SIDE
                     source = (z * SIDE + x) * E + y * 2 + core

time: 143 us -> 142 us (level)
  transfers between devices with their start and end apart: 18 -> 18, of which waited for: 11 -> 13; matrix products, arithmetic and copies ran while one was open for 1% -> 1% of each run, Pallas kernels for 9% -> 9%
where the time goes in v8:
time: 142 us; the launch traced here: 141 us
  waiting for transfers between devices  65 us (46%)
  starting transfers between devices  29.6 us (21%)
  Pallas kernels  15.7 us (11%)
  blocking collectives  15.4 us (11%)
  other arithmetic  6.41 us (5%)
  local copies, waits for them, and re-layouts  5.41 us (4%)
  matrix products  3.6 us (3%)
    ppermute x8, waiting for transfers between devices, shift_second(): return lax.ppermute(value, ('attn', 'expert'), ring_pairs(step, True))  39.1 us
    ppermute x6, waiting for transfers between devices, shift_first(): return lax.ppermute(value, ('attn', 'expert'), ring_pairs(step, False))  20.3 us
    all_gather x1, blocking collectives, on_device(): gathered = lax.all_gather(payload, 'expert', axis=0)  15.4 us
    ppermute x8, starting transfers between devices, shift_second(): return lax.ppermute(value, ('attn', 'expert'), ring_pairs(step, True))  11.4 us
    pallas_call x3, Pallas kernels, feed(): pl.pallas_call(functools.partial(feed_kernel, len(row_arrays)), in_specs=...  10.6 us
    ppermute x6, starting transfers between devices, shift_first(): return lax.ppermute(value, ('attn', 'expert'), ring_pairs(step, False))  8.34 us
    ppermute x1, starting transfers between devices, swap_cores(): lax.ppermute(value, 'expert', [(index, index ^ 1) for index in range(E)])  6.17 us
    pallas_call x1, Pallas kernels, load(): pl.pallas_call(load_kernel, in_specs=[pl.BlockSpec(memory_space=pltpu.HBM...  5.15 us
  transfers between devices with their start and end apart: 18, of which 13 were waited for; matrix products, arithmetic and copies ran while one was open for 1% of the time, Pallas kernels for 9%

profile of v8, /device:TPU:1, one launch (start us, length us, event | category | flops | bytes accessed | tf_op | source)
XLA Modules:
  0.0 141.5 jit_solution(11768214972374574864)
XLA Ops:
  7.2 15.4 %all-gather = bf16[512,896]{1,0:T(8,128)(2,1)S(1)} all-gather(bf16[64,896]{1,0:T(8,128)(2,1)S(1)} %concatenate.20), channel_id=2, replica_groups=mesh['attn'=16,'expert'=8] {'expert'}, dimensions={0}, use_global_device_ids=true | all-gather | bytes 1032192 | tf_op jit(solution)/shard_map/all_gather | solution.py:240
  23.5 1.7 %collective-permute-start = (bf16[32,6144]{1,0:T(8,128)(2,1)S(1)}, bf16[32,6144]{1,0:T(8,128)(2,1)S(1)}, u32[]{:S(2)}, u32[]{:S(2)}) collective-permute-start(bf16[32,6144]{1,0:T(8,128)(2,1)S(1)} %multiply_convert_fusion), channel_id=1, source_target_pairs={{0,8},{1,33},{2,10},{3,35},{4,12},{5,37},{6,14},{7,39},{8,16},{9,4... | collective-permute-start | bytes 1179656 | tf_op jit(solution)/shard_map/ppermute | solution.py:36
  25.2 2.2 %collective-permute-start.1 = (bf16[32,6144]{1,0:T(8,128)(2,1)S(1)}, bf16[32,6144]{1,0:T(8,128)(2,1)S(1)}, u32[]{:S(2)}, u32[]{:S(2)}) collective-permute-start(bf16[32,6144]{1,0:T(8,128)(2,1)S(1)} %multiply_convert_fusion), channel_id=1, source_target_pairs={{0,24},{1,97},{2,26},{3,99},{4,28},{5,101},{6,30},{7,103},{8,0},{9... | collective-permute-start | bytes 1179656 | tf_op jit(solution)/shard_map/ppermute | solution.py:36
  28.6 3.9 %collective-permute-done = bf16[32,6144]{1,0:T(8,128)(2,1)S(1)} collective-permute-done((bf16[32,6144]{1,0:T(8,128)(2,1)S(1)}, bf16[32,6144]{1,0:T(8,128)(2,1)S(1)}, u32[]{:S(2)}, u32[]{:S(2)}) %collective-permute-start) | collective-permute-done | bytes 393248 | tf_op jit(solution)/shard_map/ppermute | solution.py:36
  32.5 3.9 %collective-permute-done.1 = bf16[32,6144]{1,0:T(8,128)(2,1)S(1)} collective-permute-done((bf16[32,6144]{1,0:T(8,128)(2,1)S(1)}, bf16[32,6144]{1,0:T(8,128)(2,1)S(1)}, u32[]{:S(2)}, u32[]{:S(2)}) %collective-permute-start.1) | collective-permute-done | bytes 393248 | tf_op jit(solution)/shard_map/ppermute | solution.py:36
  40.8 2.8 %copy-done.2 = bf16[1,6144,512]{2,1,0:T(8,128)(2,1)S(1)} copy-done((bf16[1,6144,512]{2,1,0:T(8,128)(2,1)S(1)}, bf16[1,6144,512]{2,1,0:T(8,128)(2,1)}, u32[]{:S(2)}) %copy-start.2) | copy-done | bytes 6291480
  43.6 5.2 %shard_map.127 = (bf16[1,6144,512]{2,1,0:T(8,128)(2,1)S(1)}, bf16[1,6144,512]{2,1,0:T(8,128)(2,1)S(1)}, bf16[1,512,6144]{2,1,0:T(8,128)(2,1)S(1)}) custom-call(bf16[1,6144,512]{2,1,0:T(8,128)(2,1)S(1)} %copy-done.2, bf16[1,6144,512]{2,1,0:T(8,128)(2,1)} %refs_1_, bf16[1,512,6144]{2,1,0:T(8,128)(2,1)} %refs_2_), custom_call_target="tpu_custom_call" | custom-call | bytes 18874368 | tf_op jit(solution)/shard_map/pallas_call | solution.py:91
  48.7 2.7 %shard_map.128 = bf16[128,6144]{1,0:T(8,128)(2,1)S(1)} custom-call(bf16[128,6144]{1,0:T(8,128)(2,1)S(1)} %pad_maximum_fusion.refs_0_, bf16[1,6144,512]{2,1,0:T(8,128)(2,1)S(1)} %get-tuple-element.49.refs_1_.refs_2_, bf16[1,6144,512]{2,1,0:T(8,128)(2,1)S(1)} %get-tuple-element.50.refs_2_.refs_3_, bf16[1,512,6144]{2,1,0:T(8,128)(2,1)S(1)} %get-tuple-element.51.refs_3_.refs_4_), custom_call_target="tpu_custom_call" | custom-call | flops 2415919104 | bytes 3145728 | tf_op jit(solution)/shard_map/pallas_call | solution.py:137
  51.5 7.4 %collective-permute-done.3.refs_0_ = bf16[128,6144]{1,0:T(8,128)(2,1)S(1)} collective-permute-done((bf16[128,6144]{1,0:T(8,128)(2,1)S(1)}, bf16[128,6144]{1,0:T(8,128)(2,1)S(1)}, u32[]{:S(2)}, u32[]{:S(2)}) %collective-permute-start.3) | collective-permute-done | bytes 1572896 | tf_op jit(solution)/shard_map/ppermute | solution.py:40
  60.3 1.7 %collective-permute-start.6 = (bf16[64,6144]{1,0:T(8,128)(2,1)S(1)}, bf16[64,6144]{1,0:T(8,128)(2,1)S(1)}, u32[]{:S(2)}, u32[]{:S(2)}) collective-permute-start(bf16[64,6144]{1,0:T(8,128)(2,1)S(1)} %slice.109), channel_id=1, source_target_pairs={{0,96},{1,25},{2,98},{3,27},{4,100},{5,29},{6,102},{7,31},{8,104},... | collective-permute-start | bytes 2359304 | tf_op jit(solution)/shard_map/ppermute | solution.py:40
  62.0 5.1 %shard_map.129 = (bf16[128,6144]{1,0:T(8,128)(2,1)S(1)}, bf16[128,6144]{1,0:T(8,128)(2,1)S(1)}) custom-call(bf16[128,6144]{1,0:T(8,128)(2,1)S(1)} %collective-permute-done.3.refs_0_, bf16[128,6144]{1,0:T(8,128)(2,1)S(1)} %collective-permute-done.4.refs_1_, bf16[1,6144,512]{2,1,0:T(8,128)(2,1)S(1)} %get-tuple-element.49.refs_1_.refs_2_, ...), custom_call_target="tpu_custom_call" | custom-call | flops 4831838208 | bytes 6291456 | tf_op jit(solution)/shard_map/pallas_call | solution.py:137
  67.1 4.2 %collective-permute-done.5.refs_0_ = bf16[64,6144]{1,0:T(8,128)(2,1)S(1)} collective-permute-done((bf16[64,6144]{1,0:T(8,128)(2,1)S(1)}, bf16[64,6144]{1,0:T(8,128)(2,1)S(1)}, u32[]{:S(2)}, u32[]{:S(2)}) %collective-permute-start.5) | collective-permute-done | bytes 786464 | tf_op jit(solution)/shard_map/ppermute | solution.py:40
  71.7 2.7 %shard_map.130 = (bf16[64,6144]{1,0:T(8,128)(2,1)S(1)}, bf16[64,6144]{1,0:T(8,128)(2,1)S(1)}) custom-call(bf16[64,6144]{1,0:T(8,128)(2,1)S(1)} %collective-permute-done.5.refs_0_, bf16[64,6144]{1,0:T(8,128)(2,1)S(1)} %collective-permute-done.6.refs_1_, bf16[1,6144,512]{2,1,0:T(8,128)(2,1)S(1)} %get-tuple-element.49.refs_1_.refs_2_, ...), custom_call_target="tpu_custom_call" | custom-call | flops 2415919104 | bytes 3145728 | tf_op jit(solution)/shard_map/pallas_call | solution.py:137
  75.3 1.9 %collective-permute-start.9 = (bf16[64,6144]{1,0:T(8,128)(2,1)S(1)}, bf16[64,6144]{1,0:T(8,128)(2,1)S(1)}, u32[]{:S(2)}, u32[]{:S(2)}) collective-permute-start(bf16[64,6144]{1,0:T(8,128)(2,1)S(1)} %get-tuple-element.62), channel_id=1, source_target_pairs={{0,96},{1,25},{2,98},{3,27},{4,100},{5,29},{6,102},{7,31},{8,104},... | collective-permute-start | bytes 2359304 | tf_op jit(solution)/shard_map/ppermute | solution.py:40
  77.2 9.6 %collective-permute-done.7 = bf16[64,6144]{1,0:T(8,128)(2,1)S(1)} collective-permute-done((bf16[64,6144]{1,0:T(8,128)(2,1)S(1)}, bf16[64,6144]{1,0:T(8,128)(2,1)S(1)}, u32[]{:S(2)}, u32[]{:S(2)}) %collective-permute-start.7) | collective-permute-done | bytes 786464 | tf_op jit(solution)/shard_map/ppermute | solution.py:40
  87.7 2.7 %collective-permute-start.10 = (bf16[128,6144]{1,0:T(8,128)(2,1)S(1)}, bf16[128,6144]{1,0:T(8,128)(2,1)S(1)}, u32[]{:S(2)}, u32[]{:S(2)}) collective-permute-start(bf16[128,6144]{1,0:T(8,128)(2,1)S(1)} %fusion.17), channel_id=1, source_target_pairs={{0,96},{1,25},{2,98},{3,27},{4,100},{5,29},{6,102},{7,31},{8,104},... | collective-permute-start | bytes 4718600 | tf_op jit(solution)/shard_map/ppermute | solution.py:40
  90.5 17.6 %collective-permute-done.8 = bf16[128,6144]{1,0:T(8,128)(2,1)S(1)} collective-permute-done((bf16[128,6144]{1,0:T(8,128)(2,1)S(1)}, bf16[128,6144]{1,0:T(8,128)(2,1)S(1)}, u32[]{:S(2)}, u32[]{:S(2)}) %collective-permute-start.8) | collective-permute-done | bytes 1572896 | tf_op jit(solution)/shard_map/ppermute | solution.py:40
  108.9 1.9 %collective-permute-start.11 = (bf16[32,6144]{1,0:T(8,128)(2,1)S(1)}, bf16[32,6144]{1,0:T(8,128)(2,1)S(1)}, u32[]{:S(2)}, u32[]{:S(2)}) collective-permute-start(bf16[32,6144]{1,0:T(8,128)(2,1)S(1)} %get-tuple-element.65), channel_id=1, source_target_pairs={{0,24},{1,97},{2,26},{3,99},{4,28},{5,101},{6,30},{7,103},{8,0},{9... | collective-permute-start | bytes 1179656 | tf_op jit(solution)/shard_map/ppermute | solution.py:36
  112.2 8.7 %collective-permute-done.11 = bf16[32,6144]{1,0:T(8,128)(2,1)S(1)} collective-permute-done((bf16[32,6144]{1,0:T(8,128)(2,1)S(1)}, bf16[32,6144]{1,0:T(8,128)(2,1)S(1)}, u32[]{:S(2)}, u32[]{:S(2)}) %collective-permute-start.11) | collective-permute-done | bytes 393248 | tf_op jit(solution)/shard_map/ppermute | solution.py:36
  121.0 2.3 %collective-permute-done.12 = bf16[32,6144]{1,0:T(8,128)(2,1)} collective-permute-done((bf16[32,6144]{1,0:T(8,128)(2,1)S(1)}, bf16[32,6144]{1,0:T(8,128)(2,1)}, u32[]{:S(2)}, u32[]{:S(2)}) %collective-permute-start.12) | collective-permute-done | bytes 393248 | tf_op jit(solution)/shard_map/ppermute | solution.py:36
  125.0 6.2 %collective-permute-start.14 = (bf16[4,32,768]{2,1,0:T(8,128)(2,1)S(1)}, bf16[4,32,768]{2,1,0:T(8,128)(2,1)S(1)}, u32[]{:S(2)}, u32[]{:S(2)}) collective-permute-start(bf16[4,32,768]{2,1,0:T(8,128)(2,1)S(1)} %get-tuple-element.72), channel_id=1, source_target_pairs={{0,1},{1,0},{2,3},{3,2},{4,5},{5,4},{6,7},{7,6},{8,9},{9,8},{10,11... | collective-permute-start | bytes 589832 | tf_op jit(solution)/shard_map/ppermute | solution.py:51
  133.4 2.4 %collective-permute-start.16 = (bf16[64,768]{1,0:T(8,128)(2,1)S(1)}, bf16[64,768]{1,0:T(8,128)(2,1)S(1)}, u32[]{:S(2)}, u32[]{:S(2)}) collective-permute-start(bf16[64,768]{1,0:T(8,128)(2,1)S(1)} %get-tuple-element.70), channel_id=1, source_target_pairs={{0,4},{1,5},{2,6},{3,7},{4,0},{5,1},{6,2},{7,3},{8,12},{9,13},{10,... | collective-permute-start | bytes 294920 | tf_op jit(solution)/shard_map/ppermute | solution.py:47
  135.9 1.6 %collective-permute-done.15 = bf16[64,768]{1,0:T(8,128)(2,1)S(1)} collective-permute-done((bf16[64,768]{1,0:T(8,128)(2,1)S(1)}, bf16[64,768]{1,0:T(8,128)(2,1)S(1)}, u32[]{:S(2)}, u32[]{:S(2)}) %collective-permute-start.15) | collective-permute-done | bytes 98336 | tf_op jit(solution)/shard_map/ppermute | solution.py:47
  137.5 2.9 %collective-permute-done.16 = bf16[64,768]{1,0:T(8,128)(2,1)S(1)} collective-permute-done((bf16[64,768]{1,0:T(8,128)(2,1)S(1)}, bf16[64,768]{1,0:T(8,128)(2,1)S(1)}, u32[]{:S(2)}, u32[]{:S(2)}) %collective-permute-start.16) | collective-permute-done | bytes 98336 | tf_op jit(solution)/shard_map/ppermute | solution.py:47
  (84 shorter events, 24.3 us)
Async XLA Ops:
  0.0 3.7 %copy-start = (bf16[64,1,128,128]{3,2,1,0:T(8,128)(2,1)S(1)}, bf16[64,1,128,128]{3,2,1,0:T(8,128)(2,1)}, u32[]{:S(2)}) copy-start(bf16[64,1,128,128]{3,2,1,0:T(8,128)(2,1)} %param.19) | copy-start | bytes 6291460
  1.2 3.9 %copy-start.3 = (bf16[64,1,128,128]{3,2,1,0:T(8,128)(2,1)S(1)}, bf16[64,1,128,128]{3,2,1,0:T(8,128)(2,1)}, u32[]{:S(2)}) copy-start(bf16[64,1,128,128]{3,2,1,0:T(8,128)(2,1)} %param.20) | copy-start | bytes 6291460
  5.0 1.0 copy-start.5
  5.1 1.3 copy-start.7
  23.5 9.0 %collective-permute-start = (bf16[32,6144]{1,0:T(8,128)(2,1)S(1)}, bf16[32,6144]{1,0:T(8,128)(2,1)S(1)}, u32[]{:S(2)}, u32[]{:S(2)}) collective-permute-start(bf16[32,6144]{1,0:T(8,128)(2,1)S(1)} %multiply_convert_fusion), channel_id=1, source_target_pairs={{0,8},{1,33},{2,10},{3,35},{4,12},{5,37},{6,14},{7,39},{8,16},{9,4... | collective-permute-start | bytes 1179656 | tf_op jit(solution)/shard_map/ppermute | solution.py:36
  25.2 11.1 %collective-permute-start.1 = (bf16[32,6144]{1,0:T(8,128)(2,1)S(1)}, bf16[32,6144]{1,0:T(8,128)(2,1)S(1)}, u32[]{:S(2)}, u32[]{:S(2)}) collective-permute-start(bf16[32,6144]{1,0:T(8,128)(2,1)S(1)} %multiply_convert_fusion), channel_id=1, source_target_pairs={{0,24},{1,97},{2,26},{3,99},{4,28},{5,101},{6,30},{7,103},{8,0},{9... | collective-permute-start | bytes 1179656 | tf_op jit(solution)/shard_map/ppermute | solution.py:36
  27.4 10.5 %collective-permute-start.2 = (bf16[32,6144]{1,0:T(8,128)(2,1)S(1)}, bf16[32,6144]{1,0:T(8,128)(2,1)S(1)}, u32[]{:S(2)}, u32[]{:S(2)}) collective-permute-start(bf16[32,6144]{1,0:T(8,128)(2,1)S(1)} %multiply_convert_fusion), channel_id=1, source_target_pairs={{0,16},{1,65},{2,18},{3,67},{4,20},{5,69},{6,22},{7,71},{8,24},{9,... | collective-permute-start | bytes 1179656 | tf_op jit(solution)/shard_map/ppermute | solution.py:36
  38.0 20.8 %collective-permute-start.3 = (bf16[128,6144]{1,0:T(8,128)(2,1)S(1)}, bf16[128,6144]{1,0:T(8,128)(2,1)S(1)}, u32[]{:S(2)}, u32[]{:S(2)}) collective-permute-start(bf16[128,6144]{1,0:T(8,128)(2,1)S(1)} %pad_maximum_fusion.refs_0_), channel_id=1, source_target_pairs={{0,32},{1,9},{2,34},{3,11},{4,36},{5,13},{6,38},{7,15},{8,40},{9,1... | collective-permute-start | bytes 4718600 | tf_op jit(solution)/shard_map/ppermute | solution.py:40
  39.3 19.6 %collective-permute-start.4 = (bf16[128,6144]{1,0:T(8,128)(2,1)S(1)}, bf16[128,6144]{1,0:T(8,128)(2,1)S(1)}, u32[]{:S(2)}, u32[]{:S(2)}) collective-permute-start(bf16[128,6144]{1,0:T(8,128)(2,1)S(1)} %pad_maximum_fusion.refs_0_), channel_id=1, source_target_pairs={{0,96},{1,25},{2,98},{3,27},{4,100},{5,29},{6,102},{7,31},{8,104},... | collective-permute-start | bytes 4718600 | tf_op jit(solution)/shard_map/ppermute | solution.py:40
  40.8 2.8 %copy-start.2 = (bf16[1,6144,512]{2,1,0:T(8,128)(2,1)S(1)}, bf16[1,6144,512]{2,1,0:T(8,128)(2,1)}, u32[]{:S(2)}) copy-start(bf16[1,6144,512]{2,1,0:T(8,128)(2,1)} %refs_0_) | copy-start | bytes 18874372
  58.9 12.4 %collective-permute-start.5 = (bf16[64,6144]{1,0:T(8,128)(2,1)S(1)}, bf16[64,6144]{1,0:T(8,128)(2,1)S(1)}, u32[]{:S(2)}, u32[]{:S(2)}) collective-permute-start(bf16[64,6144]{1,0:T(8,128)(2,1)S(1)} %slice.108), channel_id=1, source_target_pairs={{0,32},{1,9},{2,34},{3,11},{4,36},{5,13},{6,38},{7,15},{8,40},{9,1... | collective-permute-start | bytes 2359304 | tf_op jit(solution)/shard_map/ppermute | solution.py:40
  60.3 11.4 %collective-permute-start.6 = (bf16[64,6144]{1,0:T(8,128)(2,1)S(1)}, bf16[64,6144]{1,0:T(8,128)(2,1)S(1)}, u32[]{:S(2)}, u32[]{:S(2)}) collective-permute-start(bf16[64,6144]{1,0:T(8,128)(2,1)S(1)} %slice.109), channel_id=1, source_target_pairs={{0,96},{1,25},{2,98},{3,27},{4,100},{5,29},{6,102},{7,31},{8,104},... | collective-permute-start | bytes 2359304 | tf_op jit(solution)/shard_map/ppermute | solution.py:40
  74.4 12.4 %collective-permute-start.7 = (bf16[64,6144]{1,0:T(8,128)(2,1)S(1)}, bf16[64,6144]{1,0:T(8,128)(2,1)S(1)}, u32[]{:S(2)}, u32[]{:S(2)}) collective-permute-start(bf16[64,6144]{1,0:T(8,128)(2,1)S(1)} %get-tuple-element.60), channel_id=1, source_target_pairs={{0,32},{1,9},{2,34},{3,11},{4,36},{5,13},{6,38},{7,15},{8,40},{9,1... | collective-permute-start | bytes 2359304 | tf_op jit(solution)/shard_map/ppermute | solution.py:40
  75.3 12.0 %collective-permute-start.9 = (bf16[64,6144]{1,0:T(8,128)(2,1)S(1)}, bf16[64,6144]{1,0:T(8,128)(2,1)S(1)}, u32[]{:S(2)}, u32[]{:S(2)}) collective-permute-start(bf16[64,6144]{1,0:T(8,128)(2,1)S(1)} %get-tuple-element.62), channel_id=1, source_target_pairs={{0,96},{1,25},{2,98},{3,27},{4,100},{5,29},{6,102},{7,31},{8,104},... | collective-permute-start | bytes 2359304 | tf_op jit(solution)/shard_map/ppermute | solution.py:40
  87.2 20.8 %collective-permute-start.8 = (bf16[128,6144]{1,0:T(8,128)(2,1)S(1)}, bf16[128,6144]{1,0:T(8,128)(2,1)S(1)}, u32[]{:S(2)}, u32[]{:S(2)}) collective-permute-start(bf16[128,6144]{1,0:T(8,128)(2,1)S(1)} %fusion.16), channel_id=1, source_target_pairs={{0,32},{1,9},{2,34},{3,11},{4,36},{5,13},{6,38},{7,15},{8,40},{9,1... | collective-permute-start | bytes 4718600 | tf_op jit(solution)/shard_map/ppermute | solution.py:40
  87.7 20.3 %collective-permute-start.10 = (bf16[128,6144]{1,0:T(8,128)(2,1)S(1)}, bf16[128,6144]{1,0:T(8,128)(2,1)S(1)}, u32[]{:S(2)}, u32[]{:S(2)}) collective-permute-start(bf16[128,6144]{1,0:T(8,128)(2,1)S(1)} %fusion.17), channel_id=1, source_target_pairs={{0,96},{1,25},{2,98},{3,27},{4,100},{5,29},{6,102},{7,31},{8,104},... | collective-permute-start | bytes 4718600 | tf_op jit(solution)/shard_map/ppermute | solution.py:40
  108.9 12.1 %collective-permute-start.11 = (bf16[32,6144]{1,0:T(8,128)(2,1)S(1)}, bf16[32,6144]{1,0:T(8,128)(2,1)S(1)}, u32[]{:S(2)}, u32[]{:S(2)}) collective-permute-start(bf16[32,6144]{1,0:T(8,128)(2,1)S(1)} %get-tuple-element.65), channel_id=1, source_target_pairs={{0,24},{1,97},{2,26},{3,99},{4,28},{5,101},{6,30},{7,103},{8,0},{9... | collective-permute-start | bytes 1179656 | tf_op jit(solution)/shard_map/ppermute | solution.py:36
  110.8 12.5 %collective-permute-start.12 = (bf16[32,6144]{1,0:T(8,128)(2,1)S(1)}, bf16[32,6144]{1,0:T(8,128)(2,1)}, u32[]{:S(2)}, u32[]{:S(2)}) collective-permute-start(bf16[32,6144]{1,0:T(8,128)(2,1)S(1)} %get-tuple-element.67), channel_id=1, source_target_pairs={{0,8},{1,33},{2,10},{3,35},{4,12},{5,37},{6,14},{7,39},{8,16},{9,4... | collective-permute-start | bytes 1179656 | tf_op jit(solution)/shard_map/ppermute | solution.py:36
  110.8 12.5 %collective-permute-start.13 = (bf16[32,6144]{1,0:T(8,128)(2,1)S(1)}, bf16[32,6144]{1,0:T(8,128)(2,1)}, u32[]{:S(2)}, u32[]{:S(2)}) collective-permute-start(bf16[32,6144]{1,0:T(8,128)(2,1)S(1)} %get-tuple-element.66), channel_id=1, source_target_pairs={{0,16},{1,65},{2,18},{3,67},{4,20},{5,69},{6,22},{7,71},{8,24},{9,... | collective-permute-start | bytes 1179656 | tf_op jit(solution)/shard_map/ppermute | solution.py:36
  125.0 7.2 %collective-permute-start.14 = (bf16[4,32,768]{2,1,0:T(8,128)(2,1)S(1)}, bf16[4,32,768]{2,1,0:T(8,128)(2,1)S(1)}, u32[]{:S(2)}, u32[]{:S(2)}) collective-permute-start(bf16[4,32,768]{2,1,0:T(8,128)(2,1)S(1)} %get-tuple-element.72), channel_id=1, source_target_pairs={{0,1},{1,0},{2,3},{3,2},{4,5},{5,4},{6,7},{7,6},{8,9},{9,8},{10,11... | collective-permute-start | bytes 589832 | tf_op jit(solution)/shard_map/ppermute | solution.py:51
  131.2 10.3 %copy-start.1 = (bf16[64,1,128,128]{3,2,1,0:T(8,128)(2,1)S(1)}, bf16[64,1,128,128]{3,2,1,0:T(8,128)(2,1)}, u32[]{:S(2)}) copy-start(bf16[64,1,128,128]{3,2,1,0:T(8,128)(2,1)} %param.19) | copy-start | bytes 6291460
  132.3 5.3 %collective-permute-start.15 = (bf16[64,768]{1,0:T(8,128)(2,1)S(1)}, bf16[64,768]{1,0:T(8,128)(2,1)S(1)}, u32[]{:S(2)}, u32[]{:S(2)}) collective-permute-start(bf16[64,768]{1,0:T(8,128)(2,1)S(1)} %get-tuple-element.69), channel_id=1, source_target_pairs={{0,2},{1,3},{2,4},{3,5},{4,6},{5,7},{6,0},{7,1},{8,10},{9,11},{10,... | collective-permute-start | bytes 294920 | tf_op jit(solution)/shard_map/ppermute | solution.py:47
  133.4 7.0 %collective-permute-start.16 = (bf16[64,768]{1,0:T(8,128)(2,1)S(1)}, bf16[64,768]{1,0:T(8,128)(2,1)S(1)}, u32[]{:S(2)}, u32[]{:S(2)}) collective-permute-start(bf16[64,768]{1,0:T(8,128)(2,1)S(1)} %get-tuple-element.70), channel_id=1, source_target_pairs={{0,4},{1,5},{2,6},{3,7},{4,0},{5,1},{6,2},{7,3},{8,12},{9,13},{10,... | collective-permute-start | bytes 294920 | tf_op jit(solution)/shard_map/ppermute | solution.py:47
  135.8 4.7 %collective-permute-start.17 = (bf16[64,768]{1,0:T(8,128)(2,1)S(1)}, bf16[64,768]{1,0:T(8,128)(2,1)S(1)}, u32[]{:S(2)}, u32[]{:S(2)}) collective-permute-start(bf16[64,768]{1,0:T(8,128)(2,1)S(1)} %get-tuple-element.71), channel_id=1, source_target_pairs={{0,6},{1,7},{2,0},{3,1},{4,2},{5,3},{6,4},{7,5},{8,14},{9,15},{10,... | collective-permute-start | bytes 294920 | tf_op jit(solution)/shard_map/ppermute | solution.py:47
  (2 other events, 1.9 us)

commit v9 on v8

--- a/solution.py
+++ b/solution.py
@@ -301,11 +301,11 @@
     kept = jnp.where(core == 0, even, odd)
     swapped = swap_cores(jnp.where(core == 0, odd, even))
     pair = jnp.concatenate([kept, swapped], axis=1)
-    blocks = []
-    for step in range(SIDE):
+    blocks = {}
+    for step in (0, 1, 3, 2):
         block = lax.dynamic_index_in_dim(pair, (row_y + step) % SIDE, 0, keepdims=False)
-        blocks.append(block if step == 0 else shift_y(block, step))
-    flat_result = jnp.concatenate(blocks, axis=0)
+        blocks[step] = block if step == 0 else shift_y(block, step)
+    flat_result = jnp.concatenate([blocks[step] for step in range(SIDE)], axis=0)
     away = (row_y - expert_ids // 2 + SIDE) % SIDE
     target_index = (away * 2 + (expert_ids + core) % 2) * CAP + slot_index
     picker = (

time: 142 us -> 142 us (level)
  no operation moved by 1% of the time
where the time goes in v9:
time: 142 us; the launch traced here: 141 us
  waiting for transfers between devices  65 us (46%)
  starting transfers between devices  29.6 us (21%)
  Pallas kernels  15.7 us (11%)
  blocking collectives  15.4 us (11%)
  other arithmetic  6.41 us (5%)
  local copies, waits for them, and re-layouts  5.41 us (4%)
  matrix products  3.6 us (3%)
    ppermute x8, waiting for transfers between devices, shift_second(): return lax.ppermute(value, ('attn', 'expert'), ring_pairs(step, True))  39.1 us
    ppermute x6, waiting for transfers between devices, shift_first(): return lax.ppermute(value, ('attn', 'expert'), ring_pairs(step, False))  20.3 us
    all_gather x1, blocking collectives, on_device(): gathered = lax.all_gather(payload, 'expert', axis=0)  15.4 us
    ppermute x8, starting transfers between devices, shift_second(): return lax.ppermute(value, ('attn', 'expert'), ring_pairs(step, True))  11.4 us
    pallas_call x3, Pallas kernels, feed(): pl.pallas_call(functools.partial(feed_kernel, len(row_arrays)), in_specs=...  10.6 us
    ppermute x6, starting transfers between devices, shift_first(): return lax.ppermute(value, ('attn', 'expert'), ring_pairs(step, False))  8.34 us
    ppermute x1, starting transfers between devices, swap_cores(): lax.ppermute(value, 'expert', [(index, index ^ 1) for index in range(E)])  6.17 us
    pallas_call x1, Pallas kernels, load(): pl.pallas_call(load_kernel, in_specs=[pl.BlockSpec(memory_space=pltpu.HBM...  5.15 us
  transfers between devices with their start and end apart: 18, of which 13 were waited for; matrix products, arithmetic and copies ran while one was open for 1% of the time, Pallas kernels for 9%

profile of v9, /device:TPU:1, one launch (start us, length us, event | category | flops | bytes accessed | tf_op | source)
XLA Modules:
  0.0 141.5 jit_solution(11768214972374574864)
XLA Ops:
  7.2 15.4 %all-gather = bf16[512,896]{1,0:T(8,128)(2,1)S(1)} all-gather(bf16[64,896]{1,0:T(8,128)(2,1)S(1)} %concatenate.20), channel_id=2, replica_groups=mesh['attn'=16,'expert'=8] {'expert'}, dimensions={0}, use_global_device_ids=true | all-gather | bytes 1032192 | tf_op jit(solution)/shard_map/all_gather | solution.py:240
  23.5 1.7 %collective-permute-start = (bf16[32,6144]{1,0:T(8,128)(2,1)S(1)}, bf16[32,6144]{1,0:T(8,128)(2,1)S(1)}, u32[]{:S(2)}, u32[]{:S(2)}) collective-permute-start(bf16[32,6144]{1,0:T(8,128)(2,1)S(1)} %multiply_convert_fusion), channel_id=1, source_target_pairs={{0,8},{1,33},{2,10},{3,35},{4,12},{5,37},{6,14},{7,39},{8,16},{9,4... | collective-permute-start | bytes 1179656 | tf_op jit(solution)/shard_map/ppermute | solution.py:36
  25.2 2.2 %collective-permute-start.1 = (bf16[32,6144]{1,0:T(8,128)(2,1)S(1)}, bf16[32,6144]{1,0:T(8,128)(2,1)S(1)}, u32[]{:S(2)}, u32[]{:S(2)}) collective-permute-start(bf16[32,6144]{1,0:T(8,128)(2,1)S(1)} %multiply_convert_fusion), channel_id=1, source_target_pairs={{0,24},{1,97},{2,26},{3,99},{4,28},{5,101},{6,30},{7,103},{8,0},{9... | collective-permute-start | bytes 1179656 | tf_op jit(solution)/shard_map/ppermute | solution.py:36
  28.6 3.9 %collective-permute-done = bf16[32,6144]{1,0:T(8,128)(2,1)S(1)} collective-permute-done((bf16[32,6144]{1,0:T(8,128)(2,1)S(1)}, bf16[32,6144]{1,0:T(8,128)(2,1)S(1)}, u32[]{:S(2)}, u32[]{:S(2)}) %collective-permute-start) | collective-permute-done | bytes 393248 | tf_op jit(solution)/shard_map/ppermute | solution.py:36
  32.5 3.9 %collective-permute-done.1 = bf16[32,6144]{1,0:T(8,128)(2,1)S(1)} collective-permute-done((bf16[32,6144]{1,0:T(8,128)(2,1)S(1)}, bf16[32,6144]{1,0:T(8,128)(2,1)S(1)}, u32[]{:S(2)}, u32[]{:S(2)}) %collective-permute-start.1) | collective-permute-done | bytes 393248 | tf_op jit(solution)/shard_map/ppermute | solution.py:36
  40.8 2.8 %copy-done.2 = bf16[1,6144,512]{2,1,0:T(8,128)(2,1)S(1)} copy-done((bf16[1,6144,512]{2,1,0:T(8,128)(2,1)S(1)}, bf16[1,6144,512]{2,1,0:T(8,128)(2,1)}, u32[]{:S(2)}) %copy-start.2) | copy-done | bytes 6291480
  43.6 5.2 %shard_map.127 = (bf16[1,6144,512]{2,1,0:T(8,128)(2,1)S(1)}, bf16[1,6144,512]{2,1,0:T(8,128)(2,1)S(1)}, bf16[1,512,6144]{2,1,0:T(8,128)(2,1)S(1)}) custom-call(bf16[1,6144,512]{2,1,0:T(8,128)(2,1)S(1)} %copy-done.2, bf16[1,6144,512]{2,1,0:T(8,128)(2,1)} %refs_1_, bf16[1,512,6144]{2,1,0:T(8,128)(2,1)} %refs_2_), custom_call_target="tpu_custom_call" | custom-call | bytes 18874368 | tf_op jit(solution)/shard_map/pallas_call | solution.py:91
  48.7 2.7 %shard_map.128 = bf16[128,6144]{1,0:T(8,128)(2,1)S(1)} custom-call(bf16[128,6144]{1,0:T(8,128)(2,1)S(1)} %pad_maximum_fusion.refs_0_, bf16[1,6144,512]{2,1,0:T(8,128)(2,1)S(1)} %get-tuple-element.49.refs_1_.refs_2_, bf16[1,6144,512]{2,1,0:T(8,128)(2,1)S(1)} %get-tuple-element.50.refs_2_.refs_3_, bf16[1,512,6144]{2,1,0:T(8,128)(2,1)S(1)} %get-tuple-element.51.refs_3_.refs_4_), custom_call_target="tpu_custom_call" | custom-call | flops 2415919104 | bytes 3145728 | tf_op jit(solution)/shard_map/pallas_call | solution.py:137
  51.5 7.4 %collective-permute-done.3.refs_0_ = bf16[128,6144]{1,0:T(8,128)(2,1)S(1)} collective-permute-done((bf16[128,6144]{1,0:T(8,128)(2,1)S(1)}, bf16[128,6144]{1,0:T(8,128)(2,1)S(1)}, u32[]{:S(2)}, u32[]{:S(2)}) %collective-permute-start.3) | collective-permute-done | bytes 1572896 | tf_op jit(solution)/shard_map/ppermute | solution.py:40
  60.3 1.7 %collective-permute-start.6 = (bf16[64,6144]{1,0:T(8,128)(2,1)S(1)}, bf16[64,6144]{1,0:T(8,128)(2,1)S(1)}, u32[]{:S(2)}, u32[]{:S(2)}) collective-permute-start(bf16[64,6144]{1,0:T(8,128)(2,1)S(1)} %slice.109), channel_id=1, source_target_pairs={{0,96},{1,25},{2,98},{3,27},{4,100},{5,29},{6,102},{7,31},{8,104},... | collective-permute-start | bytes 2359304 | tf_op jit(solution)/shard_map/ppermute | solution.py:40
  62.0 5.1 %shard_map.129 = (bf16[128,6144]{1,0:T(8,128)(2,1)S(1)}, bf16[128,6144]{1,0:T(8,128)(2,1)S(1)}) custom-call(bf16[128,6144]{1,0:T(8,128)(2,1)S(1)} %collective-permute-done.3.refs_0_, bf16[128,6144]{1,0:T(8,128)(2,1)S(1)} %collective-permute-done.4.refs_1_, bf16[1,6144,512]{2,1,0:T(8,128)(2,1)S(1)} %get-tuple-element.49.refs_1_.refs_2_, ...), custom_call_target="tpu_custom_call" | custom-call | flops 4831838208 | bytes 6291456 | tf_op jit(solution)/shard_map/pallas_call | solution.py:137
  67.1 4.2 %collective-permute-done.5.refs_0_ = bf16[64,6144]{1,0:T(8,128)(2,1)S(1)} collective-permute-done((bf16[64,6144]{1,0:T(8,128)(2,1)S(1)}, bf16[64,6144]{1,0:T(8,128)(2,1)S(1)}, u32[]{:S(2)}, u32[]{:S(2)}) %collective-permute-start.5) | collective-permute-done | bytes 786464 | tf_op jit(solution)/shard_map/ppermute | solution.py:40
  71.7 2.7 %shard_map.130 = (bf16[64,6144]{1,0:T(8,128)(2,1)S(1)}, bf16[64,6144]{1,0:T(8,128)(2,1)S(1)}) custom-call(bf16[64,6144]{1,0:T(8,128)(2,1)S(1)} %collective-permute-done.5.refs_0_, bf16[64,6144]{1,0:T(8,128)(2,1)S(1)} %collective-permute-done.6.refs_1_, bf16[1,6144,512]{2,1,0:T(8,128)(2,1)S(1)} %get-tuple-element.49.refs_1_.refs_2_, ...), custom_call_target="tpu_custom_call" | custom-call | flops 2415919104 | bytes 3145728 | tf_op jit(solution)/shard_map/pallas_call | solution.py:137
  75.3 1.9 %collective-permute-start.9 = (bf16[64,6144]{1,0:T(8,128)(2,1)S(1)}, bf16[64,6144]{1,0:T(8,128)(2,1)S(1)}, u32[]{:S(2)}, u32[]{:S(2)}) collective-permute-start(bf16[64,6144]{1,0:T(8,128)(2,1)S(1)} %get-tuple-element.62), channel_id=1, source_target_pairs={{0,96},{1,25},{2,98},{3,27},{4,100},{5,29},{6,102},{7,31},{8,104},... | collective-permute-start | bytes 2359304 | tf_op jit(solution)/shard_map/ppermute | solution.py:40
  77.2 9.6 %collective-permute-done.7 = bf16[64,6144]{1,0:T(8,128)(2,1)S(1)} collective-permute-done((bf16[64,6144]{1,0:T(8,128)(2,1)S(1)}, bf16[64,6144]{1,0:T(8,128)(2,1)S(1)}, u32[]{:S(2)}, u32[]{:S(2)}) %collective-permute-start.7) | collective-permute-done | bytes 786464 | tf_op jit(solution)/shard_map/ppermute | solution.py:40
  87.7 2.7 %collective-permute-start.10 = (bf16[128,6144]{1,0:T(8,128)(2,1)S(1)}, bf16[128,6144]{1,0:T(8,128)(2,1)S(1)}, u32[]{:S(2)}, u32[]{:S(2)}) collective-permute-start(bf16[128,6144]{1,0:T(8,128)(2,1)S(1)} %fusion.17), channel_id=1, source_target_pairs={{0,96},{1,25},{2,98},{3,27},{4,100},{5,29},{6,102},{7,31},{8,104},... | collective-permute-start | bytes 4718600 | tf_op jit(solution)/shard_map/ppermute | solution.py:40
  90.5 17.6 %collective-permute-done.8 = bf16[128,6144]{1,0:T(8,128)(2,1)S(1)} collective-permute-done((bf16[128,6144]{1,0:T(8,128)(2,1)S(1)}, bf16[128,6144]{1,0:T(8,128)(2,1)S(1)}, u32[]{:S(2)}, u32[]{:S(2)}) %collective-permute-start.8) | collective-permute-done | bytes 1572896 | tf_op jit(solution)/shard_map/ppermute | solution.py:40
  108.9 1.9 %collective-permute-start.11 = (bf16[32,6144]{1,0:T(8,128)(2,1)S(1)}, bf16[32,6144]{1,0:T(8,128)(2,1)S(1)}, u32[]{:S(2)}, u32[]{:S(2)}) collective-permute-start(bf16[32,6144]{1,0:T(8,128)(2,1)S(1)} %get-tuple-element.65), channel_id=1, source_target_pairs={{0,24},{1,97},{2,26},{3,99},{4,28},{5,101},{6,30},{7,103},{8,0},{9... | collective-permute-start | bytes 1179656 | tf_op jit(solution)/shard_map/ppermute | solution.py:36
  112.2 8.7 %collective-permute-done.11 = bf16[32,6144]{1,0:T(8,128)(2,1)S(1)} collective-permute-done((bf16[32,6144]{1,0:T(8,128)(2,1)S(1)}, bf16[32,6144]{1,0:T(8,128)(2,1)S(1)}, u32[]{:S(2)}, u32[]{:S(2)}) %collective-permute-start.11) | collective-permute-done | bytes 393248 | tf_op jit(solution)/shard_map/ppermute | solution.py:36
  121.0 2.3 %collective-permute-done.12 = bf16[32,6144]{1,0:T(8,128)(2,1)} collective-permute-done((bf16[32,6144]{1,0:T(8,128)(2,1)S(1)}, bf16[32,6144]{1,0:T(8,128)(2,1)}, u32[]{:S(2)}, u32[]{:S(2)}) %collective-permute-start.12) | collective-permute-done | bytes 393248 | tf_op jit(solution)/shard_map/ppermute | solution.py:36
  125.0 6.2 %collective-permute-start.14 = (bf16[4,32,768]{2,1,0:T(8,128)(2,1)S(1)}, bf16[4,32,768]{2,1,0:T(8,128)(2,1)S(1)}, u32[]{:S(2)}, u32[]{:S(2)}) collective-permute-start(bf16[4,32,768]{2,1,0:T(8,128)(2,1)S(1)} %get-tuple-element.72), channel_id=1, source_target_pairs={{0,1},{1,0},{2,3},{3,2},{4,5},{5,4},{6,7},{7,6},{8,9},{9,8},{10,11... | collective-permute-start | bytes 589832 | tf_op jit(solution)/shard_map/ppermute | solution.py:51
  133.4 2.4 %collective-permute-start.16 = (bf16[64,768]{1,0:T(8,128)(2,1)S(1)}, bf16[64,768]{1,0:T(8,128)(2,1)S(1)}, u32[]{:S(2)}, u32[]{:S(2)}) collective-permute-start(bf16[64,768]{1,0:T(8,128)(2,1)S(1)} %get-tuple-element.70), channel_id=1, source_target_pairs={{0,4},{1,5},{2,6},{3,7},{4,0},{5,1},{6,2},{7,3},{8,12},{9,13},{10,... | collective-permute-start | bytes 294920 | tf_op jit(solution)/shard_map/ppermute | solution.py:47
  135.9 1.6 %collective-permute-done.15 = bf16[64,768]{1,0:T(8,128)(2,1)S(1)} collective-permute-done((bf16[64,768]{1,0:T(8,128)(2,1)S(1)}, bf16[64,768]{1,0:T(8,128)(2,1)S(1)}, u32[]{:S(2)}, u32[]{:S(2)}) %collective-permute-start.15) | collective-permute-done | bytes 98336 | tf_op jit(solution)/shard_map/ppermute | solution.py:47
  137.5 2.9 %collective-permute-done.16 = bf16[64,768]{1,0:T(8,128)(2,1)S(1)} collective-permute-done((bf16[64,768]{1,0:T(8,128)(2,1)S(1)}, bf16[64,768]{1,0:T(8,128)(2,1)S(1)}, u32[]{:S(2)}, u32[]{:S(2)}) %collective-permute-start.16) | collective-permute-done | bytes 98336 | tf_op jit(solution)/shard_map/ppermute | solution.py:47
  (84 shorter events, 24.3 us)
Async XLA Ops:
  0.0 3.7 %copy-start = (bf16[64,1,128,128]{3,2,1,0:T(8,128)(2,1)S(1)}, bf16[64,1,128,128]{3,2,1,0:T(8,128)(2,1)}, u32[]{:S(2)}) copy-start(bf16[64,1,128,128]{3,2,1,0:T(8,128)(2,1)} %param.19) | copy-start | bytes 6291460
  1.2 3.9 %copy-start.3 = (bf16[64,1,128,128]{3,2,1,0:T(8,128)(2,1)S(1)}, bf16[64,1,128,128]{3,2,1,0:T(8,128)(2,1)}, u32[]{:S(2)}) copy-start(bf16[64,1,128,128]{3,2,1,0:T(8,128)(2,1)} %param.20) | copy-start | bytes 6291460
  5.0 1.0 copy-start.5
  5.1 1.3 copy-start.7
  23.5 9.0 %collective-permute-start = (bf16[32,6144]{1,0:T(8,128)(2,1)S(1)}, bf16[32,6144]{1,0:T(8,128)(2,1)S(1)}, u32[]{:S(2)}, u32[]{:S(2)}) collective-permute-start(bf16[32,6144]{1,0:T(8,128)(2,1)S(1)} %multiply_convert_fusion), channel_id=1, source_target_pairs={{0,8},{1,33},{2,10},{3,35},{4,12},{5,37},{6,14},{7,39},{8,16},{9,4... | collective-permute-start | bytes 1179656 | tf_op jit(solution)/shard_map/ppermute | solution.py:36
  25.2 11.1 %collective-permute-start.1 = (bf16[32,6144]{1,0:T(8,128)(2,1)S(1)}, bf16[32,6144]{1,0:T(8,128)(2,1)S(1)}, u32[]{:S(2)}, u32[]{:S(2)}) collective-permute-start(bf16[32,6144]{1,0:T(8,128)(2,1)S(1)} %multiply_convert_fusion), channel_id=1, source_target_pairs={{0,24},{1,97},{2,26},{3,99},{4,28},{5,101},{6,30},{7,103},{8,0},{9... | collective-permute-start | bytes 1179656 | tf_op jit(solution)/shard_map/ppermute | solution.py:36
  27.4 10.5 %collective-permute-start.2 = (bf16[32,6144]{1,0:T(8,128)(2,1)S(1)}, bf16[32,6144]{1,0:T(8,128)(2,1)S(1)}, u32[]{:S(2)}, u32[]{:S(2)}) collective-permute-start(bf16[32,6144]{1,0:T(8,128)(2,1)S(1)} %multiply_convert_fusion), channel_id=1, source_target_pairs={{0,16},{1,65},{2,18},{3,67},{4,20},{5,69},{6,22},{7,71},{8,24},{9,... | collective-permute-start | bytes 1179656 | tf_op jit(solution)/shard_map/ppermute | solution.py:36
  38.0 20.8 %collective-permute-start.3 = (bf16[128,6144]{1,0:T(8,128)(2,1)S(1)}, bf16[128,6144]{1,0:T(8,128)(2,1)S(1)}, u32[]{:S(2)}, u32[]{:S(2)}) collective-permute-start(bf16[128,6144]{1,0:T(8,128)(2,1)S(1)} %pad_maximum_fusion.refs_0_), channel_id=1, source_target_pairs={{0,32},{1,9},{2,34},{3,11},{4,36},{5,13},{6,38},{7,15},{8,40},{9,1... | collective-permute-start | bytes 4718600 | tf_op jit(solution)/shard_map/ppermute | solution.py:40
  39.3 19.6 %collective-permute-start.4 = (bf16[128,6144]{1,0:T(8,128)(2,1)S(1)}, bf16[128,6144]{1,0:T(8,128)(2,1)S(1)}, u32[]{:S(2)}, u32[]{:S(2)}) collective-permute-start(bf16[128,6144]{1,0:T(8,128)(2,1)S(1)} %pad_maximum_fusion.refs_0_), channel_id=1, source_target_pairs={{0,96},{1,25},{2,98},{3,27},{4,100},{5,29},{6,102},{7,31},{8,104},... | collective-permute-start | bytes 4718600 | tf_op jit(solution)/shard_map/ppermute | solution.py:40
  40.8 2.8 %copy-start.2 = (bf16[1,6144,512]{2,1,0:T(8,128)(2,1)S(1)}, bf16[1,6144,512]{2,1,0:T(8,128)(2,1)}, u32[]{:S(2)}) copy-start(bf16[1,6144,512]{2,1,0:T(8,128)(2,1)} %refs_0_) | copy-start | bytes 18874372
  58.9 12.4 %collective-permute-start.5 = (bf16[64,6144]{1,0:T(8,128)(2,1)S(1)}, bf16[64,6144]{1,0:T(8,128)(2,1)S(1)}, u32[]{:S(2)}, u32[]{:S(2)}) collective-permute-start(bf16[64,6144]{1,0:T(8,128)(2,1)S(1)} %slice.108), channel_id=1, source_target_pairs={{0,32},{1,9},{2,34},{3,11},{4,36},{5,13},{6,38},{7,15},{8,40},{9,1... | collective-permute-start | bytes 2359304 | tf_op jit(solution)/shard_map/ppermute | solution.py:40
  60.3 11.4 %collective-permute-start.6 = (bf16[64,6144]{1,0:T(8,128)(2,1)S(1)}, bf16[64,6144]{1,0:T(8,128)(2,1)S(1)}, u32[]{:S(2)}, u32[]{:S(2)}) collective-permute-start(bf16[64,6144]{1,0:T(8,128)(2,1)S(1)} %slice.109), channel_id=1, source_target_pairs={{0,96},{1,25},{2,98},{3,27},{4,100},{5,29},{6,102},{7,31},{8,104},... | collective-permute-start | bytes 2359304 | tf_op jit(solution)/shard_map/ppermute | solution.py:40
  74.4 12.4 %collective-permute-start.7 = (bf16[64,6144]{1,0:T(8,128)(2,1)S(1)}, bf16[64,6144]{1,0:T(8,128)(2,1)S(1)}, u32[]{:S(2)}, u32[]{:S(2)}) collective-permute-start(bf16[64,6144]{1,0:T(8,128)(2,1)S(1)} %get-tuple-element.60), channel_id=1, source_target_pairs={{0,32},{1,9},{2,34},{3,11},{4,36},{5,13},{6,38},{7,15},{8,40},{9,1... | collective-permute-start | bytes 2359304 | tf_op jit(solution)/shard_map/ppermute | solution.py:40
  75.3 12.0 %collective-permute-start.9 = (bf16[64,6144]{1,0:T(8,128)(2,1)S(1)}, bf16[64,6144]{1,0:T(8,128)(2,1)S(1)}, u32[]{:S(2)}, u32[]{:S(2)}) collective-permute-start(bf16[64,6144]{1,0:T(8,128)(2,1)S(1)} %get-tuple-element.62), channel_id=1, source_target_pairs={{0,96},{1,25},{2,98},{3,27},{4,100},{5,29},{6,102},{7,31},{8,104},... | collective-permute-start | bytes 2359304 | tf_op jit(solution)/shard_map/ppermute | solution.py:40
  87.2 20.8 %collective-permute-start.8 = (bf16[128,6144]{1,0:T(8,128)(2,1)S(1)}, bf16[128,6144]{1,0:T(8,128)(2,1)S(1)}, u32[]{:S(2)}, u32[]{:S(2)}) collective-permute-start(bf16[128,6144]{1,0:T(8,128)(2,1)S(1)} %fusion.16), channel_id=1, source_target_pairs={{0,32},{1,9},{2,34},{3,11},{4,36},{5,13},{6,38},{7,15},{8,40},{9,1... | collective-permute-start | bytes 4718600 | tf_op jit(solution)/shard_map/ppermute | solution.py:40
  87.7 20.3 %collective-permute-start.10 = (bf16[128,6144]{1,0:T(8,128)(2,1)S(1)}, bf16[128,6144]{1,0:T(8,128)(2,1)S(1)}, u32[]{:S(2)}, u32[]{:S(2)}) collective-permute-start(bf16[128,6144]{1,0:T(8,128)(2,1)S(1)} %fusion.17), channel_id=1, source_target_pairs={{0,96},{1,25},{2,98},{3,27},{4,100},{5,29},{6,102},{7,31},{8,104},... | collective-permute-start | bytes 4718600 | tf_op jit(solution)/shard_map/ppermute | solution.py:40
  108.9 12.1 %collective-permute-start.11 = (bf16[32,6144]{1,0:T(8,128)(2,1)S(1)}, bf16[32,6144]{1,0:T(8,128)(2,1)S(1)}, u32[]{:S(2)}, u32[]{:S(2)}) collective-permute-start(bf16[32,6144]{1,0:T(8,128)(2,1)S(1)} %get-tuple-element.65), channel_id=1, source_target_pairs={{0,24},{1,97},{2,26},{3,99},{4,28},{5,101},{6,30},{7,103},{8,0},{9... | collective-permute-start | bytes 1179656 | tf_op jit(solution)/shard_map/ppermute | solution.py:36
  110.8 12.5 %collective-permute-start.12 = (bf16[32,6144]{1,0:T(8,128)(2,1)S(1)}, bf16[32,6144]{1,0:T(8,128)(2,1)}, u32[]{:S(2)}, u32[]{:S(2)}) collective-permute-start(bf16[32,6144]{1,0:T(8,128)(2,1)S(1)} %get-tuple-element.67), channel_id=1, source_target_pairs={{0,8},{1,33},{2,10},{3,35},{4,12},{5,37},{6,14},{7,39},{8,16},{9,4... | collective-permute-start | bytes 1179656 | tf_op jit(solution)/shard_map/ppermute | solution.py:36
  110.8 12.5 %collective-permute-start.13 = (bf16[32,6144]{1,0:T(8,128)(2,1)S(1)}, bf16[32,6144]{1,0:T(8,128)(2,1)}, u32[]{:S(2)}, u32[]{:S(2)}) collective-permute-start(bf16[32,6144]{1,0:T(8,128)(2,1)S(1)} %get-tuple-element.66), channel_id=1, source_target_pairs={{0,16},{1,65},{2,18},{3,67},{4,20},{5,69},{6,22},{7,71},{8,24},{9,... | collective-permute-start | bytes 1179656 | tf_op jit(solution)/shard_map/ppermute | solution.py:36
  125.0 7.2 %collective-permute-start.14 = (bf16[4,32,768]{2,1,0:T(8,128)(2,1)S(1)}, bf16[4,32,768]{2,1,0:T(8,128)(2,1)S(1)}, u32[]{:S(2)}, u32[]{:S(2)}) collective-permute-start(bf16[4,32,768]{2,1,0:T(8,128)(2,1)S(1)} %get-tuple-element.72), channel_id=1, source_target_pairs={{0,1},{1,0},{2,3},{3,2},{4,5},{5,4},{6,7},{7,6},{8,9},{9,8},{10,11... | collective-permute-start | bytes 589832 | tf_op jit(solution)/shard_map/ppermute | solution.py:51
  131.2 10.3 %copy-start.1 = (bf16[64,1,128,128]{3,2,1,0:T(8,128)(2,1)S(1)}, bf16[64,1,128,128]{3,2,1,0:T(8,128)(2,1)}, u32[]{:S(2)}) copy-start(bf16[64,1,128,128]{3,2,1,0:T(8,128)(2,1)} %param.19) | copy-start | bytes 6291460
  132.3 5.3 %collective-permute-start.15 = (bf16[64,768]{1,0:T(8,128)(2,1)S(1)}, bf16[64,768]{1,0:T(8,128)(2,1)S(1)}, u32[]{:S(2)}, u32[]{:S(2)}) collective-permute-start(bf16[64,768]{1,0:T(8,128)(2,1)S(1)} %get-tuple-element.69), channel_id=1, source_target_pairs={{0,2},{1,3},{2,4},{3,5},{4,6},{5,7},{6,0},{7,1},{8,10},{9,11},{10,... | collective-permute-start | bytes 294920 | tf_op jit(solution)/shard_map/ppermute | solution.py:47
  133.4 7.0 %collective-permute-start.16 = (bf16[64,768]{1,0:T(8,128)(2,1)S(1)}, bf16[64,768]{1,0:T(8,128)(2,1)S(1)}, u32[]{:S(2)}, u32[]{:S(2)}) collective-permute-start(bf16[64,768]{1,0:T(8,128)(2,1)S(1)} %get-tuple-element.70), channel_id=1, source_target_pairs={{0,4},{1,5},{2,6},{3,7},{4,0},{5,1},{6,2},{7,3},{8,12},{9,13},{10,... | collective-permute-start | bytes 294920 | tf_op jit(solution)/shard_map/ppermute | solution.py:47
  135.8 4.7 %collective-permute-start.17 = (bf16[64,768]{1,0:T(8,128)(2,1)S(1)}, bf16[64,768]{1,0:T(8,128)(2,1)S(1)}, u32[]{:S(2)}, u32[]{:S(2)}) collective-permute-start(bf16[64,768]{1,0:T(8,128)(2,1)S(1)} %get-tuple-element.71), channel_id=1, source_target_pairs={{0,6},{1,7},{2,0},{3,1},{4,2},{5,3},{6,4},{7,5},{8,14},{9,15},{10,... | collective-permute-start | bytes 294920 | tf_op jit(solution)/shard_map/ppermute | solution.py:47
  (2 other events, 1.9 us)
